TPU v7x, 32 devices: a whole 2x2x4 slice. The times are simulated.
32 devices in a mesh: group: 2 (over x), row: 2 (over core), col: 8 (over z, y).
Axes of the slice: x: 2, y: 2, z: 4, core: 2. Of those that a mesh axis runs over, the one named last changes fastest.
Arguments:
- alignment: bfloat16 [256, 64, 256], P(('group', 'row'), 'col'), parts along dimension 0, may hold values from -6 to 6
- norm_mean: float32 [256, 64], P(('group', 'row'), 'col'), parts along dimension 0, may hold values from -3 to 3
- norm_inverse: float32 [256, 64], P(('group', 'row'), 'col'), parts along dimension 0, may hold values from 0.5 to 2
- norm_gain: float32 [256], replicated, may hold values from 0.5 to 1.5
- norm_shift: float32 [256], replicated, may hold values from -3 to 3
- input_weight: bfloat16 [256, 64], replicated, may hold values from -0.375 to 0.375
- input_bias: float32 [64], replicated, may hold values from -3 to 3
- output_weight: bfloat16 [1024, 128], replicated, may hold values from -0.1875 to 0.1875
- pair_cotangent: bfloat16 [64, 128, 128], P('col', 'group'), parts along dimension 1, may hold values from -6 to 6
- residue_mask: int32 [128], P('group'), parts along dimension 0, may hold values 0 or 1
- sequence_mask: int32 [256, 64], P(('group', 'row'), 'col'), parts along dimension 0, may hold values 0 or 1
Outputs:
- activation_grad: bfloat16 [256, 64, 256], P(('group', 'row'), 'col'), parts along dimension 0
- input_weight_grad: float32 [512, 64], P('group'), parts along dimension 0
- input_bias_grad: float32 [128], P('group'), parts along dimension 0
- output_weight_grad: float32 [2048, 128], P('group'), parts along dimension 0
- output_bias_grad: float32 [256], P('group'), parts along dimension 0
- gain_grad: float32 [512], P('group'), parts along dimension 0
- shift_grad: float32 [512], P('group'), parts along dimension 0
There are 2 independent parts, one for each index of `group`. A program takes and returns all parts, laid end to end along the dimension named above; an argument that names none is the same for every part. Nothing has to cross between parts.
All inputs are finite; a program needn't handle non-finite values. No bound on the sum of `sequence_mask` on one device may be relied on, other than what follows from the above.
Results may differ from a plain program's by a relative error of at most 0.0075.
Values may be sent and summed in bfloat16 or wider, within the bound.
No kernel may reach another device: no remote copies, remote signals or barrier semaphores. Data moves between devices by JAX's collectives and lax.ppermute only.
A program may use at most 64 MiB of HBM per device.

v0:
```python
import math

import jax
import jax.numpy as jnp
from jax import lax
from jax.sharding import PartitionSpec as P

C = 256
P_SIZE = 32
Z = 128


def normalize(alignment, norm_mean, norm_inverse, norm_gain, norm_shift):
    hatted = (alignment.astype(jnp.float32) - norm_mean[..., None]) * norm_inverse[..., None]
    normed = (hatted * norm_gain + norm_shift).astype(jnp.bfloat16)
    return (hatted, normed)


def project(normed, input_weight, input_bias, live):
    flat = normed.reshape(-1, normed.shape[-1])
    projected = jnp.dot(flat, input_weight, preferred_element_type=jnp.float32) + input_bias
    projected = projected.reshape(normed.shape[:-1] + (input_weight.shape[1],)) * live[..., None]
    return projected.astype(jnp.bfloat16)


def contract(left, right, counts, cotangent, pair_live, output_weight):
    sequence_count, row_count, _ = left.shape
    column_total = right.shape[1]
    width = math.gcd(column_total, 128)
    left_acc = jnp.zeros(left.shape, jnp.float32)
    weight_acc = jnp.zeros((P_SIZE * P_SIZE, Z), jnp.float32)
    bias_acc = jnp.zeros((Z,), jnp.float32)
    pieces = []
    for offset in range(0, column_total, width):
        right_cols = right[:, offset : offset + width]
        scale = pair_live[:, offset : offset + width] / jnp.maximum(
            counts[:, offset : offset + width], 1.0
        )
        pair_grad = cotangent[:, offset : offset + width].astype(jnp.float32) * scale[..., None]
        pair_low = pair_grad.astype(jnp.bfloat16).reshape(-1, Z)
        outer_grad = jnp.einsum(
            "ne,ke->nk", pair_low, output_weight, preferred_element_type=jnp.float32
        )
        outer_grad = outer_grad.astype(jnp.bfloat16).reshape(row_count, width, P_SIZE, P_SIZE)
        left_acc = left_acc + jnp.einsum(
            "ijpq,sjq->sip", outer_grad, right_cols, preferred_element_type=jnp.float32
        )
        pieces.append(
            jnp.einsum("ijpq,sip->sjq", outer_grad, left, preferred_element_type=jnp.float32)
        )
        outer = jnp.einsum(
            "sip,sjq->ijpq", left, right_cols, preferred_element_type=jnp.float32
        ).reshape(-1, P_SIZE * P_SIZE)
        outer_high = outer.astype(jnp.bfloat16)
        outer_rest = (outer - outer_high.astype(jnp.float32)).astype(jnp.bfloat16)
        weight_acc = weight_acc + jnp.einsum(
            "nk,ne->ke", outer_high, pair_low, preferred_element_type=jnp.float32
        )
        weight_acc = weight_acc + jnp.einsum(
            "nk,ne->ke", outer_rest, pair_low, preferred_element_type=jnp.float32
        )
        bias_acc = bias_acc + jnp.sum(pair_grad, axis=(0, 1))
    right_out = jnp.concatenate(pieces, axis=1)
    return (left_acc, right_out, weight_acc, bias_acc)


def local(
    alignment,
    norm_mean,
    norm_inverse,
    norm_gain,
    norm_shift,
    input_weight,
    input_bias,
    output_weight,
    pair_cotangent,
    residue_mask,
    sequence_mask,
):
    sequence_count, residue_count = sequence_mask.shape
    residue_total = residue_mask.shape[0]
    column = lax.axis_index("col")
    residue_float = residue_mask.astype(jnp.float32)
    own_residues = lax.dynamic_slice_in_dim(residue_float, column * residue_count, residue_count, 0)
    own_mask = lax.dynamic_slice_in_dim(residue_mask, column * residue_count, residue_count, 0)
    live_int = sequence_mask * own_mask[None, :]
    live = live_int.astype(jnp.float32)
    hatted, normed = normalize(alignment, norm_mean, norm_inverse, norm_gain, norm_shift)
    projected = project(normed, input_weight, input_bias, live)
    left = projected[..., :P_SIZE]
    right = projected[..., P_SIZE:]
    gathered, mask_cols = (
        lax.all_gather(
            right.reshape(sequence_count, residue_count * P_SIZE), "col", axis=1, tiled=True
        ),
        lax.all_gather(live_int, "col", axis=1, tiled=True),
    )
    right_all = gathered.reshape(sequence_count, residue_total, P_SIZE)
    partial_counts = jnp.dot(live.T, mask_cols.astype(jnp.float32), precision=lax.Precision.HIGHEST)
    counts = lax.psum(partial_counts, "row")
    pair_live = own_residues[:, None] * residue_float[None, :]
    left_grad, right_part, weight_out, bias_out = contract(
        left, right_all, counts, pair_cotangent, pair_live, output_weight
    )
    bias_out = bias_out / lax.axis_size("row")
    summed = lax.psum_scatter(
        right_part.reshape(sequence_count, residue_total * P_SIZE),
        "col",
        scatter_dimension=1,
        tiled=True,
    )
    right_grad = summed.reshape(sequence_count, residue_count, P_SIZE)
    proj_grad = jnp.concatenate([left_grad, right_grad], axis=-1) * live[..., None]
    proj_low = proj_grad.astype(jnp.bfloat16).reshape(-1, 2 * P_SIZE)
    flat_normed = normed.reshape(-1, C)
    weight_part = jnp.einsum("nc,nk->ck", flat_normed, proj_low, preferred_element_type=jnp.float32)
    bias_part = jnp.sum(proj_grad, axis=(0, 1))
    normed_grad = jnp.einsum(
        "nk,ck->nc", proj_low, input_weight, preferred_element_type=jnp.float32
    ).reshape(hatted.shape)
    gain_part = jnp.sum(normed_grad * hatted, axis=(0, 1))
    shift_part = jnp.sum(normed_grad, axis=(0, 1))
    hat_grad = normed_grad * norm_gain
    centered = (
        hat_grad
        - jnp.mean(hat_grad, axis=-1, keepdims=True)
        - hatted * jnp.mean(hat_grad * hatted, axis=-1, keepdims=True)
    )
    activation_grad = (norm_inverse[..., None] * centered).astype(jnp.bfloat16)
    totals = lax.psum(
        (weight_part, bias_part, gain_part, shift_part, weight_out, bias_out), ("row", "col")
    )
    return (activation_grad, totals[0], totals[1], totals[4], totals[5], totals[2], totals[3])


def solution(mesh):
    in_specs = (
        P(("group", "row"), "col", None),
        P(("group", "row"), "col"),
        P(("group", "row"), "col"),
        P(),
        P(),
        P(),
        P(),
        P(),
        P("col", "group", None),
        P("group"),
        P(("group", "row"), "col"),
    )
    out_specs = (
        P(("group", "row"), "col", None),
        P("group", None),
        P("group"),
        P("group", None),
        P("group"),
        P("group"),
        P("group"),
    )
    return jax.shard_map(local, mesh=mesh, in_specs=in_specs, out_specs=out_specs, check_vma=False)
```

profile of v0, /device:TPU:0, one launch (start us, length us, event | category | flops | bytes accessed | tf_op | source)
XLA Modules:
  0.0 233.0 jit_solution(2524973011357860974)
XLA Ops:
  7.2 0.0 copy-start
  7.2 0.0 copy-start.8
  7.2 0.0 copy-start.9
  7.2 0.0 copy-start.10
  7.2 0.0 reduce-scatter.2.cloned.1.call-start
  7.3 0.7 convert_element_type.57
  8.0 0.7 dynamic_slice.6
  8.7 0.8 fusion.16
  9.4 32.2 %all_gather.7 = s32[64,64]{0,1:T(8,128)S(1)} all-gather(s32[64,8]{0,1:T(8,128)S(1)} %get-tuple-element.20), channel_id=1, replica_groups=mesh['group'=2,'row'=2,'col'=8] {'col'}, dimensions={1}, use_global_device_ids=true | all-gather | bytes 18432 | tf_op jit(solution)/shard_map/all_gather | solution.py:96
  41.6 0.1 fusion.13
  41.8 2.5 %psum.49 = f32[8,64]{1,0:T(8,128)S(1)} all-reduce(f32[8,64]{1,0:T(8,128)S(1)} %fusion.13), channel_id=1, replica_groups=mesh['group'=2,'row'=2,'col'=8] {'row'}, use_global_device_ids=true, to_apply=%region_0.0 | all-reduce | flops 512 | bytes 4096 | tf_op jit(solution)/shard_map/psum | solution.py:100
  44.2 0.1 dynamic_slice.7
  44.3 0.1 maximum_divide_fusion
  44.4 1.6 fusion.4
  46.0 0.4 convolution_convert_fusion
  46.4 0.5 copy.30
  47.0 1.1 reshape.78
  48.1 0.0 copy-done.8
  48.1 0.1 copy.26
  48.2 0.1 copy.27
  48.3 0.5 copy-done.4
  48.8 0.6 copy-done.6
  49.4 1.3 convolution_add_fusion.1
  50.7 0.1 copy.28
  50.8 0.9 copy.29
  51.7 3.4 %copy.33 = bf16[64,32,8,32]{1,0,3,2:T(8,128)(2,1)} copy(bf16[64,32,8,32]{0,2,1,3:T(8,128)(2,1)S(1)} %bitcast.61) | data formatting | bytes 2097152 | tf_op jit(solution)/shard_map/ijpq,sip->sjq/dot_general | solution.py:49
  55.1 6.0 %dot_general.39 = bf16[2048,8,32]{0,2,1:T(8,128)(2,1)S(1)} reshape(bf16[64,32,8,32]{1,0,3,2:T(8,128)(2,1)} %copy.33) | data formatting | bytes 2097152 | tf_op jit(solution)/shard_map/ijpq,sip->sjq/dot_general | solution.py:49
  61.1 1.0 multiply_convert_fusion.1
  62.1 0.0 copy-start.1
  62.1 0.6 copy-done.1
  62.7 1.1 convolution_bitcast_fusion
  63.9 0.0 reduce-scatter.2.cloned.1.call-update
  63.9 0.0 all-reduce.4.cloned.1.call-start
  63.9 4.8 %copy.41 = bf16[8,64,32,32]{2,3,1,0:T(8,128)(2,1)} copy(bf16[8,64,32,32]{1,0,3,2:T(8,128)(2,1)S(1)} %reshape.78) | data formatting | bytes 2097152 | tf_op jit(solution)/shard_map/reshape | solution.py:44
  68.7 31.9 %all_gather.6 = bf16[64,2048]{0,1:T(8,128)(2,1)S(1)} all-gather(bf16[64,256]{0,1:T(8,128)(2,1)S(1)} %bitcast.68), channel_id=1, replica_groups=mesh['group'=2,'row'=2,'col'=8] {'col'}, dimensions={1}, use_global_device_ids=true | all-gather | bytes 294912 | tf_op jit(solution)/shard_map/all_gather | solution.py:93
  100.6 0.9 fusion
  101.5 2.1 copy.38
  103.7 4.1 %convert_element_type.64 = bf16[512,1024]{0,1:T(8,128)(2,1)} reshape(bf16[8,64,32,32]{1,0,3,2:T(8,128)(2,1)} %copy.38) | data formatting | bytes 2097152 | tf_op jit(solution)/shard_map/convert_element_type | solution.py:54
  107.7 2.1 copy.39
  109.9 3.2 %convert_element_type.67 = bf16[512,1024]{0,1:T(8,128)(2,1)S(1)} reshape(bf16[8,64,32,32]{1,0,3,2:T(8,128)(2,1)} %copy.39) | data formatting | bytes 2097152 | tf_op jit(solution)/shard_map/convert_element_type | solution.py:55
  113.1 1.7 fusion.17
  114.7 0.0 copy-start.3
  114.7 0.0 copy-start.5
  114.7 0.0 copy-start.7
  114.8 0.0 copy-start.12
  114.8 1.2 convolution_add_fusion
  116.0 3.4 %convolution_bitcast_fusion.1 = f32[64,8,32]{0,2,1:T(8,128)S(1)} fusion(bf16[64,64,32,1]{0,2,1,3:T(8,128)(2,1)S(1)} %bitcast.63, bf16[8,64,32,32]{2,3,1,0:T(8,128)(2,1)} %copy.41), kind=kOutput, calls=%fused_computation.6 | convolution fusion | flops 67108864 | bytes 1376256 | tf_op jit(solution)/shard_map/ijpq,sjq->sip/dot_general | solution.py:45
  119.5 8.1 %reduce-scatter.2.cloned.1.call-done = f32[64,256]{1,0:T(8,128)} async-done(((f32[64,2048]{1,0:T(8,128)}), f32[64,256]{1,0:T(8,128)}) %reduce-scatter.2.cloned.1.call-update) | async-done | bytes 65552 | tf_op jit(solution)/shard_map/reduce_scatter | solution.py:106
  127.5 0.9 copy.34
  128.5 0.1 fusion.6
  128.6 0.1 copy.35
  128.8 0.0 copy-done.3
  128.8 0.0 copy-done.5
  128.8 0.0 copy-done.7
  128.8 0.0 copy-done.12
  128.8 0.4 multiply_reduce_fusion
  129.3 0.0 copy-done.13
  129.3 1.0 convolution_bitcast_fusion.2
  130.3 0.0 all-reduce.4.cloned.1.call-update
  130.3 31.5 %all-reduce = (f32[64]{0:T(128)}, f32[128]{0:T(128)}, f32[256]{0:T(256)}, f32[256]{0:T(256)}) all-reduce(f32[64]{0:T(128)S(1)} %get-tuple-element.21, f32[128]{0:T(128)S(1)} %broadcast_multiply_fusion.3, f32[256]{0:T(256)S(1)} %get-tuple-element.7, f32[256]{0:T(256)S(1)} %get-tuple-element.10), channel_id=1, replica_groups=mesh['group'=2,'row'=2,'col'=8] {'row','col'}, use_global_device_ids=true, to_apply=%region_6.0 | all-reduce | flops 704 | bytes 5632 | tf_op jit(solution)/shard_map/psum | solution.py:130
  161.8 1.0 multiply_convert_fusion
  162.9 60.0 %all-reduce.4.cloned.1.call-done = (f32[256,64]{0,1:T(8,128)}, f32[1024,128]{1,0:T(8,128)}) async-done(((f32[256,64]{0,1:T(8,128)}, f32[1024,128]{1,0:T(8,128)}), (f32[256,64]{0,1:T(8,128)}, f32[1024,128]{1,0:T(8,128)})) %all-reduce.4.cloned.1.call-update) | async-done | bytes 589840 | tf_op jit(solution)/shard_map/psum | solution.py:130
  222.8 1.5 copy.55
  224.3 1.9 copy.56
  (14 shorter events, 0.0 us)
Async XLA Ops:
  7.2 38.8 %copy-start = (bf16[1024,128]{1,0:T(8,128)(2,1)S(1)}, bf16[1024,128]{1,0:T(8,128)(2,1)}, u32[]{:S(2)}) copy-start(bf16[1024,128]{1,0:T(8,128)(2,1)} %param.18) | copy-start | bytes 786436
  7.2 40.9 %copy-start.8 = (f32[64,8]{0,1:T(8,128)S(1)}, f32[64,8]{0,1:T(8,128)}, u32[]{:S(2)}) copy-start(f32[64,8]{0,1:T(8,128)} %param.13) | copy-start | bytes 6148
  7.2 41.0 %copy-start.9 = (f32[64,8]{0,1:T(8,128)S(1)}, f32[64,8]{0,1:T(8,128)}, u32[]{:S(2)}) copy-start(f32[64,8]{0,1:T(8,128)} %param.12) | copy-start | bytes 6148
  7.2 42.2 %copy-start.10 = (f32[256]{0:T(256)S(1)}, f32[256]{0:T(256)}, u32[]{:S(2)}) copy-start(f32[256]{0:T(256)} %param.14) | copy-start | bytes 3076
  7.2 120.3 %reduce-scatter.2.cloned.1.call-start = ((), (), s32[]{:S(2)}) async-start(), calls=%async_computation.1 | async-start | bytes 589824 | tf_op jit(solution)/shard_map/reduce_scatter | solution.py:106
  48.2 0.6 copy-start.4
  48.8 0.6 copy-start.6
  62.1 0.7 copy-start.1
  63.8 4.9 %slice-start = ((bf16[64,8,64]{0,2,1:T(8,128)(2,1)}), bf16[64,8,32]{0,2,1:T(8,128)(2,1)S(1)}, s32[]{:S(2)}) async-start(bf16[64,8,64]{0,2,1:T(8,128)(2,1)} %copy-done.1), calls=%async_computation.3 | async-start | bytes 131072 | tf_op jit(solution)/shard_map/slice | solution.py:91
  63.8 36.7 %copy-start.2 = (bf16[64,8,64]{0,2,1:T(8,128)(2,1)S(1)}, bf16[64,8,64]{0,2,1:T(8,128)(2,1)}, u32[]{:S(2)}) copy-start(bf16[64,8,64]{0,2,1:T(8,128)(2,1)} %copy-done.1) | copy-start | bytes 196612
  63.9 159.0 %all-reduce.4.cloned.1.call-start = ((), (), s32[]{:S(2)}) async-start(), calls=%async_computation.2 | async-start | bytes 1179648 | tf_op jit(solution)/shard_map/psum | solution.py:130
  107.7 5.3 %copy-start.11 = (f32[128]{0:T(128)S(1)}, f32[128]{0:T(128)}, u32[]{:S(2)}) copy-start(f32[128]{0:T(128)} %get-tuple-element.23) | copy-start | bytes 1540
  114.7 14.0 %copy-start.3 = (bf16[64,8,256]{2,1,0:T(8,128)(2,1)S(1)}, bf16[64,8,256]{2,1,0:T(8,128)(2,1)}, u32[]{:S(2)}) copy-start(bf16[64,8,256]{2,1,0:T(8,128)(2,1)} %param.11) | copy-start | bytes 786436
  114.7 14.0 %copy-start.5 = (f32[64,8]{1,0:T(8,128)S(1)}, f32[64,8]{1,0:T(8,128)}, u32[]{:S(2)}) copy-start(f32[64,8]{1,0:T(8,128)} %copy-done.4) | copy-start | bytes 6148
  114.7 14.0 %copy-start.7 = (f32[64,8]{1,0:T(8,128)S(1)}, f32[64,8]{1,0:T(8,128)}, u32[]{:S(2)}) copy-start(f32[64,8]{1,0:T(8,128)} %copy-done.6) | copy-start | bytes 6148
  114.8 14.0 %copy-start.12 = (bf16[256,64]{0,1:T(8,128)(2,1)S(1)}, bf16[256,64]{0,1:T(8,128)(2,1)}, u32[]{:S(2)}) copy-start(bf16[256,64]{0,1:T(8,128)(2,1)} %param.16) | copy-start | bytes 98308
  116.0 13.3 %copy-start.13 = (f32[256]{0:T(256)S(1)}, f32[256]{0:T(256)}, u32[]{:S(2)}) copy-start(f32[256]{0:T(256)} %param.15) | copy-start | bytes 3076
Sparse Core Ops, SparseCore 0:
  64.0 63.4 reduce-scatter.1
  132.0 90.7 all-reduce.3
where the time goes:
time: 234 us; the launch traced here: 233 us
  blocking collectives  98.1 us (42%)
  waiting for transfers between devices  68.1 us (29%)
  local copies, waits for them, and re-layouts  35.5 us (15%)
  between operations  14.3 us (6%)
  matrix products  11.7 us (5%)
  other arithmetic  5.27 us (2%)
    psum x1, waiting for transfers between devices, local(): lax.psum((weight_part, bias_part, gain_part, shift_part, weight_out, bias...  60 us
    all_gather x1, blocking collectives, local(): lax.all_gather(live_int, 'col', axis=1, tiled=True)  32.2 us
    all_gather x1, blocking collectives, local(): lax.all_gather(right.reshape(sequence_count, residue_count * P_SIZE), 'co...  31.9 us
    psum x1, blocking collectives, local(): lax.psum((weight_part, bias_part, gain_part, shift_part, weight_out, bias...  31.5 us
    dot_general x2, local copies, waits for them, and re-layouts, contract(): jnp.einsum('ijpq,sip->sjq', outer_grad, left, preferred_element_type=jnp....  9.41 us
    reduce_scatter x1, waiting for transfers between devices, local(): lax.psum_scatter(right_part.reshape(sequence_count, residue_total * P_SIZ...  8.08 us
    convert_element_type x2, local copies, waits for them, and re-layouts, contract(): outer_high = outer.astype(jnp.bfloat16)  6.19 us
    reshape x2, local copies, waits for them, and re-layouts, contract(): outer_grad.astype(jnp.bfloat16).reshape(row_count, width, P_SIZE, P_SIZE)  5.88 us
  transfers between devices with their start and end apart: 2, of which 2 were waited for; matrix products, arithmetic and copies ran while one was open for 11% of the time, Pallas kernels for 0%

commit v1 on v0

--- a/solution.py
+++ b/solution.py
@@ -3,6 +3,8 @@
 import jax
 import jax.numpy as jnp
 from jax import lax
+from jax.experimental import pallas as pl
+from jax.experimental.pallas import tpu as pltpu
 from jax.sharding import PartitionSpec as P
 
 C = 256
@@ -64,7 +66,7 @@
     return (left_acc, right_out, weight_acc, bias_acc)
 
 
-def local(
+def general(
     alignment,
     norm_mean,
     norm_inverse,
@@ -133,6 +135,415 @@
     return (activation_grad, totals[0], totals[1], totals[4], totals[5], totals[2], totals[3])
 
 
+LANES = 128
+PROJ_ROWS = 256
+MASK_AT = 256
+TURNED_AT = 272
+SLICE_AT = 336
+MESSAGE = 400
+SMALL_AT = 256
+PARTIAL = 288
+VMEM = pltpu.CompilerParams(vmem_limit_bytes=48 * 1024 * 1024)
+F32 = jnp.float32
+BF16 = jnp.bfloat16
+
+
+def dot_nt(a, b):
+    return lax.dot_general(a, b, (((1,), (1,)), ((), ())), preferred_element_type=F32)
+
+
+def dot_nn(a, b):
+    return lax.dot_general(a, b, (((1,), (0,)), ((), ())), preferred_element_type=F32)
+
+
+def low_lanes(shape):
+    return lax.broadcasted_iota(jnp.int32, shape, 1) < LANES // 2
+
+
+def swap_halves(x):
+    return pltpu.roll(x, LANES // 2, 1)
+
+
+def columns_of(square, rows):
+    at = 0
+    for block in rows:
+        square[at : at + block.shape[0], : block.shape[1]] = block
+        at += block.shape[0]
+    return square[...].T
+
+
+def spread(wide, alignment):
+    values = alignment[...].astype(F32)
+    for h in range(2):
+        wide[h, 0 : values.shape[0] * values.shape[1], :] = values[
+            :, :, h * LANES : (h + 1) * LANES
+        ].reshape(-1, LANES)
+
+
+def strided(wide, start, size, stride):
+    return jnp.concatenate([wide[h, pl.ds(start, size, stride=stride), :] for h in range(2)], axis=1)
+
+
+def prepare(
+    column, residue, alignment, mean, inverse, gain, shift, weight, bias, mask, mate, cotangent, *rest
+):
+    count = (len(rest) - 4) // 1
+    messages, (wide, packed, cot, turned) = rest[:count], rest[count:]
+    col = column[0]
+    seqs, own, channels = alignment.shape
+    square = cot.at[0:LANES, :]
+    stats = columns_of(
+        square, [mean[...], inverse[...], jnp.broadcast_to(bias[...], (8, bias.shape[1]))]
+    )
+    row = lax.broadcasted_iota(jnp.int32, (own, LANES), 0)
+    present = jnp.zeros((own, LANES), F32)
+    for r in range(own):
+        present = jnp.where(row == r, residue[col * own + r].astype(F32), present)
+    live = jnp.concatenate([mask[...], mate[...]], axis=1).astype(F32) * present
+    spread(wide, alignment)
+    for r in range(own):
+        hatted = (strided(wide, r, seqs, own) - stats[:seqs, r : r + 1]) * stats[
+            :seqs, own + r : own + r + 1
+        ]
+        normed = (hatted * gain[...] + shift[...]).astype(BF16)
+        projected = dot_nt(weight[...], normed) + stats[: 2 * P_SIZE, 2 * own : 2 * own + 1]
+        projected = projected * live[r : r + 1, :seqs]
+        packed[pl.ds(r, P_SIZE, stride=own), :] = jnp.concatenate(
+            [projected[:P_SIZE], projected[P_SIZE:]], axis=1
+        )
+    shared = packed[...].astype(BF16)
+    masks = jnp.concatenate([live, present], axis=0).astype(BF16)
+    total = cotangent.shape[1]
+    cot[...] = cotangent[...].astype(F32).reshape(own * total, Z)
+    for i in range(own // 2):
+        pair = jnp.concatenate(
+            [cot[i * total : (i + 1) * total, :], cot[(i + own // 2) * total : (i + own // 2 + 1) * total, :]],
+            axis=0,
+        )
+        turned[i] = pair.T.astype(BF16)
+    depth = Z // count
+    for k in range(count):
+        peer = col ^ k
+        out = messages[k]
+        out[0:PROJ_ROWS, :] = shared
+        out[MASK_AT:TURNED_AT, :] = masks
+        out[TURNED_AT:SLICE_AT, :] = jnp.concatenate(
+            [cot[pl.ds(own * peer + j, own, stride=total), :] for j in range(own)], axis=0
+        ).astype(BF16)
+        for i in range(own // 2):
+            out[SLICE_AT + i * depth : SLICE_AT + (i + 1) * depth, :] = turned[
+                i, pl.ds(pl.multiple_of(peer * depth, depth), depth), :
+            ]
+
+
+def interleave(product, target, group, at):
+    half = LANES // 2
+    low = low_lanes((P_SIZE, LANES))
+    for a in range(0, product.shape[0] // P_SIZE, 2):
+        for b in range(0, group, 2):
+            first = product[a * P_SIZE : (a + 1) * P_SIZE, b * half : (b + 2) * half]
+            second = product[(a + 1) * P_SIZE : (a + 2) * P_SIZE, b * half : (b + 2) * half]
+            lanes = slice((at + a) * half, (at + a + 2) * half)
+            target[b * P_SIZE : (b + 1) * P_SIZE, lanes] = jnp.where(
+                low, first, swap_halves(second)
+            ).astype(BF16)
+            target[(b + 1) * P_SIZE : (b + 2) * P_SIZE, lanes] = jnp.where(
+                low, swap_halves(first), second
+            ).astype(BF16)
+
+
+def work(
+    column, cotangent, out_weight, alignment, mean, inverse, gain, shift, weight, *rest
+):
+    count = len(rest) - 15
+    messages = rest[:count]
+    activation, partial = rest[count : count + 2]
+    (every, live_all, present_all, turned, slices, grad_own, grad_turned, grad_slice, left_outer, right_outer, right_rows, mixed, wide) = rest[count + 2 :]
+    col = column[0]
+    seqs, own, channels = alignment.shape
+    total = cotangent.shape[1]
+    depth = Z // count
+    half = LANES // 2
+    pairs = own // 2
+    for k in range(count):
+        peer = col ^ k
+        at = pl.multiple_of(peer * own, own)
+        message = messages[k]
+        block = message[0:PROJ_ROWS, :].astype(F32)
+        for q in range(P_SIZE):
+            every[pl.ds(q * total + at, own), :] = block[q * own : (q + 1) * own]
+        masks = message[MASK_AT:TURNED_AT, :].astype(F32)
+        live_all[pl.ds(at, own), :] = masks[:own]
+        present_all[pl.ds(at, own), :] = masks[own:]
+        block = message[TURNED_AT:SLICE_AT, :].astype(F32)
+        for j in range(own):
+            turned[pl.ds(j * total + at, own), :] = block[j * own : (j + 1) * own]
+        slices[peer] = message[SLICE_AT:MESSAGE, :]
+    live = live_all[...].astype(BF16)
+    present = present_all[...].astype(BF16)
+    masks = messages[0][MASK_AT:TURNED_AT, :]
+    live_own = masks[:own].astype(F32)
+    present_own = masks[own:]
+
+    def scale_of(live_other, present_other):
+        counts = dot_nt(live, live_other)
+        return dot_nt(present, present_other) * (1.0 / LANES) / jnp.maximum(counts, 1.0)
+
+    scale_own = scale_of(masks[:own], present_own)
+    scale_twice = scale_of(
+        jnp.concatenate([live, live], axis=0), jnp.concatenate([present, present], axis=0)
+    )
+    for i in range(own):
+        rows = slice(i * total, (i + 1) * total)
+        grad_own[rows, :] = (cotangent[i].astype(F32) * scale_own[:, i : i + 1]).astype(BF16)
+        grad_turned[rows, :] = (turned[rows, :] * scale_own[:, i : i + 1]).astype(BF16)
+    low = low_lanes((own, LANES))
+    bias_acc = jnp.zeros((depth, LANES), F32)
+    for c in range(count):
+        tile = scale_twice[c * own : (c + 1) * own]
+        tile = jnp.where(low, tile, jnp.concatenate([tile[pairs:], tile[:pairs]], axis=0))
+        for i in range(pairs):
+            piece = slices[c, i * depth : (i + 1) * depth, :].astype(F32) * tile[i : i + 1, :]
+            bias_acc = bias_acc + piece
+            grad_slice[(c * pairs + i) * depth : (c * pairs + i + 1) * depth, :] = piece.astype(BF16)
+
+    wide[0] = out_weight[...].astype(F32)
+    eight = 8
+    for a in range(0, P_SIZE, eight):
+        rows = slice(a * P_SIZE, (a + eight) * P_SIZE)
+        by_second = jnp.concatenate(
+            [wide[0, pl.ds(q, P_SIZE, stride=P_SIZE), :] for q in range(a, a + eight)], axis=0
+        ).astype(BF16)
+        interleave(dot_nt(by_second, grad_own[...]), left_outer, own, a)
+        interleave(dot_nt(out_weight[rows, :], grad_turned[...]), right_outer, own, a)
+    gathered = every[...].astype(BF16)
+    left_grad = swap_halves(dot_nn(left_outer[...], gathered))
+    right_grad = dot_nn(right_outer[...], gathered)
+
+    square = wide.at[0, 0:LANES, :]
+    stats = columns_of(square, [mean[...], inverse[...]])
+    spread(wide, alignment)
+    input_acc = jnp.zeros((2 * P_SIZE, channels), F32)
+    proj_acc = jnp.zeros((2 * P_SIZE, seqs), F32)
+    gain_acc = jnp.zeros((1, channels), F32)
+    shift_acc = jnp.zeros((1, channels), F32)
+    for r in range(own):
+        spot = pl.ds(r, seqs, stride=own)
+        scale = stats[:seqs, own + r : own + r + 1]
+        hatted = (strided(wide, r, seqs, own) - stats[:seqs, r : r + 1]) * scale
+        normed = (hatted * gain[...] + shift[...]).astype(BF16)
+        rows = slice(r * P_SIZE, (r + 1) * P_SIZE)
+        proj_grad = jnp.concatenate([left_grad[rows, :seqs], right_grad[rows, :seqs]], axis=0)
+        proj_grad = proj_grad * live_own[r : r + 1, :seqs]
+        proj_acc = proj_acc + proj_grad
+        input_acc = input_acc + dot_nn(proj_grad.astype(BF16), normed)
+        normed_grad = dot_nn(proj_grad.T.astype(BF16), weight[...])
+        gain_acc = gain_acc + jnp.sum(normed_grad * hatted, axis=0, keepdims=True)
+        shift_acc = shift_acc + jnp.sum(normed_grad, axis=0, keepdims=True)
+        hat_grad = normed_grad * gain[...]
+        first = jnp.sum(hat_grad, axis=1, keepdims=True) * (1.0 / channels)
+        second = jnp.sum(hat_grad * hatted, axis=1, keepdims=True) * (1.0 / channels)
+        result = scale * (hat_grad - first - hatted * second)
+        for h in range(2):
+            wide[h, spot, :] = result[:, h * LANES : (h + 1) * LANES]
+    activation[...] = jnp.concatenate(
+        [wide[h, 0 : seqs * own, :].reshape(seqs, own, LANES) for h in range(2)], axis=2
+    ).astype(BF16)
+
+    right_rows[0:total, :] = jnp.zeros((total, P_SIZE * half), BF16)
+    right_rows[2 * total : 3 * total, :] = jnp.zeros((total, P_SIZE * half), BF16)
+    low = low_lanes((total, LANES))
+    for q in range(0, P_SIZE, 2):
+        first = every[q * total : (q + 1) * total, :]
+        second = every[(q + 1) * total : (q + 2) * total, :]
+        right_rows[total : 2 * total, q * half : (q + 2) * half] = jnp.where(
+            low, swap_halves(first), second
+        ).astype(BF16)
+    low = low_lanes((P_SIZE, LANES))
+    none = jnp.zeros((P_SIZE, LANES), BF16)
+    weight_acc = jnp.zeros((LANES, LANES), F32)
+    quarter = 4
+    for top in range(2):
+        right_side = right_rows[(1 - top) * total : (3 - top) * total, :]
+        for c0 in range(0, count, quarter):
+            span = quarter * pairs * depth
+            mixed[...] = dot_nn(
+                grad_slice[c0 * pairs * depth : c0 * pairs * depth + span, :], right_side
+            ).astype(BF16)
+            for c in range(quarter):
+                for i in range(pairs):
+                    at = (c * pairs + i) * depth
+                    lhs = jnp.concatenate(
+                        [mixed[at : at + depth, a * 256 : (a + 1) * 256] for a in range(8)], axis=0
+                    )
+                    left = every[pl.ds((c0 + c) * own + top * pairs + i, P_SIZE, stride=total), :]
+                    left = jnp.where(low, left, 0.0)
+                    moved = swap_halves(left).astype(BF16)
+                    left = left.astype(BF16)
+                    rhs = jnp.concatenate(
+                        [
+                            jnp.concatenate([left, none], axis=1),
+                            jnp.concatenate([moved, none], axis=1),
+                            jnp.concatenate([none, left], axis=1),
+                            jnp.concatenate([none, moved], axis=1),
+                        ],
+                        axis=0,
+                    )
+                    weight_acc = weight_acc + dot_nt(lhs, rhs)
+
+    square[...] = jnp.zeros((LANES, LANES), F32)
+    square[0 : 2 * P_SIZE, :seqs] = proj_acc
+    square[half : half + depth, :] = bias_acc
+    sums = jnp.sum(square[...].T, axis=0, keepdims=True)
+    small = jnp.concatenate(
+        [gain_acc[:, :LANES], gain_acc[:, LANES:], shift_acc[:, :LANES], shift_acc[:, LANES:], sums, jnp.zeros((11, LANES), F32)],
+        axis=0,
+    )
+    high = small.astype(BF16)
+    rest_of = (small - high.astype(F32)).astype(BF16)
+    whole = jnp.concatenate(
+        [weight_acc.astype(BF16), input_acc[:, :LANES].astype(BF16), input_acc[:, LANES:].astype(BF16), high, rest_of],
+        axis=0,
+    )
+    for k in range(count):
+        partial[k] = whole
+
+
+def finish(own, mate, input_out, bias_out, weight_out, out_bias_out, gain_out, shift_out):
+    count = own.shape[0]
+    depth = Z // count
+    input_acc = jnp.zeros((LANES, LANES), F32)
+    small_acc = jnp.zeros((16, LANES), F32)
+    lane = lax.broadcasted_iota(jnp.int32, (1, LANES), 1)
+    out_bias = jnp.zeros((1, LANES), F32)
+    pieces = []
+    for k in range(count):
+        mine = own[k].astype(F32)
+        both = mine + mate[k].astype(F32)
+        pieces.append(both[:LANES])
+        input_acc = input_acc + both[LANES:SMALL_AT]
+        small_acc = small_acc + (both[SMALL_AT : SMALL_AT + 16] + both[SMALL_AT + 16 :])
+        bias = mine[SMALL_AT + 4 : SMALL_AT + 5] + mine[SMALL_AT + 20 : SMALL_AT + 21]
+        bias = pltpu.roll(bias, (k * depth + LANES // 2) % LANES, 1)
+        out_bias = jnp.where((lane >= k * depth) & (lane < (k + 1) * depth), bias, out_bias)
+    for a in range(8):
+        turned = jnp.concatenate([p[a * depth : (a + 1) * depth] for p in pieces], axis=0).T
+        for b in range(4):
+            weight_out[pl.ds(4 * a + b, P_SIZE, stride=P_SIZE), :] = turned[b * P_SIZE : (b + 1) * P_SIZE]
+    input_out[:, :LANES] = input_acc[: LANES // 2]
+    input_out[:, LANES:] = input_acc[LANES // 2 :]
+    gain_out[:, :LANES] = small_acc[0:1]
+    gain_out[:, LANES:] = small_acc[1:2]
+    shift_out[:, :LANES] = small_acc[2:3]
+    shift_out[:, LANES:] = small_acc[3:4]
+    bias_out[...] = small_acc[4:5, : LANES // 2]
+    out_bias_out[...] = out_bias
+
+
+def shape(dims, dtype):
+    return jax.ShapeDtypeStruct(dims, dtype)
+
+
+def tiled(
+    alignment,
+    norm_mean,
+    norm_inverse,
+    norm_gain,
+    norm_shift,
+    input_weight,
+    input_bias,
+    output_weight,
+    pair_cotangent,
+    residue_mask,
+    sequence_mask,
+):
+    count = lax.axis_size("col")
+    seqs, own, channels = alignment.shape
+    total = pair_cotangent.shape[1]
+    column = lax.axis_index("col").reshape(1).astype(jnp.int32)
+    mask = sequence_mask.T
+    mate = lax.ppermute(mask, "row", [(0, 1), (1, 0)])
+    mean, inverse = norm_mean.T, norm_inverse.T
+    gain, shift = norm_gain[None, :], norm_shift[None, :]
+    weight = input_weight.T
+    smem = pl.BlockSpec(memory_space=pltpu.SMEM)
+    vmem = pl.BlockSpec(memory_space=pltpu.VMEM)
+    messages = pl.pallas_call(
+        prepare,
+        out_shape=[shape((MESSAGE, LANES), BF16)] * count,
+        in_specs=[smem, smem] + [vmem] * 10,
+        out_specs=[vmem] * count,
+        scratch_shapes=[
+            pltpu.VMEM((2, seqs * own, LANES), F32),
+            pltpu.VMEM((PROJ_ROWS, LANES), F32),
+            pltpu.VMEM((own * total, Z), F32),
+            pltpu.VMEM((own // 2, Z, LANES), BF16),
+        ],
+        compiler_params=VMEM,
+        name="prepare",
+    )(column, residue_mask, alignment, mean, inverse, gain, shift, weight, input_bias[None, :], mask, mate, pair_cotangent)
+    received = [messages[0]] + [
+        lax.ppermute(messages[k], "col", [(c, c ^ k) for c in range(count)]) for k in range(1, count)
+    ]
+    activation, partial = pl.pallas_call(
+        work,
+        out_shape=[shape(alignment.shape, BF16), shape((count, PARTIAL, LANES), BF16)],
+        in_specs=[smem] + [vmem] * (8 + count),
+        out_specs=[vmem] * 2,
+        scratch_shapes=[
+            pltpu.VMEM((P_SIZE * total, LANES), F32),
+            pltpu.VMEM((total, LANES), F32),
+            pltpu.VMEM((total, LANES), F32),
+            pltpu.VMEM((own * total, Z), F32),
+            pltpu.VMEM((count, MESSAGE - SLICE_AT, LANES), BF16),
+            pltpu.VMEM((own * total, Z), BF16),
+            pltpu.VMEM((own * total, Z), BF16),
+            pltpu.VMEM((count * (MESSAGE - SLICE_AT), LANES), BF16),
+            pltpu.VMEM((own * P_SIZE, P_SIZE * total), BF16),
+            pltpu.VMEM((own * P_SIZE, P_SIZE * total), BF16),
+            pltpu.VMEM((3 * total, P_SIZE * seqs), BF16),
+            pltpu.VMEM((4 * (MESSAGE - SLICE_AT), P_SIZE * seqs), BF16),
+            pltpu.VMEM((2, P_SIZE * P_SIZE, LANES), F32),
+        ],
+        compiler_params=VMEM,
+        name="work",
+    )(column, pair_cotangent, output_weight, alignment, mean, inverse, gain, shift, weight, *received)
+    ours = lax.all_to_all(partial, "col", 0, 0)
+    theirs = lax.ppermute(ours, "row", [(0, 1), (1, 0)])
+    input_grad, bias_grad, weight_grad, out_bias_grad, gain_grad, shift_grad = pl.pallas_call(
+        finish,
+        out_shape=[
+            shape((2 * P_SIZE, channels), F32),
+            shape((1, 2 * P_SIZE), F32),
+            shape((P_SIZE * P_SIZE, Z), F32),
+            shape((1, Z), F32),
+            shape((1, channels), F32),
+            shape((1, channels), F32),
+        ],
+        in_specs=[vmem] * 2,
+        out_specs=[vmem] * 6,
+        compiler_params=VMEM,
+        name="finish",
+    )(ours, theirs)
+    return (activation, input_grad.T, bias_grad[0], weight_grad, out_bias_grad[0], gain_grad[0], shift_grad[0])
+
+
+def local(*args):
+    alignment, cotangent = args[0], args[8]
+    seqs, own, channels = alignment.shape
+    total = cotangent.shape[1]
+    count = lax.axis_size("col")
+    fits = (
+        2 * seqs == LANES
+        and 2 * total == LANES
+        and own == 8
+        and channels == 2 * LANES
+        and count == 8
+        and lax.axis_size("row") == 2
+    )
+    return tiled(*args) if fits else general(*args)
+
+
 def solution(mesh):
     in_specs = (
         P(("group", "row"), "col", None),

time: 234 us -> 63.1 us (0.27)
  blocking collectives: 98.1 us -> 22.9 us
  waiting for transfers between devices: 68.1 us -> 13.7 us
  local copies, waits for them, and re-layouts: 35.5 us -> 4.27 us
  between operations: 14.3 us -> 0.71 us
  starting transfers between devices: 0.08 us -> 12.9 us
  matrix products: 11.7 us -> 0 us
  Pallas kernels: 0 us -> 8.3 us
  other arithmetic: 5.27 us -> 0 us
    all_gather x2 -> x0, blocking collectives: 64.1 us -> none  [the longest x1 32.2 us: local(): lax.all_gather(live_int, 'col', axis=1, tiled=True)]
    psum x1 -> x0, waiting for transfers between devices: 60 us -> none  [local(): lax.psum((weight_part, bias_part, gain_part, shift_part, weight_out, bias...]
    psum x2 -> x0, blocking collectives: 34 us -> none  [the longest x1 31.5 us: local(): lax.psum((weight_part, bias_part, gain_part, shift_part, weight_out, bias...]
    all_to_all x0 -> x1, blocking collectives: none -> 22.9 us  [tiled(): ours = lax.all_to_all(partial, 'col', 0, 0)]
    ppermute x0 -> x9, waiting for transfers between devices: none -> 13.7 us  [the longest x7 10.6 us: tiled(): lax.ppermute(messages[k], 'col', [(c, c ^ k) for c in range(count)])]
    ppermute x0 -> x9, starting transfers between devices: none -> 12.9 us  [the longest x7 12.4 us: tiled(): lax.ppermute(messages[k], 'col', [(c, c ^ k) for c in range(count)])]
    convert_element_type x6 -> x0, local copies, waits for them, and re-layouts: 12.2 us -> none  [the longest x2 6.19 us: contract(): outer_high = outer.astype(jnp.bfloat16)]
    dot_general x10 -> x0, matrix products: 11.7 us -> none  [the longest x1 3.44 us: contract(): jnp.einsum('ijpq,sjq->sip', outer_grad, right_cols, preferred_element_typ...]
  transfers between devices with their start and end apart: 2 -> 9, of which waited for: 2 -> 3; matrix products, arithmetic and copies ran while one was open for 11% -> 0% of each run, Pallas kernels for 0% -> 0%
where the time goes in v1:
time: 63.1 us; the launch traced here: 62.8 us
  blocking collectives  22.9 us (36%)
  waiting for transfers between devices  13.7 us (22%)
  starting transfers between devices  12.9 us (20%)
  Pallas kernels  8.3 us (13%)
  local copies, waits for them, and re-layouts  4.27 us (7%)
  between operations  0.71 us (1%)
    all_to_all x1, blocking collectives, tiled(): ours = lax.all_to_all(partial, 'col', 0, 0)  22.9 us
    ppermute x7, starting transfers between devices, tiled(): lax.ppermute(messages[k], 'col', [(c, c ^ k) for c in range(count)])  12.4 us
    ppermute x7, waiting for transfers between devices, tiled(): lax.ppermute(messages[k], 'col', [(c, c ^ k) for c in range(count)])  10.6 us
    pallas_call x1, Pallas kernels, tiled(): pl.pallas_call(work, out_shape=[shape(alignment.shape, BF16), shape((coun...  5.77 us
    unnamed x26, local copies, waits for them, and re-layouts  4.27 us
    ppermute x1, waiting for transfers between devices, tiled(): theirs = lax.ppermute(ours, 'row', [(0, 1), (1, 0)])  2 us
    pallas_call x1, Pallas kernels, tiled(): pl.pallas_call(finish, out_shape=[shape((2 * P_SIZE, channels), F32), sha...  1.27 us
  transfers between devices with their start and end apart: 9, of which 3 were waited for; matrix products, arithmetic and copies ran while one was open for 0% of the time, Pallas kernels for 0%

profile of v1, /device:TPU:0, one launch (start us, length us, event | category | flops | bytes accessed | tf_op | source)
XLA Modules:
  0.0 62.8 jit_solution(11377569254862831491)
XLA Ops:
  0.6 0.5 collective-permute-start
  1.2 0.0 copy-start.10
  1.2 0.0 copy-start.11
  1.2 0.0 copy-start.12
  1.2 1.0 %collective-permute-done.mate = s32[8,64]{1,0:T(8,128)S(1)} collective-permute-done((s32[8,64]{1,0:T(8,128)}, s32[8,64]{1,0:T(8,128)S(1)}, u32[]{:S(2)}, u32[]{:S(2)}) %collective-permute-start) | collective-permute-done | bytes 2080 | tf_op jit(solution)/shard_map/ppermute | solution.py:465
  2.2 0.0 copy-start.8
  2.2 0.0 copy-start.7
  2.2 0.0 copy-start.6
  2.2 0.0 copy-start.9
  2.2 0.0 copy-done.10
  2.2 0.0 copy-done.11
  2.2 0.0 copy-done.12
  2.2 0.7 %copy-done.8 = s32[64,8]{0,1:T(8,128)S(1)} copy-done((s32[64,8]{0,1:T(8,128)S(1)}, s32[64,8]{0,1:T(8,128)}, u32[]{:S(2)}) %copy-start.8) | copy-done | bytes 2072
  2.9 0.0 copy-done.7
  2.9 0.0 copy-done.6
  2.9 0.0 copy-done.9
  2.9 0.0 copy-start
  2.9 0.9 %copy-done = bf16[64,8,256]{2,1,0:T(8,128)(2,1)S(1)} copy-done((bf16[64,8,256]{2,1,0:T(8,128)(2,1)S(1)}, bf16[64,8,256]{2,1,0:T(8,128)(2,1)}, u32[]{:S(2)}) %copy-start) | copy-done | bytes 262168
  3.9 0.0 copy-start.2
  3.9 0.9 %copy-done.2 = bf16[8,64,128]{2,1,0:T(8,128)(2,1)S(1)} copy-done((bf16[8,64,128]{2,1,0:T(8,128)(2,1)S(1)}, bf16[8,64,128]{2,1,0:T(8,128)(2,1)}, u32[]{:S(2)}) %copy-start.2) | copy-done | bytes 131096
  4.8 0.0 copy-start.5
  4.8 0.8 %copy-done.5 = bf16[256,64]{0,1:T(8,128)(2,1)S(1)} copy-done((bf16[256,64]{0,1:T(8,128)(2,1)S(1)}, bf16[256,64]{0,1:T(8,128)(2,1)}, u32[]{:S(2)}) %copy-start.5) | copy-done | bytes 32792
  5.5 0.0 copy-start.1
  5.5 0.0 copy-start.3
  5.5 1.3 %prepare.1 = (bf16[400,128]{1,0:T(8,128)(2,1)S(1)}, bf16[400,128]{1,0:T(8,128)(2,1)S(1)}, bf16[400,128]{1,0:T(8,128)(2,1)S(1)}, bf16[400,128]{1,0:T(8,128)(2,1)S...) custom-call(s32[1]{0:T(128)} %bitcast.column, ...), custom_call_target="tpu_custom_call" | custom-call | tf_op jit(solution)/shard_map/prepare/pallas_call | solution.py:471
  6.8 2.9 %collective-permute-start.1 = (bf16[400,128]{1,0:T(8,128)(2,1)S(1)}, bf16[400,128]{1,0:T(8,128)(2,1)S(1)}, u32[]{:S(2)}, u32[]{:S(2)}) collective-permute-start(bf16[400,128]{1,0:T(8,128)(2,1)S(1)} %get-tuple-element.24), channel_id=1, source_target_pairs={{0,1},{1,0},{2,3},{3,2},{4,5},{5,4},{6,7},{7,6},{8,9},{9,8},{10,11... | collective-permute-start | bytes 307208 | tf_op jit(solution)/shard_map/ppermute | solution.py:486
  9.7 1.6 %collective-permute-start.2 = (bf16[400,128]{1,0:T(8,128)(2,1)S(1)}, bf16[400,128]{1,0:T(8,128)(2,1)S(1)}, u32[]{:S(2)}, u32[]{:S(2)}) collective-permute-start(bf16[400,128]{1,0:T(8,128)(2,1)S(1)} %get-tuple-element.25), channel_id=1, source_target_pairs={{0,2},{1,3},{2,0},{3,1},{4,6},{5,7},{6,4},{7,5},{8,10},{9,11},{10,... | collective-permute-start | bytes 307208 | tf_op jit(solution)/shard_map/ppermute | solution.py:486
  11.3 0.0 collective-permute-start.3
  11.3 3.0 %collective-permute-start.4 = (bf16[400,128]{1,0:T(8,128)(2,1)S(1)}, bf16[400,128]{1,0:T(8,128)(2,1)S(1)}, u32[]{:S(2)}, u32[]{:S(2)}) collective-permute-start(bf16[400,128]{1,0:T(8,128)(2,1)S(1)} %get-tuple-element.27), channel_id=1, source_target_pairs={{0,4},{1,5},{2,6},{3,7},{4,0},{5,1},{6,2},{7,3},{8,12},{9,13},{10,... | collective-permute-start | bytes 307208 | tf_op jit(solution)/shard_map/ppermute | solution.py:486
  14.3 1.3 %collective-permute-start.5 = (bf16[400,128]{1,0:T(8,128)(2,1)S(1)}, bf16[400,128]{1,0:T(8,128)(2,1)S(1)}, u32[]{:S(2)}, u32[]{:S(2)}) collective-permute-start(bf16[400,128]{1,0:T(8,128)(2,1)S(1)} %get-tuple-element.28), channel_id=1, source_target_pairs={{0,5},{1,4},{2,7},{3,6},{4,1},{5,0},{6,3},{7,2},{8,13},{9,12},{10,... | collective-permute-start | bytes 307208 | tf_op jit(solution)/shard_map/ppermute | solution.py:486
  15.6 0.0 collective-permute-done.1.rest_1_
  15.6 3.6 %collective-permute-start.6 = (bf16[400,128]{1,0:T(8,128)(2,1)S(1)}, bf16[400,128]{1,0:T(8,128)(2,1)S(1)}, u32[]{:S(2)}, u32[]{:S(2)}) collective-permute-start(bf16[400,128]{1,0:T(8,128)(2,1)S(1)} %get-tuple-element.29), channel_id=1, source_target_pairs={{0,6},{1,7},{2,4},{3,5},{4,2},{5,3},{6,0},{7,1},{8,14},{9,15},{10,... | collective-permute-start | bytes 307208 | tf_op jit(solution)/shard_map/ppermute | solution.py:486
  19.2 0.0 collective-permute-done.2.rest_2_
  19.2 0.0 collective-permute-start.7
  19.2 0.0 collective-permute-done.3.rest_3_
  19.2 0.0 collective-permute-done.4.rest_4_
  19.2 10.6 %collective-permute-done.5.rest_5_ = bf16[400,128]{1,0:T(8,128)(2,1)S(1)} collective-permute-done((bf16[400,128]{1,0:T(8,128)(2,1)S(1)}, bf16[400,128]{1,0:T(8,128)(2,1)S(1)}, u32[]{:S(2)}, u32[]{:S(2)}) %collective-permute-start.5) | collective-permute-done | bytes 102432 | tf_op jit(solution)/shard_map/ppermute | solution.py:486
  29.8 0.0 collective-permute-done.6.rest_6_
  29.8 0.0 collective-permute-done.7.rest_7_
  29.8 0.0 copy-done.1
  29.8 0.0 copy-done.3
  29.8 0.0 copy-start.4
  29.8 0.9 %copy-done.4 = bf16[1024,128]{1,0:T(8,128)(2,1)S(1)} copy-done((bf16[1024,128]{1,0:T(8,128)(2,1)S(1)}, bf16[1024,128]{1,0:T(8,128)(2,1)}, u32[]{:S(2)}) %copy-start.4) | copy-done | bytes 262168
  30.8 5.8 %work.1 = (bf16[64,8,256]{2,1,0:T(8,128)(2,1)}, bf16[8,288,128]{2,1,0:T(8,128)(2,1)S(1)}) custom-call(s32[1]{0:T(128)} %bitcast.column, bf16[8,64,128]{2,1,0:T(8,128)(2,1)S(1)} %copy-done.3, bf16[1024,128]{1,0:T(8,128)(2,1)S(1)} %copy-done.4, bf16[64,8,256]{2,1,0:T(8,128)(2,1)S(1)} %copy-done.1, f32[8,64]{1,0:T(8,128)S(1)} %bitcast.16, ...), custom_call_target="tpu_custom_call" | custom-call | tf_op jit(solution)/shard_map/work/pallas_call | solution.py:488
  36.6 22.9 %all_to_all.5.own = bf16[8,288,128]{2,1,0:T(8,128)(2,1)S(1)} all-to-all(bf16[8,288,128]{2,1,0:T(8,128)(2,1)S(1)} %get-tuple-element.32), channel_id=1, replica_groups=mesh['group'=2,'row'=2,'col'=8] {'col'}, dimensions={0} | all-to-all | bytes 1179648 | tf_op jit(solution)/shard_map/all_to_all | solution.py:511
  59.5 0.0 collective-permute-start.8
  59.5 2.0 %collective-permute-done.8.mate = bf16[8,288,128]{2,1,0:T(8,128)(2,1)S(1)} collective-permute-done((bf16[8,288,128]{2,1,0:T(8,128)(2,1)S(1)}, bf16[8,288,128]{2,1,0:T(8,128)(2,1)S(1)}, u32[]{:S(2)}, u32[]{:S(2)}) %collective-permute-start.8) | collective-permute-done | bytes 589856 | tf_op jit(solution)/shard_map/ppermute | solution.py:512
  61.5 1.3 %finish.1 = (f32[64,256]{1,0:T(8,128)}, f32[1,64]{1,0:T(1,128)}, f32[1024,128]{1,0:T(8,128)}, f32[1,128]{1,0:T(1,128)}, f32[1,256]{1,0:T(1,128)}, /*index=5*/f32[1,256]{1,0:T(1,128)}) custom-call(bf16[8,288,128]{2,1,0:T(8,128)(2,1)S(1)} %all_to_all.5.own, bf16[8,288,128]{2,1,0:T(8,128)(2,1)S(1)} %collective-permute-done.8.mate), custom_call_target="tpu_custom_call" | custom-call | tf_op jit(solution)/shard_map/finish/pallas_call | solution.py:513
Async XLA Ops:
  0.6 1.6 %collective-permute-start = (s32[8,64]{1,0:T(8,128)}, s32[8,64]{1,0:T(8,128)S(1)}, u32[]{:S(2)}, u32[]{:S(2)}) collective-permute-start(s32[8,64]{1,0:T(8,128)} %bitcast.19), channel_id=1, source_target_pairs={{0,8},{8,0},{1,9},{9,1},{2,10},{10,2},{3,11},{11,3},{4,12},{12,4},... | collective-permute-start | bytes 6152 | tf_op jit(solution)/shard_map/ppermute | solution.py:465
  1.2 1.0 %copy-start.10 = (f32[256]{0:T(256)S(1)}, f32[256]{0:T(256)}, u32[]{:S(2)}) copy-start(f32[256]{0:T(256)} %param.15) | copy-start | bytes 3076
  1.2 1.0 %copy-start.11 = (s32[64]{0:T(128)S(1)}, s32[64]{0:T(128)}, u32[]{:S(2)}) copy-start(s32[64]{0:T(128)} %residue.1) | copy-start | bytes 772
  1.2 1.1 %copy-start.12 = (f32[64]{0:T(128)S(1)}, f32[64]{0:T(128)}, u32[]{:S(2)}) copy-start(f32[64]{0:T(128)} %param.17) | copy-start | bytes 772
  2.2 0.7 %copy-start.8 = (s32[64,8]{0,1:T(8,128)S(1)}, s32[64,8]{0,1:T(8,128)}, u32[]{:S(2)}) copy-start(s32[64,8]{0,1:T(8,128)} %param.21) | copy-start | bytes 6148
  2.2 0.7 %copy-start.7 = (f32[64,8]{0,1:T(8,128)S(1)}, f32[64,8]{0,1:T(8,128)}, u32[]{:S(2)}) copy-start(f32[64,8]{0,1:T(8,128)} %param.13) | copy-start | bytes 6148
  2.2 0.7 %copy-start.6 = (f32[64,8]{0,1:T(8,128)S(1)}, f32[64,8]{0,1:T(8,128)}, u32[]{:S(2)}) copy-start(f32[64,8]{0,1:T(8,128)} %param.12) | copy-start | bytes 6148
  2.2 0.7 %copy-start.9 = (f32[256]{0:T(256)S(1)}, f32[256]{0:T(256)}, u32[]{:S(2)}) copy-start(f32[256]{0:T(256)} %param.14) | copy-start | bytes 3076
  2.9 0.9 %copy-start = (bf16[64,8,256]{2,1,0:T(8,128)(2,1)S(1)}, bf16[64,8,256]{2,1,0:T(8,128)(2,1)}, u32[]{:S(2)}) copy-start(bf16[64,8,256]{2,1,0:T(8,128)(2,1)} %alignment.3) | copy-start | bytes 786436
  3.9 0.9 %copy-start.2 = (bf16[8,64,128]{2,1,0:T(8,128)(2,1)S(1)}, bf16[8,64,128]{2,1,0:T(8,128)(2,1)}, u32[]{:S(2)}) copy-start(bf16[8,64,128]{2,1,0:T(8,128)(2,1)} %cotangent.3) | copy-start | bytes 393220
  4.8 0.8 %copy-start.5 = (bf16[256,64]{0,1:T(8,128)(2,1)S(1)}, bf16[256,64]{0,1:T(8,128)(2,1)}, u32[]{:S(2)}) copy-start(bf16[256,64]{0,1:T(8,128)(2,1)} %param.16) | copy-start | bytes 98308
  5.5 24.3 %copy-start.1 = (bf16[64,8,256]{2,1,0:T(8,128)(2,1)S(1)}, bf16[64,8,256]{2,1,0:T(8,128)(2,1)}, u32[]{:S(2)}) copy-start(bf16[64,8,256]{2,1,0:T(8,128)(2,1)} %alignment.3) | copy-start | bytes 786436
  5.5 24.3 %copy-start.3 = (bf16[8,64,128]{2,1,0:T(8,128)(2,1)S(1)}, bf16[8,64,128]{2,1,0:T(8,128)(2,1)}, u32[]{:S(2)}) copy-start(bf16[8,64,128]{2,1,0:T(8,128)(2,1)} %cotangent.3) | copy-start | bytes 393220
  6.8 8.8 %collective-permute-start.1 = (bf16[400,128]{1,0:T(8,128)(2,1)S(1)}, bf16[400,128]{1,0:T(8,128)(2,1)S(1)}, u32[]{:S(2)}, u32[]{:S(2)}) collective-permute-start(bf16[400,128]{1,0:T(8,128)(2,1)S(1)} %get-tuple-element.24), channel_id=1, source_target_pairs={{0,1},{1,0},{2,3},{3,2},{4,5},{5,4},{6,7},{7,6},{8,9},{9,8},{10,11... | collective-permute-start | bytes 307208 | tf_op jit(solution)/shard_map/ppermute | solution.py:486
  9.7 9.5 %collective-permute-start.2 = (bf16[400,128]{1,0:T(8,128)(2,1)S(1)}, bf16[400,128]{1,0:T(8,128)(2,1)S(1)}, u32[]{:S(2)}, u32[]{:S(2)}) collective-permute-start(bf16[400,128]{1,0:T(8,128)(2,1)S(1)} %get-tuple-element.25), channel_id=1, source_target_pairs={{0,2},{1,3},{2,0},{3,1},{4,6},{5,7},{6,4},{7,5},{8,10},{9,11},{10,... | collective-permute-start | bytes 307208 | tf_op jit(solution)/shard_map/ppermute | solution.py:486
  11.3 7.9 %collective-permute-start.3 = (bf16[400,128]{1,0:T(8,128)(2,1)S(1)}, bf16[400,128]{1,0:T(8,128)(2,1)S(1)}, u32[]{:S(2)}, u32[]{:S(2)}) collective-permute-start(bf16[400,128]{1,0:T(8,128)(2,1)S(1)} %get-tuple-element.26), channel_id=1, source_target_pairs={{0,3},{1,2},{2,1},{3,0},{4,7},{5,6},{6,5},{7,4},{8,11},{9,10},{10,... | collective-permute-start | bytes 307208 | tf_op jit(solution)/shard_map/ppermute | solution.py:486
  11.3 7.9 %collective-permute-start.4 = (bf16[400,128]{1,0:T(8,128)(2,1)S(1)}, bf16[400,128]{1,0:T(8,128)(2,1)S(1)}, u32[]{:S(2)}, u32[]{:S(2)}) collective-permute-start(bf16[400,128]{1,0:T(8,128)(2,1)S(1)} %get-tuple-element.27), channel_id=1, source_target_pairs={{0,4},{1,5},{2,6},{3,7},{4,0},{5,1},{6,2},{7,3},{8,12},{9,13},{10,... | collective-permute-start | bytes 307208 | tf_op jit(solution)/shard_map/ppermute | solution.py:486
  14.3 15.5 %collective-permute-start.5 = (bf16[400,128]{1,0:T(8,128)(2,1)S(1)}, bf16[400,128]{1,0:T(8,128)(2,1)S(1)}, u32[]{:S(2)}, u32[]{:S(2)}) collective-permute-start(bf16[400,128]{1,0:T(8,128)(2,1)S(1)} %get-tuple-element.28), channel_id=1, source_target_pairs={{0,5},{1,4},{2,7},{3,6},{4,1},{5,0},{6,3},{7,2},{8,13},{9,12},{10,... | collective-permute-start | bytes 307208 | tf_op jit(solution)/shard_map/ppermute | solution.py:486
  15.6 14.2 %collective-permute-start.6 = (bf16[400,128]{1,0:T(8,128)(2,1)S(1)}, bf16[400,128]{1,0:T(8,128)(2,1)S(1)}, u32[]{:S(2)}, u32[]{:S(2)}) collective-permute-start(bf16[400,128]{1,0:T(8,128)(2,1)S(1)} %get-tuple-element.29), channel_id=1, source_target_pairs={{0,6},{1,7},{2,4},{3,5},{4,2},{5,3},{6,0},{7,1},{8,14},{9,15},{10,... | collective-permute-start | bytes 307208 | tf_op jit(solution)/shard_map/ppermute | solution.py:486
  19.2 10.6 %collective-permute-start.7 = (bf16[400,128]{1,0:T(8,128)(2,1)S(1)}, bf16[400,128]{1,0:T(8,128)(2,1)S(1)}, u32[]{:S(2)}, u32[]{:S(2)}) collective-permute-start(bf16[400,128]{1,0:T(8,128)(2,1)S(1)} %get-tuple-element.30), channel_id=1, source_target_pairs={{0,7},{1,6},{2,5},{3,4},{4,3},{5,2},{6,1},{7,0},{8,15},{9,14},{10,... | collective-permute-start | bytes 307208 | tf_op jit(solution)/shard_map/ppermute | solution.py:486
  29.8 1.0 %copy-start.4 = (bf16[1024,128]{1,0:T(8,128)(2,1)S(1)}, bf16[1024,128]{1,0:T(8,128)(2,1)}, u32[]{:S(2)}) copy-start(bf16[1024,128]{1,0:T(8,128)(2,1)} %out_weight.1) | copy-start | bytes 786436
  59.5 2.0 %collective-permute-start.8 = (bf16[8,288,128]{2,1,0:T(8,128)(2,1)S(1)}, bf16[8,288,128]{2,1,0:T(8,128)(2,1)S(1)}, u32[]{:S(2)}, u32[]{:S(2)}) collective-permute-start(bf16[8,288,128]{2,1,0:T(8,128)(2,1)S(1)} %all_to_all.5.own), channel_id=1, source_target_pairs={{0,8},{8,0},{1,9},{9,1},{2,10},{10,2},{3,11},{11,3},{4,12},{12,4},... | collective-permute-start | bytes 1769480 | tf_op jit(solution)/shard_map/ppermute | solution.py:512

commit v2 on v1

--- a/solution.py
+++ b/solution.py
@@ -141,8 +141,8 @@
 TURNED_AT = 272
 SLICE_AT = 336
 MESSAGE = 400
-SMALL_AT = 256
-PARTIAL = 288
+PARTIAL = 136
+SENT = 144
 VMEM = pltpu.CompilerParams(vmem_limit_bytes=48 * 1024 * 1024)
 F32 = jnp.float32
 BF16 = jnp.bfloat16
@@ -184,11 +184,20 @@
     return jnp.concatenate([wide[h, pl.ds(start, size, stride=stride), :] for h in range(2)], axis=1)
 
 
-def prepare(
-    column, residue, alignment, mean, inverse, gain, shift, weight, bias, mask, mate, cotangent, *rest
-):
-    count = (len(rest) - 4) // 1
-    messages, (wide, packed, cot, turned) = rest[:count], rest[count:]
+def fetch(sources, targets, arrived):
+    copies = [pltpu.make_async_copy(s, t, arrived.at[i]) for i, (s, t) in enumerate(zip(sources, targets))]
+    for copy in copies:
+        copy.start()
+    return copies
+
+
+def prepare(column, residue, mate, *rest):
+    count = len(rest) - 23
+    sources, messages, targets = rest[:9], rest[9 : 9 + count], rest[9 + count : 18 + count]
+    wide, packed, cot, turned, arrived = rest[18 + count :]
+    alignment, mean, inverse, gain, shift, weight, bias, mask, cotangent = targets
+    for copy in fetch(sources, targets, arrived):
+        copy.wait()
     col = column[0]
     seqs, own, channels = alignment.shape
     square = cot.at[0:LANES, :]
@@ -252,14 +261,20 @@
             ).astype(BF16)
 
 
-def work(
-    column, cotangent, out_weight, alignment, mean, inverse, gain, shift, weight, *rest
-):
-    count = len(rest) - 15
-    messages = rest[:count]
-    activation, partial = rest[count : count + 2]
-    (every, live_all, present_all, turned, slices, grad_own, grad_turned, grad_slice, left_outer, right_outer, right_rows, mixed, wide) = rest[count + 2 :]
-    col = column[0]
+def quad_members(quad):
+    base = quad // 2 * 8 + quad % 2 * 2
+    return ((base, base + 4), (base + 1, base + 5))
+
+
+def work(place, *rest):
+    count = len(rest) - 33
+    messages, sources = rest[:count], rest[count : count + 8]
+    activation, keep, give = rest[count + 8 : count + 11]
+    targets = rest[count + 11 : count + 19]
+    (every, live_all, present_all, turned, slices, grad_own, grad_turned, grad_slice, left_outer, right_outer, corner, mixed, wide, arrived) = rest[count + 19 :]
+    cotangent, out_weight, alignment, mean, inverse, gain, shift, weight = targets
+    copies = fetch(sources, targets, arrived)
+    col, row = place[0], place[1]
     seqs, own, channels = alignment.shape
     total = cotangent.shape[1]
     depth = Z // count
@@ -293,6 +308,7 @@
     scale_twice = scale_of(
         jnp.concatenate([live, live], axis=0), jnp.concatenate([present, present], axis=0)
     )
+    copies[0].wait()
     for i in range(own):
         rows = slice(i * total, (i + 1) * total)
         grad_own[rows, :] = (cotangent[i].astype(F32) * scale_own[:, i : i + 1]).astype(BF16)
@@ -305,8 +321,12 @@
         for i in range(pairs):
             piece = slices[c, i * depth : (i + 1) * depth, :].astype(F32) * tile[i : i + 1, :]
             bias_acc = bias_acc + piece
-            grad_slice[(c * pairs + i) * depth : (c * pairs + i + 1) * depth, :] = piece.astype(BF16)
-
+            grad_slice[
+                (c * 2 + i // 2) * depth : (c * 2 + i // 2 + 1) * depth,
+                i % 2 * LANES : (i % 2 + 1) * LANES,
+            ] = piece.astype(BF16)
+
+    copies[1].wait()
     wide[0] = out_weight[...].astype(F32)
     eight = 8
     for a in range(0, P_SIZE, eight):
@@ -320,6 +340,8 @@
     left_grad = swap_halves(dot_nn(left_outer[...], gathered))
     right_grad = dot_nn(right_outer[...], gathered)
 
+    for copy in copies[2:]:
+        copy.wait()
     square = wide.at[0, 0:LANES, :]
     stats = columns_of(square, [mean[...], inverse[...]])
     spread(wide, alignment)
@@ -350,94 +372,99 @@
         [wide[h, 0 : seqs * own, :].reshape(seqs, own, LANES) for h in range(2)], axis=2
     ).astype(BF16)
 
-    right_rows[0:total, :] = jnp.zeros((total, P_SIZE * half), BF16)
-    right_rows[2 * total : 3 * total, :] = jnp.zeros((total, P_SIZE * half), BF16)
+    quads = count * own // 4
+    span = quads * depth
     low = low_lanes((total, LANES))
-    for q in range(0, P_SIZE, 2):
-        first = every[q * total : (q + 1) * total, :]
-        second = every[(q + 1) * total : (q + 2) * total, :]
-        right_rows[total : 2 * total, q * half : (q + 2) * half] = jnp.where(
-            low, swap_halves(first), second
-        ).astype(BF16)
+    corner[...] = jnp.zeros_like(corner)
+    for q in range(P_SIZE):
+        block = every[q * total : (q + 1) * total, :]
+        here = jnp.where(low, 0.0, block)
+        moved = swap_halves(here).astype(BF16)
+        here = here.astype(BF16)
+        slot = q % corner.shape[0]
+        for at in range(4):
+            lanes = slice(at // 2 * LANES, (at // 2 + 1) * LANES)
+            corner[slot, at * total : (at + 1) * total, lanes] = here if at % 2 else moved
+        mixed[:, q * depth : (q + 1) * depth, :] = (
+            dot_nn(grad_slice[...], corner[slot]).astype(BF16).reshape(quads, depth, 4 * total)
+        )
     low = low_lanes((P_SIZE, LANES))
-    none = jnp.zeros((P_SIZE, LANES), BF16)
-    weight_acc = jnp.zeros((LANES, LANES), F32)
-    quarter = 4
-    for top in range(2):
-        right_side = right_rows[(1 - top) * total : (3 - top) * total, :]
-        for c0 in range(0, count, quarter):
-            span = quarter * pairs * depth
-            mixed[...] = dot_nn(
-                grad_slice[c0 * pairs * depth : c0 * pairs * depth + span, :], right_side
-            ).astype(BF16)
-            for c in range(quarter):
-                for i in range(pairs):
-                    at = (c * pairs + i) * depth
-                    lhs = jnp.concatenate(
-                        [mixed[at : at + depth, a * 256 : (a + 1) * 256] for a in range(8)], axis=0
-                    )
-                    left = every[pl.ds((c0 + c) * own + top * pairs + i, P_SIZE, stride=total), :]
-                    left = jnp.where(low, left, 0.0)
-                    moved = swap_halves(left).astype(BF16)
-                    left = left.astype(BF16)
-                    rhs = jnp.concatenate(
-                        [
-                            jnp.concatenate([left, none], axis=1),
-                            jnp.concatenate([moved, none], axis=1),
-                            jnp.concatenate([none, left], axis=1),
-                            jnp.concatenate([none, moved], axis=1),
-                        ],
-                        axis=0,
-                    )
-                    weight_acc = weight_acc + dot_nt(lhs, rhs)
+    weight_acc = jnp.zeros((P_SIZE * depth, P_SIZE), F32)
+    for quad in range(quads):
+        rhs = []
+        for first in quad_members(quad):
+            one, two = (every[pl.ds(i, P_SIZE, stride=total), :] for i in first)
+            rhs.append(jnp.where(low, one, swap_halves(two)))
+        weight_acc = weight_acc + dot_nt(mixed[quad], jnp.concatenate(rhs, axis=1).astype(BF16))
+    group = P_SIZE * depth // 4
+    weight_acc = jnp.concatenate([weight_acc[b * group : (b + 1) * group] for b in range(4)], axis=1)
 
     square[...] = jnp.zeros((LANES, LANES), F32)
     square[0 : 2 * P_SIZE, :seqs] = proj_acc
     square[half : half + depth, :] = bias_acc
     sums = jnp.sum(square[...].T, axis=0, keepdims=True)
-    small = jnp.concatenate(
-        [gain_acc[:, :LANES], gain_acc[:, LANES:], shift_acc[:, :LANES], shift_acc[:, LANES:], sums, jnp.zeros((11, LANES), F32)],
-        axis=0,
-    )
-    high = small.astype(BF16)
-    rest_of = (small - high.astype(F32)).astype(BF16)
-    whole = jnp.concatenate(
-        [weight_acc.astype(BF16), input_acc[:, :LANES].astype(BF16), input_acc[:, LANES:].astype(BF16), high, rest_of],
-        axis=0,
-    )
-    for k in range(count):
+    lane = lax.broadcasted_iota(jnp.int32, (1, LANES), 1)
+    small = [gain_acc[:, :LANES], gain_acc[:, LANES:], shift_acc[:, :LANES], shift_acc[:, LANES:]]
+    none = jnp.zeros((3, LANES), F32)
+    first = row == 0
+    keep[0:half, :] = jnp.where(first, weight_acc[:half], weight_acc[half:])
+    give[0:half, :] = jnp.where(first, weight_acc[half:], weight_acc[:half])
+    keep[half:LANES, :] = jnp.where(first, input_acc[:, :LANES], input_acc[:, LANES:])
+    give[half:LANES, :] = jnp.where(first, input_acc[:, LANES:], input_acc[:, :LANES])
+    keep[LANES:PARTIAL, :] = jnp.concatenate(small + [sums, none], axis=0)
+    give[LANES:PARTIAL, :] = jnp.concatenate(small + [jnp.where(lane < half, sums, 0.0), none], axis=0)
+
+
+def pack(kept, given, partial):
+    both = kept[...] + given[...]
+    high = both.astype(BF16)
+    small = both[LANES:] - high[LANES:].astype(F32)
+    whole = jnp.concatenate([high, small.astype(BF16)], axis=0)
+    for k in range(partial.shape[0]):
         partial[k] = whole
 
 
-def finish(own, mate, input_out, bias_out, weight_out, out_bias_out, gain_out, shift_out):
+def finish(place, own, mate, input_out, bias_out, weight_out, out_bias_out, gain_out, shift_out):
+    row = place[1]
     count = own.shape[0]
     depth = Z // count
-    input_acc = jnp.zeros((LANES, LANES), F32)
-    small_acc = jnp.zeros((16, LANES), F32)
+    half = LANES // 2
     lane = lax.broadcasted_iota(jnp.int32, (1, LANES), 1)
+    sums = []
+    for side, part in enumerate((own, mate)):
+        top = row if side == 0 else 1 - row
+        input_acc = jnp.zeros((half, LANES), F32)
+        pieces = []
+        for k in range(count):
+            pieces.append(part[k, :half].astype(F32))
+            input_acc = input_acc + part[k, half:LANES].astype(F32)
+        sums.append(input_acc)
+        for a in range(4):
+            turned = jnp.concatenate([p[a * depth : (a + 1) * depth] for p in pieces], axis=0).T
+            for b in range(4):
+                weight_out[pl.ds(4 * top + a + 8 * b, P_SIZE, stride=P_SIZE), :] = turned[
+                    b * P_SIZE : (b + 1) * P_SIZE
+                ]
+    input_out[:, :LANES] = jnp.where(row == 0, sums[0], sums[1])
+    input_out[:, LANES:] = jnp.where(row == 0, sums[1], sums[0])
+    small_acc = jnp.zeros((8, LANES), F32)
     out_bias = jnp.zeros((1, LANES), F32)
-    pieces = []
     for k in range(count):
-        mine = own[k].astype(F32)
-        both = mine + mate[k].astype(F32)
-        pieces.append(both[:LANES])
-        input_acc = input_acc + both[LANES:SMALL_AT]
-        small_acc = small_acc + (both[SMALL_AT : SMALL_AT + 16] + both[SMALL_AT + 16 :])
-        bias = mine[SMALL_AT + 4 : SMALL_AT + 5] + mine[SMALL_AT + 20 : SMALL_AT + 21]
-        bias = pltpu.roll(bias, (k * depth + LANES // 2) % LANES, 1)
+        small = part_of_small(own, k)
+        small_acc = small_acc + small
+        bias = pltpu.roll(small[4:5], (k * depth + half) % LANES, 1)
         out_bias = jnp.where((lane >= k * depth) & (lane < (k + 1) * depth), bias, out_bias)
-    for a in range(8):
-        turned = jnp.concatenate([p[a * depth : (a + 1) * depth] for p in pieces], axis=0).T
-        for b in range(4):
-            weight_out[pl.ds(4 * a + b, P_SIZE, stride=P_SIZE), :] = turned[b * P_SIZE : (b + 1) * P_SIZE]
-    input_out[:, :LANES] = input_acc[: LANES // 2]
-    input_out[:, LANES:] = input_acc[LANES // 2 :]
     gain_out[:, :LANES] = small_acc[0:1]
     gain_out[:, LANES:] = small_acc[1:2]
     shift_out[:, :LANES] = small_acc[2:3]
     shift_out[:, LANES:] = small_acc[3:4]
-    bias_out[...] = small_acc[4:5, : LANES // 2]
+    bias_out[...] = small_acc[4:5, :half]
     out_bias_out[...] = out_bias
+
+
+def part_of_small(own, k):
+    both = own[k, LANES:].astype(F32)
+    return both[:8] + both[8:]
 
 
 def shape(dims, dtype):
@@ -460,37 +487,51 @@
     count = lax.axis_size("col")
     seqs, own, channels = alignment.shape
     total = pair_cotangent.shape[1]
-    column = lax.axis_index("col").reshape(1).astype(jnp.int32)
+    place = jnp.stack([lax.axis_index("col"), lax.axis_index("row")]).astype(jnp.int32)
     mask = sequence_mask.T
-    mate = lax.ppermute(mask, "row", [(0, 1), (1, 0)])
+    turn = [(0, 1), (1, 0)]
+    mate = lax.ppermute(mask, "row", turn)
     mean, inverse = norm_mean.T, norm_inverse.T
     gain, shift = norm_gain[None, :], norm_shift[None, :]
     weight = input_weight.T
     smem = pl.BlockSpec(memory_space=pltpu.SMEM)
     vmem = pl.BlockSpec(memory_space=pltpu.VMEM)
+    hbm = pl.BlockSpec(memory_space=pltpu.HBM)
+
+    def room(arrays):
+        return [pltpu.VMEM(a.shape, a.dtype) for a in arrays]
+
+    def stay(arrays):
+        return [pltpu.with_memory_space_constraint(a, pltpu.HBM) for a in arrays]
+
+    operands = [alignment, mean, inverse, gain, shift, weight, input_bias[None, :], mask, pair_cotangent]
     messages = pl.pallas_call(
         prepare,
         out_shape=[shape((MESSAGE, LANES), BF16)] * count,
-        in_specs=[smem, smem] + [vmem] * 10,
+        in_specs=[smem, smem, vmem] + [hbm] * len(operands),
         out_specs=[vmem] * count,
-        scratch_shapes=[
+        scratch_shapes=room(operands)
+        + [
             pltpu.VMEM((2, seqs * own, LANES), F32),
             pltpu.VMEM((PROJ_ROWS, LANES), F32),
             pltpu.VMEM((own * total, Z), F32),
             pltpu.VMEM((own // 2, Z, LANES), BF16),
+            pltpu.SemaphoreType.DMA((len(operands),)),
         ],
         compiler_params=VMEM,
         name="prepare",
-    )(column, residue_mask, alignment, mean, inverse, gain, shift, weight, input_bias[None, :], mask, mate, pair_cotangent)
+    )(place, stay([residue_mask])[0], mate, *stay(operands))
     received = [messages[0]] + [
         lax.ppermute(messages[k], "col", [(c, c ^ k) for c in range(count)]) for k in range(1, count)
     ]
-    activation, partial = pl.pallas_call(
+    operands = [pair_cotangent, output_weight, alignment, mean, inverse, gain, shift, weight]
+    activation, keep, give = pl.pallas_call(
         work,
-        out_shape=[shape(alignment.shape, BF16), shape((count, PARTIAL, LANES), BF16)],
-        in_specs=[smem] + [vmem] * (8 + count),
-        out_specs=[vmem] * 2,
-        scratch_shapes=[
+        out_shape=[shape(alignment.shape, BF16)] + [shape((PARTIAL, LANES), F32)] * 2,
+        in_specs=[smem] + [vmem] * count + [hbm] * len(operands),
+        out_specs=[vmem] * 3,
+        scratch_shapes=room(operands)
+        + [
             pltpu.VMEM((P_SIZE * total, LANES), F32),
             pltpu.VMEM((total, LANES), F32),
             pltpu.VMEM((total, LANES), F32),
@@ -498,18 +539,27 @@
             pltpu.VMEM((count, MESSAGE - SLICE_AT, LANES), BF16),
             pltpu.VMEM((own * total, Z), BF16),
             pltpu.VMEM((own * total, Z), BF16),
-            pltpu.VMEM((count * (MESSAGE - SLICE_AT), LANES), BF16),
+            pltpu.VMEM((count * (MESSAGE - SLICE_AT) // 2, 2 * LANES), BF16),
             pltpu.VMEM((own * P_SIZE, P_SIZE * total), BF16),
             pltpu.VMEM((own * P_SIZE, P_SIZE * total), BF16),
-            pltpu.VMEM((3 * total, P_SIZE * seqs), BF16),
-            pltpu.VMEM((4 * (MESSAGE - SLICE_AT), P_SIZE * seqs), BF16),
+            pltpu.VMEM((4, 4 * total, 2 * LANES), BF16),
+            pltpu.VMEM((count * own // 4, P_SIZE * (Z // count), 4 * seqs), BF16),
             pltpu.VMEM((2, P_SIZE * P_SIZE, LANES), F32),
+            pltpu.SemaphoreType.DMA((len(operands),)),
         ],
         compiler_params=VMEM,
         name="work",
-    )(column, pair_cotangent, output_weight, alignment, mean, inverse, gain, shift, weight, *received)
+    )(place, *received, *stay(operands))
+    partial = pl.pallas_call(
+        pack,
+        out_shape=shape((count, SENT, LANES), BF16),
+        in_specs=[vmem] * 2,
+        out_specs=vmem,
+        compiler_params=VMEM,
+        name="pack",
+    )(keep, lax.ppermute(give, "row", turn))
     ours = lax.all_to_all(partial, "col", 0, 0)
-    theirs = lax.ppermute(ours, "row", [(0, 1), (1, 0)])
+    theirs = lax.ppermute(ours, "row", turn)
     input_grad, bias_grad, weight_grad, out_bias_grad, gain_grad, shift_grad = pl.pallas_call(
         finish,
         out_shape=[
@@ -520,11 +570,11 @@
             shape((1, channels), F32),
             shape((1, channels), F32),
         ],
-        in_specs=[vmem] * 2,
+        in_specs=[smem] + [vmem] * 2,
         out_specs=[vmem] * 6,
         compiler_params=VMEM,
         name="finish",
-    )(ours, theirs)
+    )(place, ours, theirs)
     return (activation, input_grad.T, bias_grad[0], weight_grad, out_bias_grad[0], gain_grad[0], shift_grad[0])
 
 

time: 63.1 us -> 57.4 us (0.910)
  blocking collectives: 22.9 us -> 17.6 us
  local copies, waits for them, and re-layouts: 4.27 us -> 0 us
  Pallas kernels: 8.3 us -> 11.5 us
  waiting for transfers between devices: 13.7 us -> 14.4 us
    all_to_all x1, blocking collectives: 22.9 us -> 17.6 us  [tiled(): ours = lax.all_to_all(partial, 'col', 0, 0)]
    unnamed x26 -> x0, local copies, waits for them, and re-layouts: 4.27 us -> none
    pallas_call x1, Pallas kernels: 1.25 us -> 2.64 us  [tiled(): pl.pallas_call(prepare, out_shape=[shape((MESSAGE, LANES), BF16)] * count...]
    pallas_call x1 -> x2, Pallas kernels: 5.77 us -> 7.14 us  [the longest x1 7.11 us: tiled(): pl.pallas_call(work, out_shape=[shape(alignment.shape, BF16)] + [shape((P...]
    ppermute x2 -> x3, waiting for transfers between devices: 3.03 us -> 3.78 us  [the longest x1 1.58 us: tiled(): theirs = lax.ppermute(ours, 'row', turn)]
  transfers between devices with their start and end apart: 9 -> 10, of which waited for: 3 -> 4; matrix products, arithmetic and copies ran while one was open for 0% -> 0% of each run, Pallas kernels for 0% -> 0%
where the time goes in v2:
time: 57.4 us; the launch traced here: 57.2 us
  blocking collectives  17.6 us (31%)
  waiting for transfers between devices  14.4 us (25%)
  starting transfers between devices  13 us (23%)
  Pallas kernels  11.5 us (20%)
  between operations  0.67 us (1%)
    all_to_all x1, blocking collectives, tiled(): ours = lax.all_to_all(partial, 'col', 0, 0)  17.6 us
    ppermute x7, starting transfers between devices, tiled(): lax.ppermute(messages[k], 'col', [(c, c ^ k) for c in range(count)])  12.4 us
    ppermute x7, waiting for transfers between devices, tiled(): lax.ppermute(messages[k], 'col', [(c, c ^ k) for c in range(count)])  10.6 us
    pallas_call x1, Pallas kernels, tiled(): pl.pallas_call(work, out_shape=[shape(alignment.shape, BF16)] + [shape((P...  7.11 us
    pallas_call x1, Pallas kernels, tiled(): pl.pallas_call(prepare, out_shape=[shape((MESSAGE, LANES), BF16)] * count...  2.64 us
    pallas_call x1, Pallas kernels, tiled(): pl.pallas_call(finish, out_shape=[shape((2 * P_SIZE, channels), F32), sha...  1.72 us
    ppermute x1, waiting for transfers between devices, tiled(): theirs = lax.ppermute(ours, 'row', turn)  1.58 us
    ppermute x1, waiting for transfers between devices, tiled(): lax.ppermute(give, 'row', turn)  1.25 us
  transfers between devices with their start and end apart: 10, of which 4 were waited for; matrix products, arithmetic and copies ran while one was open for 0% of the time, Pallas kernels for 0%

profile of v2, /device:TPU:0, one launch (start us, length us, event | category | flops | bytes accessed | tf_op | source)
XLA Modules:
  0.0 57.2 jit_solution(18128085351732762186)
XLA Ops:
  0.6 0.5 collective-permute-start
  1.1 0.1 pad_add_fusion.column.place
  1.2 1.0 %collective-permute-done.mate = s32[8,64]{1,0:T(8,128)S(1)} collective-permute-done((s32[8,64]{1,0:T(8,128)}, s32[8,64]{1,0:T(8,128)S(1)}, u32[]{:S(2)}, u32[]{:S(2)}) %collective-permute-start) | collective-permute-done | bytes 2080 | tf_op jit(solution)/shard_map/ppermute | solution.py:493
  2.2 2.6 %prepare.1 = (bf16[400,128]{1,0:T(8,128)(2,1)S(1)}, bf16[400,128]{1,0:T(8,128)(2,1)S(1)}, bf16[400,128]{1,0:T(8,128)(2,1)S(1)}, bf16[400,128]{1,0:T(8,128)(2,1)S...) custom-call(s32[2]{0:T(128)S(1)} %pad_add_fusion.column.place, ...), custom_call_target="tpu_custom_call" | custom-call | tf_op jit(solution)/shard_map/prepare/pallas_call | solution.py:508
  4.8 2.9 %collective-permute-start.1 = (bf16[400,128]{1,0:T(8,128)(2,1)S(1)}, bf16[400,128]{1,0:T(8,128)(2,1)S(1)}, u32[]{:S(2)}, u32[]{:S(2)}) collective-permute-start(bf16[400,128]{1,0:T(8,128)(2,1)S(1)} %get-tuple-element.25), channel_id=1, source_target_pairs={{0,1},{1,0},{2,3},{3,2},{4,5},{5,4},{6,7},{7,6},{8,9},{9,8},{10,11... | collective-permute-start | bytes 307208 | tf_op jit(solution)/shard_map/ppermute | solution.py:525
  7.8 1.6 %collective-permute-start.2 = (bf16[400,128]{1,0:T(8,128)(2,1)S(1)}, bf16[400,128]{1,0:T(8,128)(2,1)S(1)}, u32[]{:S(2)}, u32[]{:S(2)}) collective-permute-start(bf16[400,128]{1,0:T(8,128)(2,1)S(1)} %get-tuple-element.26), channel_id=1, source_target_pairs={{0,2},{1,3},{2,0},{3,1},{4,6},{5,7},{6,4},{7,5},{8,10},{9,11},{10,... | collective-permute-start | bytes 307208 | tf_op jit(solution)/shard_map/ppermute | solution.py:525
  9.3 0.0 collective-permute-start.3
  9.3 3.0 %collective-permute-start.4 = (bf16[400,128]{1,0:T(8,128)(2,1)S(1)}, bf16[400,128]{1,0:T(8,128)(2,1)S(1)}, u32[]{:S(2)}, u32[]{:S(2)}) collective-permute-start(bf16[400,128]{1,0:T(8,128)(2,1)S(1)} %get-tuple-element.28), channel_id=1, source_target_pairs={{0,4},{1,5},{2,6},{3,7},{4,0},{5,1},{6,2},{7,3},{8,12},{9,13},{10,... | collective-permute-start | bytes 307208 | tf_op jit(solution)/shard_map/ppermute | solution.py:525
  12.3 1.3 %collective-permute-start.5 = (bf16[400,128]{1,0:T(8,128)(2,1)S(1)}, bf16[400,128]{1,0:T(8,128)(2,1)S(1)}, u32[]{:S(2)}, u32[]{:S(2)}) collective-permute-start(bf16[400,128]{1,0:T(8,128)(2,1)S(1)} %get-tuple-element.29), channel_id=1, source_target_pairs={{0,5},{1,4},{2,7},{3,6},{4,1},{5,0},{6,3},{7,2},{8,13},{9,12},{10,... | collective-permute-start | bytes 307208 | tf_op jit(solution)/shard_map/ppermute | solution.py:525
  13.6 0.0 collective-permute-done.1.rest_1_
  13.6 3.6 %collective-permute-start.6 = (bf16[400,128]{1,0:T(8,128)(2,1)S(1)}, bf16[400,128]{1,0:T(8,128)(2,1)S(1)}, u32[]{:S(2)}, u32[]{:S(2)}) collective-permute-start(bf16[400,128]{1,0:T(8,128)(2,1)S(1)} %get-tuple-element.30), channel_id=1, source_target_pairs={{0,6},{1,7},{2,4},{3,5},{4,2},{5,3},{6,0},{7,1},{8,14},{9,15},{10,... | collective-permute-start | bytes 307208 | tf_op jit(solution)/shard_map/ppermute | solution.py:525
  17.2 0.0 collective-permute-done.2.rest_2_
  17.2 0.0 collective-permute-start.7
  17.2 0.0 collective-permute-done.3.rest_3_
  17.2 0.0 collective-permute-done.4.rest_4_
  17.2 10.6 %collective-permute-done.5.rest_5_ = bf16[400,128]{1,0:T(8,128)(2,1)S(1)} collective-permute-done((bf16[400,128]{1,0:T(8,128)(2,1)S(1)}, bf16[400,128]{1,0:T(8,128)(2,1)S(1)}, u32[]{:S(2)}, u32[]{:S(2)}) %collective-permute-start.5) | collective-permute-done | bytes 102432 | tf_op jit(solution)/shard_map/ppermute | solution.py:525
  27.9 0.0 collective-permute-done.6.rest_6_
  27.9 0.0 collective-permute-done.7.rest_7_
  27.9 7.1 %work.1 = (bf16[64,8,256]{2,1,0:T(8,128)(2,1)}, f32[136,128]{1,0:T(8,128)S(1)}, f32[136,128]{1,0:T(8,128)S(1)}) custom-call(s32[2]{0:T(128)S(1)} %pad_add_fusion.column.place, bf16[400,128]{1,0:T(8,128)(2,1)S(1)} %get-tuple-element.24.rest_0_, bf16[400,128]{1,0:T(8,128)(2,1)S(1)} %collective-permute-done.1.rest_1_, ...), custom_call_target="tpu_custom_call" | custom-call | tf_op jit(solution)/shard_map/work/pallas_call | solution.py:528
  35.0 0.1 collective-permute-start.8
  35.1 1.2 %collective-permute-done.8.given = f32[136,128]{1,0:T(8,128)S(1)} collective-permute-done((f32[136,128]{1,0:T(8,128)S(1)}, f32[136,128]{1,0:T(8,128)S(1)}, u32[]{:S(2)}, u32[]{:S(2)}) %collective-permute-start.8) | collective-permute-done | bytes 69664 | tf_op jit(solution)/shard_map/ppermute | solution.py:560
  36.3 17.6 %all_to_all.5.own = bf16[8,144,128]{2,1,0:T(8,128)(2,1)S(1)} all-to-all(bf16[8,144,128]{2,1,0:T(8,128)(2,1)S(1)} %pack.1), channel_id=1, replica_groups=mesh['group'=2,'row'=2,'col'=8] {'col'}, dimensions={0} | all-to-all | bytes 589824 | tf_op jit(solution)/shard_map/all_to_all | solution.py:561
  53.9 0.0 collective-permute-start.9
  53.9 1.6 %collective-permute-done.9.mate = bf16[8,144,128]{2,1,0:T(8,128)(2,1)S(1)} collective-permute-done((bf16[8,144,128]{2,1,0:T(8,128)(2,1)S(1)}, bf16[8,144,128]{2,1,0:T(8,128)(2,1)S(1)}, u32[]{:S(2)}, u32[]{:S(2)}) %collective-permute-start.9) | collective-permute-done | bytes 294944 | tf_op jit(solution)/shard_map/ppermute | solution.py:562
  55.5 1.7 %finish.1 = (f32[64,256]{1,0:T(8,128)}, f32[1,64]{1,0:T(1,128)}, f32[1024,128]{1,0:T(8,128)}, f32[1,128]{1,0:T(1,128)}, f32[1,256]{1,0:T(1,128)}, /*index=5*/f32[1,256]{1,0:T(1,128)}) custom-call(s32[2]{0:T(128)S(1)} %pad_add_fusion.column.place, bf16[8,144,128]{2,1,0:T(8,128)(2,1)S(1)} %all_to_all.5.own, bf16[8,144,128]{2,1,0:T(8,128)(2,1)S(1)} %collective-permute-done.9.mate), custom_call_target="tpu_custom_call" | custom-call | tf_op jit(solution)/shard_map/finish/pallas_call | solution.py:563
  (1 shorter events, 0.0 us)
Async XLA Ops:
  0.6 1.6 %collective-permute-start = (s32[8,64]{1,0:T(8,128)}, s32[8,64]{1,0:T(8,128)S(1)}, u32[]{:S(2)}, u32[]{:S(2)}) collective-permute-start(s32[8,64]{1,0:T(8,128)} %bitcast.20), channel_id=1, source_target_pairs={{0,8},{8,0},{1,9},{9,1},{2,10},{10,2},{3,11},{11,3},{4,12},{12,4},... | collective-permute-start | bytes 6152 | tf_op jit(solution)/shard_map/ppermute | solution.py:493
  4.8 8.8 %collective-permute-start.1 = (bf16[400,128]{1,0:T(8,128)(2,1)S(1)}, bf16[400,128]{1,0:T(8,128)(2,1)S(1)}, u32[]{:S(2)}, u32[]{:S(2)}) collective-permute-start(bf16[400,128]{1,0:T(8,128)(2,1)S(1)} %get-tuple-element.25), channel_id=1, source_target_pairs={{0,1},{1,0},{2,3},{3,2},{4,5},{5,4},{6,7},{7,6},{8,9},{9,8},{10,11... | collective-permute-start | bytes 307208 | tf_op jit(solution)/shard_map/ppermute | solution.py:525
  7.8 9.5 %collective-permute-start.2 = (bf16[400,128]{1,0:T(8,128)(2,1)S(1)}, bf16[400,128]{1,0:T(8,128)(2,1)S(1)}, u32[]{:S(2)}, u32[]{:S(2)}) collective-permute-start(bf16[400,128]{1,0:T(8,128)(2,1)S(1)} %get-tuple-element.26), channel_id=1, source_target_pairs={{0,2},{1,3},{2,0},{3,1},{4,6},{5,7},{6,4},{7,5},{8,10},{9,11},{10,... | collective-permute-start | bytes 307208 | tf_op jit(solution)/shard_map/ppermute | solution.py:525
  9.3 7.9 %collective-permute-start.3 = (bf16[400,128]{1,0:T(8,128)(2,1)S(1)}, bf16[400,128]{1,0:T(8,128)(2,1)S(1)}, u32[]{:S(2)}, u32[]{:S(2)}) collective-permute-start(bf16[400,128]{1,0:T(8,128)(2,1)S(1)} %get-tuple-element.27), channel_id=1, source_target_pairs={{0,3},{1,2},{2,1},{3,0},{4,7},{5,6},{6,5},{7,4},{8,11},{9,10},{10,... | collective-permute-start | bytes 307208 | tf_op jit(solution)/shard_map/ppermute | solution.py:525
  9.3 7.9 %collective-permute-start.4 = (bf16[400,128]{1,0:T(8,128)(2,1)S(1)}, bf16[400,128]{1,0:T(8,128)(2,1)S(1)}, u32[]{:S(2)}, u32[]{:S(2)}) collective-permute-start(bf16[400,128]{1,0:T(8,128)(2,1)S(1)} %get-tuple-element.28), channel_id=1, source_target_pairs={{0,4},{1,5},{2,6},{3,7},{4,0},{5,1},{6,2},{7,3},{8,12},{9,13},{10,... | collective-permute-start | bytes 307208 | tf_op jit(solution)/shard_map/ppermute | solution.py:525
  12.3 15.5 %collective-permute-start.5 = (bf16[400,128]{1,0:T(8,128)(2,1)S(1)}, bf16[400,128]{1,0:T(8,128)(2,1)S(1)}, u32[]{:S(2)}, u32[]{:S(2)}) collective-permute-start(bf16[400,128]{1,0:T(8,128)(2,1)S(1)} %get-tuple-element.29), channel_id=1, source_target_pairs={{0,5},{1,4},{2,7},{3,6},{4,1},{5,0},{6,3},{7,2},{8,13},{9,12},{10,... | collective-permute-start | bytes 307208 | tf_op jit(solution)/shard_map/ppermute | solution.py:525
  13.6 14.2 %collective-permute-start.6 = (bf16[400,128]{1,0:T(8,128)(2,1)S(1)}, bf16[400,128]{1,0:T(8,128)(2,1)S(1)}, u32[]{:S(2)}, u32[]{:S(2)}) collective-permute-start(bf16[400,128]{1,0:T(8,128)(2,1)S(1)} %get-tuple-element.30), channel_id=1, source_target_pairs={{0,6},{1,7},{2,4},{3,5},{4,2},{5,3},{6,0},{7,1},{8,14},{9,15},{10,... | collective-permute-start | bytes 307208 | tf_op jit(solution)/shard_map/ppermute | solution.py:525
  17.2 10.6 %collective-permute-start.7 = (bf16[400,128]{1,0:T(8,128)(2,1)S(1)}, bf16[400,128]{1,0:T(8,128)(2,1)S(1)}, u32[]{:S(2)}, u32[]{:S(2)}) collective-permute-start(bf16[400,128]{1,0:T(8,128)(2,1)S(1)} %get-tuple-element.31), channel_id=1, source_target_pairs={{0,7},{1,6},{2,5},{3,4},{4,3},{5,2},{6,1},{7,0},{8,15},{9,14},{10,... | collective-permute-start | bytes 307208 | tf_op jit(solution)/shard_map/ppermute | solution.py:525
  35.0 1.3 %collective-permute-start.8 = (f32[136,128]{1,0:T(8,128)S(1)}, f32[136,128]{1,0:T(8,128)S(1)}, u32[]{:S(2)}, u32[]{:S(2)}) collective-permute-start(f32[136,128]{1,0:T(8,128)S(1)} %get-tuple-element.34), channel_id=1, source_target_pairs={{0,8},{8,0},{1,9},{9,1},{2,10},{10,2},{3,11},{11,3},{4,12},{12,4},... | collective-permute-start | bytes 208904 | tf_op jit(solution)/shard_map/ppermute | solution.py:560
  53.9 1.6 %collective-permute-start.9 = (bf16[8,144,128]{2,1,0:T(8,128)(2,1)S(1)}, bf16[8,144,128]{2,1,0:T(8,128)(2,1)S(1)}, u32[]{:S(2)}, u32[]{:S(2)}) collective-permute-start(bf16[8,144,128]{2,1,0:T(8,128)(2,1)S(1)} %all_to_all.5.own), channel_id=1, source_target_pairs={{0,8},{8,0},{1,9},{9,1},{2,10},{10,2},{3,11},{11,3},{4,12},{12,4},... | collective-permute-start | bytes 884744 | tf_op jit(solution)/shard_map/ppermute | solution.py:562

commit v3 on v0

--- a/solution.py
+++ b/solution.py
@@ -3,6 +3,8 @@
 import jax
 import jax.numpy as jnp
 from jax import lax
+from jax.experimental import pallas as pl
+from jax.experimental.pallas import tpu as pltpu
 from jax.sharding import PartitionSpec as P
 
 C = 256
@@ -64,7 +66,7 @@
     return (left_acc, right_out, weight_acc, bias_acc)
 
 
-def local(
+def general(
     alignment,
     norm_mean,
     norm_inverse,
@@ -133,6 +135,509 @@
     return (activation_grad, totals[0], totals[1], totals[4], totals[5], totals[2], totals[3])
 
 
+LANES = 128
+PROJ_ROWS = 256
+MASK_AT = 256
+COT_AT = 272
+MESSAGE = 336
+SMALL_AT = 256
+PARTIAL = 264
+SENT = 272
+PEERS = ((4, 5, 1, 0), (6, 7, 2, 3))
+ORDER = (0, 4, 1, 5, 6, 2, 7, 3)
+VMEM = pltpu.CompilerParams(vmem_limit_bytes=24 * 1024 * 1024)
+F32 = jnp.float32
+BF16 = jnp.bfloat16
+
+
+def dot_nt(a, b):
+    return lax.dot_general(a, b, (((1,), (1,)), ((), ())), preferred_element_type=F32)
+
+
+def dot_nn(a, b):
+    return lax.dot_general(a, b, (((1,), (0,)), ((), ())), preferred_element_type=F32)
+
+
+def low_lanes(shape):
+    return lax.broadcasted_iota(jnp.int32, shape, 1) < LANES // 2
+
+
+def swap_halves(x):
+    return pltpu.roll(x, LANES // 2, 1)
+
+
+def strided(wide, start, size, stride):
+    return jnp.concatenate([wide[h, pl.ds(start, size, stride=stride), :] for h in range(2)], axis=1)
+
+
+def prepare(*rest):
+    sources = rest[:11]
+    mask, gain, shift, weight, cotangent, out_weight, hat, stats, present = rest[11:20]
+    messages = rest[20:-12]
+    count = len(messages)
+    alignment, mean, inverse, bias, residue, wide, packed, cot, turned, square, arrived, late = rest[-12:]
+    targets = (alignment, mean, inverse, bias, residue, mask, gain, shift, weight, cotangent)
+    copies = [pltpu.make_async_copy(f, t, arrived.at[i]) for i, (f, t) in enumerate(zip(sources, targets))]
+    for copy in copies:
+        copy.start()
+    last = pltpu.make_async_copy(sources[-1], out_weight, late)
+    last.start()
+    for copy in copies:
+        copy.wait()
+    col, row = lax.axis_index("col"), lax.axis_index("row")
+    seqs, own, channels = alignment.shape
+    total = cotangent.shape[1]
+    square[0:own, :seqs] = mean[...]
+    square[own : 2 * own, :seqs] = inverse[...]
+    square[2 * own : 3 * own, : 2 * P_SIZE] = jnp.broadcast_to(bias[...], (own, 2 * P_SIZE))
+    square[3 * own : 4 * own, :total] = jnp.broadcast_to(residue[...].astype(F32), (own, total))
+    stats[...] = square[...].T
+    own_rows = pl.ds(pl.multiple_of(col * own, own), own)
+    present[...] = jnp.broadcast_to(stats[own_rows, 3 * own : 3 * own + 1], (own, LANES))
+    live = mask[...].astype(F32) * present[:, :seqs]
+    values = alignment[...].astype(F32)
+    for h in range(2):
+        wide[h] = values[:, :, h * LANES : (h + 1) * LANES].reshape(seqs * own, LANES)
+    for r in range(own):
+        hatted = (strided(wide, r, seqs, own) - stats[:seqs, r : r + 1]) * stats[
+            :seqs, own + r : own + r + 1
+        ]
+        hat[r] = hatted
+        normed = (hatted * gain[...] + shift[...]).astype(BF16)
+        projected = dot_nt(weight[...], normed) + stats[: 2 * P_SIZE, 2 * own : 2 * own + 1]
+        projected = projected * live[r : r + 1]
+        packed[pl.ds(r, P_SIZE, stride=own), :] = jnp.concatenate(
+            [projected[:P_SIZE], projected[P_SIZE:]], axis=1
+        )
+    shared = packed[...].astype(BF16)
+    depth = Z // count
+    for message in messages:
+        message[0:PROJ_ROWS, :] = shared
+
+    @pl.when(row == 0)
+    def _():
+        cot[...] = cotangent[...].astype(F32).reshape(own * total, Z)
+        for k, message in enumerate(messages):
+            peer = col ^ ORDER[k]
+            message[COT_AT:MESSAGE, :] = jnp.concatenate(
+                [cot[pl.ds(own * peer + j, own, stride=total), :] for j in range(own)], axis=0
+            ).astype(BF16)
+
+    @pl.when(row != 0)
+    def _():
+        for i in range(own // 2):
+            pair = jnp.concatenate([cotangent[i], cotangent[i + own // 2]], axis=0).astype(F32)
+            turned[i] = pair.T.astype(BF16)
+        for k, message in enumerate(messages):
+            at = pl.multiple_of((col ^ ORDER[k]) * depth, depth)
+            for i in range(own // 2):
+                message[COT_AT + i * depth : COT_AT + (i + 1) * depth, :] = turned[i, pl.ds(at, depth), :]
+
+    last.wait()
+
+
+def add_masks(mask, present, mate, *rest):
+    messages = rest[len(rest) // 2 :]
+    here = present[...]
+    live = jnp.concatenate([mask[...], mate[...]], axis=1).astype(F32) * here
+    masks = jnp.concatenate([live, here], axis=0).astype(BF16)
+    for message in messages:
+        message[MASK_AT:COT_AT, :] = masks
+
+
+def collect(*rest):
+    messages, cots = rest[:-1], rest[-1]
+    col = lax.axis_index("col")
+    for k, message in enumerate(messages):
+        cots[col ^ ORDER[k]] = message[COT_AT:MESSAGE, :]
+
+
+def interleave(product, target, group, at):
+    half = LANES // 2
+    low = low_lanes((P_SIZE, LANES))
+    for a in range(0, product.shape[0] // P_SIZE, 2):
+        for b in range(0, group, 2):
+            first = product[a * P_SIZE : (a + 1) * P_SIZE, b * half : (b + 2) * half]
+            second = product[(a + 1) * P_SIZE : (a + 2) * P_SIZE, b * half : (b + 2) * half]
+            lanes = slice((at + a) * half, (at + a + 2) * half)
+            target[b * P_SIZE : (b + 1) * P_SIZE, lanes] = jnp.where(
+                low, first, swap_halves(second)
+            ).astype(BF16)
+            target[(b + 1) * P_SIZE : (b + 2) * P_SIZE, lanes] = jnp.where(
+                low, swap_halves(first), second
+            ).astype(BF16)
+
+
+BLOCK = 8
+
+
+def left_part(cotangent, out_weight, *rest):
+    messages = rest[:-11]
+    every, gathered, scale_own, scale_twice, live_out, left_grad, live_all, present_all, grad_own, outer, wide = rest[-11:]
+    col = lax.axis_index("col")
+    own, total = cotangent.shape[:2]
+    for k, message in enumerate(messages):
+        at = pl.multiple_of((col ^ ORDER[k]) * own, own)
+        block = message[0:PROJ_ROWS, :].astype(F32)
+        for q in range(P_SIZE):
+            every[pl.ds(q * total + at, own), :] = block[q * own : (q + 1) * own]
+        masks = message[MASK_AT:COT_AT, :].astype(F32)
+        live_all[pl.ds(at, own), :] = masks[:own]
+        present_all[pl.ds(at, own), :] = masks[own:]
+    live = live_all[...].astype(BF16)
+    present = present_all[...].astype(BF16)
+    masks = messages[0][MASK_AT:COT_AT, :]
+    live_out[...] = masks[:own].astype(F32)
+
+    def scale_of(live_other, present_other):
+        counts = dot_nt(live, live_other)
+        return dot_nt(present, present_other) * (1.0 / LANES) / jnp.maximum(counts, 1.0)
+
+    scale_own[:, :own] = scale_of(masks[:own], masks[own:])
+    scale_twice[...] = scale_of(
+        jnp.concatenate([live, live], axis=0), jnp.concatenate([present, present], axis=0)
+    )
+    for i in range(own):
+        grad_own[i * total : (i + 1) * total, :] = (
+            cotangent[i].astype(F32) * scale_own[:, i : i + 1]
+        ).astype(BF16)
+    wide[...] = out_weight[...].astype(F32)
+    for a in range(0, P_SIZE, BLOCK):
+        by_second = jnp.concatenate(
+            [wide[pl.ds(q, P_SIZE, stride=P_SIZE), :] for q in range(a, a + BLOCK)], axis=0
+        ).astype(BF16)
+        interleave(dot_nt(by_second, grad_own[...]), outer, own, a)
+    gathered[...] = every[...].astype(BF16)
+    left_grad[...] = swap_halves(dot_nn(outer[...], gathered[...]))
+
+
+def quad_members(quad):
+    base = quad // 2 * 8 + quad % 2 * 2
+    return ((base, base + 4), (base + 1, base + 5))
+
+
+def sums_part(
+    cots, mate, out_weight, every, gathered, scale_own, scale_twice, live, left_grad, hat, gain, shift, weight, normed_grads, keep, turned, grad_turned, grad_slice, outer, corner, mixed, square
+):
+    row = lax.axis_index("row")
+    count = cots.shape[0]
+    own, seqs, channels = hat.shape
+    total = grad_turned.shape[0] // own
+    depth = Z // count
+    half = LANES // 2
+    pairs = own // 2
+    mine = row == 0
+    low = low_lanes((own, LANES))
+    bias_acc = jnp.zeros((depth, LANES), F32)
+    for c in range(count):
+        one, two = cots[c].astype(F32), mate[c].astype(F32)
+        block = jnp.where(mine, one, two)
+        for j in range(own):
+            turned[j * total + c * own : j * total + (c + 1) * own, :] = block[j * own : (j + 1) * own]
+        block = jnp.where(mine, two, one)
+        tile = scale_twice[c * own : (c + 1) * own, :]
+        tile = jnp.where(low, tile, jnp.concatenate([tile[pairs:], tile[:pairs]], axis=0))
+        for i in range(pairs):
+            piece = block[i * depth : (i + 1) * depth] * tile[i : i + 1, :]
+            bias_acc = bias_acc + piece
+            grad_slice[
+                (c * 2 + i // 2) * depth : (c * 2 + i // 2 + 1) * depth,
+                i % 2 * LANES : (i % 2 + 1) * LANES,
+            ] = piece.astype(BF16)
+    for j in range(own):
+        spot = slice(j * total, (j + 1) * total)
+        grad_turned[spot, :] = (turned[spot, :] * scale_own[:, j : j + 1]).astype(BF16)
+    for a in range(0, P_SIZE, BLOCK):
+        interleave(
+            dot_nt(out_weight[a * P_SIZE : (a + BLOCK) * P_SIZE, :], grad_turned[...]), outer, own, a
+        )
+    right_grad = dot_nn(outer[...], gathered[...])
+
+    input_acc = jnp.zeros((2 * P_SIZE, channels), F32)
+    proj_acc = jnp.zeros((2 * P_SIZE, seqs), F32)
+    gain_acc = jnp.zeros((1, channels), F32)
+    shift_acc = jnp.zeros((1, channels), F32)
+    for r in range(own):
+        hatted = hat[r]
+        normed = (hatted * gain[...] + shift[...]).astype(BF16)
+        spot = slice(r * P_SIZE, (r + 1) * P_SIZE)
+        proj_grad = jnp.concatenate([left_grad[spot, :seqs], right_grad[spot, :seqs]], axis=0)
+        proj_grad = proj_grad * live[r : r + 1, :seqs]
+        proj_acc = proj_acc + proj_grad
+        input_acc = input_acc + dot_nn(proj_grad.astype(BF16), normed)
+        normed_grad = dot_nn(proj_grad.T.astype(BF16), weight[...])
+        gain_acc = gain_acc + jnp.sum(normed_grad * hatted, axis=0, keepdims=True)
+        shift_acc = shift_acc + jnp.sum(normed_grad, axis=0, keepdims=True)
+        normed_grads[r] = normed_grad
+
+    quads = count * own // 4
+    low = low_lanes((total, LANES))
+    corner[...] = jnp.zeros_like(corner)
+    for q in range(P_SIZE):
+        block = every[q * total : (q + 1) * total, :]
+        here = jnp.where(low, 0.0, block)
+        moved = swap_halves(here).astype(BF16)
+        here = here.astype(BF16)
+        slot = q % corner.shape[0]
+        for at in range(4):
+            lanes = slice(at // 2 * LANES, (at // 2 + 1) * LANES)
+            corner[slot, at * total : (at + 1) * total, lanes] = here if at % 2 else moved
+        mixed[:, q * depth : (q + 1) * depth, :] = (
+            dot_nn(grad_slice[...], corner[slot]).astype(BF16).reshape(quads, depth, 4 * total)
+        )
+    low = low_lanes((P_SIZE, LANES))
+    weight_acc = jnp.zeros((P_SIZE * depth, P_SIZE), F32)
+    for quad in range(quads):
+        rhs = []
+        for pair in quad_members(quad):
+            one, two = (every[pl.ds(i, P_SIZE, stride=total), :] for i in pair)
+            rhs.append(jnp.where(low, one, swap_halves(two)))
+        weight_acc = weight_acc + dot_nt(mixed[quad], jnp.concatenate(rhs, axis=1).astype(BF16))
+    group = P_SIZE * depth // 4
+    weight_acc = jnp.concatenate([weight_acc[b * group : (b + 1) * group] for b in range(4)], axis=1)
+
+    square[...] = jnp.zeros((LANES, LANES), F32)
+    square[0 : 2 * P_SIZE, :seqs] = proj_acc
+    square[half : half + depth, :] = bias_acc * 0.5
+    sums = jnp.sum(square[...].T, axis=0, keepdims=True)
+    keep[0:LANES, :] = weight_acc
+    for h in range(2):
+        lanes = slice(h * LANES, (h + 1) * LANES)
+        keep[LANES + h * half : LANES + (h + 1) * half, :] = input_acc[:, lanes]
+        keep[SMALL_AT + h : SMALL_AT + h + 1, :] = gain_acc[:, lanes]
+        keep[SMALL_AT + 2 + h : SMALL_AT + 3 + h, :] = shift_acc[:, lanes]
+    keep[SMALL_AT + 4 : PARTIAL, :] = jnp.concatenate([sums, jnp.zeros((3, LANES), F32)], axis=0)
+
+
+def activations(normed_grads, hat, stats, gain, activation, wide):
+    own, seqs, channels = hat.shape
+    for r in range(own):
+        hatted = hat[r]
+        hat_grad = normed_grads[r] * gain[...]
+        first = jnp.sum(hat_grad, axis=1, keepdims=True) * (1.0 / channels)
+        second = jnp.sum(hat_grad * hatted, axis=1, keepdims=True) * (1.0 / channels)
+        result = stats[:seqs, own + r : own + r + 1] * (hat_grad - first - hatted * second)
+        for h in range(2):
+            wide[h, pl.ds(r, seqs, stride=own), :] = result[:, h * LANES : (h + 1) * LANES]
+    activation[...] = jnp.concatenate(
+        [wide[h].reshape(seqs, own, LANES) for h in range(2)], axis=2
+    ).astype(BF16)
+
+
+def pack(kept, given, partial):
+    both = kept[...] + given[...]
+    high = both.astype(BF16)
+    small = both[SMALL_AT:] - high[SMALL_AT:].astype(F32)
+    partial[...] = jnp.concatenate([high, small.astype(BF16)], axis=0)
+
+
+def stack(*rest):
+    for k, part in enumerate(rest[:-1]):
+        rest[-1][k] = part[...]
+
+
+def finish(own, received, mate, input_out, bias_out, weight_out, out_bias_out, gain_out, shift_out, ordered):
+    col, row = lax.axis_index("col"), lax.axis_index("row")
+    count = ordered.shape[0]
+    depth = Z // count
+    half = LANES // 2
+    lane = lax.broadcasted_iota(jnp.int32, (1, LANES), 1)
+    ordered[col] = own[...]
+    for k, (one, two) in enumerate(zip(*PEERS)):
+        ordered[col ^ jnp.where(row == 0, one, two)] = received[k]
+        ordered[col ^ jnp.where(row == 0, two, one)] = mate[k]
+    ordered[col] = own[...]
+    for a in range(8):
+        turned = jnp.concatenate(
+            [ordered[c, a * depth : (a + 1) * depth] for c in range(count)], axis=0
+        ).astype(F32).T
+        for b in range(4):
+            weight_out[pl.ds(8 * b + a, P_SIZE, stride=P_SIZE), :] = turned[b * P_SIZE : (b + 1) * P_SIZE]
+    input_acc = jnp.zeros((LANES, LANES), F32)
+    small_acc = jnp.zeros((8, LANES), F32)
+    out_bias = jnp.zeros((1, LANES), F32)
+    for c in range(count):
+        input_acc = input_acc + ordered[c, LANES:SMALL_AT].astype(F32)
+        both = ordered[c, SMALL_AT:].astype(F32)
+        small = both[:8] + both[8:]
+        small_acc = small_acc + small
+        bias = pltpu.roll(small[4:5], (c * depth + half) % LANES, 1)
+        out_bias = jnp.where((lane >= c * depth) & (lane < (c + 1) * depth), bias, out_bias)
+    for h in range(2):
+        lanes = slice(h * LANES, (h + 1) * LANES)
+        input_out[:, lanes] = input_acc[h * half : (h + 1) * half]
+        gain_out[:, lanes] = small_acc[h : h + 1]
+        shift_out[:, lanes] = small_acc[2 + h : 3 + h]
+    bias_out[...] = small_acc[4:5, :half]
+    out_bias_out[...] = out_bias
+
+
+def shape(dims, dtype):
+    return jax.ShapeDtypeStruct(dims, dtype)
+
+
+VMEM_SPEC = pl.BlockSpec(memory_space=pltpu.VMEM)
+HBM_SPEC = pl.BlockSpec(memory_space=pltpu.HBM)
+
+
+def call(kernel, outputs, specs, arguments, scratch=(), aliases=None):
+    return pl.pallas_call(
+        kernel,
+        out_shape=outputs,
+        in_specs=specs,
+        out_specs=[VMEM_SPEC] * len(outputs),
+        scratch_shapes=list(scratch),
+        input_output_aliases=aliases or {},
+        compiler_params=VMEM,
+        name=kernel.__name__,
+    )(*arguments)
+
+
+def tiled(
+    alignment,
+    norm_mean,
+    norm_inverse,
+    norm_gain,
+    norm_shift,
+    input_weight,
+    input_bias,
+    output_weight,
+    pair_cotangent,
+    residue_mask,
+    sequence_mask,
+):
+    count = lax.axis_size("col")
+    seqs, own, channels = alignment.shape
+    total = pair_cotangent.shape[1]
+    depth = Z // count
+    mask = sequence_mask.T
+    turn = [(0, 1), (1, 0)]
+    mate = lax.ppermute(mask, "row", turn)
+    fetched = [alignment, norm_mean.T, norm_inverse.T, input_bias[None, :], residue_mask[None, :]]
+    passed = [mask, norm_gain[None, :], norm_shift[None, :], input_weight.T, pair_cotangent, output_weight]
+    operands = [pltpu.with_memory_space_constraint(a, pltpu.HBM) for a in fetched + passed]
+    mask, gain, shift, weight, cotangent, out_weight, hat, stats, present, *messages = call(
+        prepare,
+        [shape(a.shape, a.dtype) for a in passed]
+        + [shape((own, seqs, channels), F32), shape((LANES, LANES), F32), shape((own, LANES), F32)]
+        + [shape((MESSAGE, LANES), BF16)] * count,
+        [HBM_SPEC] * len(operands),
+        operands,
+        [pltpu.VMEM(a.shape, a.dtype) for a in fetched]
+        + [
+            pltpu.VMEM((2, seqs * own, LANES), F32),
+            pltpu.VMEM((PROJ_ROWS, LANES), F32),
+            pltpu.VMEM((own * total, Z), F32),
+            pltpu.VMEM((own // 2, Z, LANES), BF16),
+            pltpu.VMEM((LANES, LANES), F32),
+            pltpu.SemaphoreType.DMA((len(operands) - 1,)),
+            pltpu.SemaphoreType.DMA,
+        ],
+    )
+    messages = call(
+        add_masks,
+        [shape((MESSAGE, LANES), BF16)] * count,
+        [VMEM_SPEC] * (3 + count),
+        [mask, present, mate, *messages],
+        aliases={3 + k: k for k in range(count)},
+    )
+    messages = [messages[0]] + [
+        lax.ppermute(messages[k], "col", [(c, c ^ ORDER[k]) for c in range(count)]) for k in range(1, count)
+    ]
+    (cots,) = call(
+        collect,
+        [shape((count, MESSAGE - COT_AT, LANES), BF16)],
+        [VMEM_SPEC] * count,
+        messages,
+    )
+    mate_cots = lax.ppermute(cots, "row", turn)
+    every, gathered, scale_own, scale_twice, live, left_grad = call(
+        left_part,
+        [
+            shape((P_SIZE * total, LANES), F32),
+            shape((P_SIZE * total, LANES), BF16),
+            shape((total, LANES), F32),
+            shape((total, LANES), F32),
+            shape((own, LANES), F32),
+            shape((own * P_SIZE, LANES), F32),
+        ],
+        [VMEM_SPEC] * (2 + count),
+        [cotangent, out_weight, *messages],
+        [
+            pltpu.VMEM((total, LANES), F32),
+            pltpu.VMEM((total, LANES), F32),
+            pltpu.VMEM((own * total, Z), BF16),
+            pltpu.VMEM((own * P_SIZE, P_SIZE * total), BF16),
+            pltpu.VMEM((P_SIZE * P_SIZE, LANES), F32),
+        ],
+    )
+    normed_grads, keep = call(
+        sums_part,
+        [shape((own, seqs, channels), F32), shape((PARTIAL, LANES), F32)],
+        [VMEM_SPEC] * 13,
+        [cots, mate_cots, out_weight, every, gathered, scale_own, scale_twice, live, left_grad, hat, gain, shift, weight],
+        [
+            pltpu.VMEM((own * total, Z), F32),
+            pltpu.VMEM((own * total, Z), BF16),
+            pltpu.VMEM((count * own // 4 * depth, 2 * LANES), BF16),
+            pltpu.VMEM((own * P_SIZE, P_SIZE * total), BF16),
+            pltpu.VMEM((4, 4 * total, 2 * LANES), BF16),
+            pltpu.VMEM((count * own // 4, P_SIZE * depth, 4 * seqs), BF16),
+            pltpu.VMEM((LANES, LANES), F32),
+        ],
+    )
+    given = lax.ppermute(keep, "row", turn)
+    (activation,) = call(
+        activations,
+        [shape(alignment.shape, BF16)],
+        [VMEM_SPEC] * 4,
+        [normed_grads, hat, stats, gain],
+        [pltpu.VMEM((2, seqs * own, LANES), F32)],
+    )
+    (partial,) = call(pack, [shape((SENT, LANES), BF16)], [VMEM_SPEC] * 2, [keep, given])
+    parts = []
+    for pair in zip(*PEERS):
+        turns = [
+            (row * count + c, row * count + (c ^ pair[row])) for row in range(2) if pair[row] for c in range(count)
+        ]
+        parts.append(lax.ppermute(partial, ("row", "col"), turns))
+    (received,) = call(
+        stack, [shape((len(parts), SENT, LANES), BF16)], [VMEM_SPEC] * len(parts), parts
+    )
+    theirs = lax.ppermute(received, "row", turn)
+    input_grad, bias_grad, weight_grad, out_bias_grad, gain_grad, shift_grad = call(
+        finish,
+        [
+            shape((2 * P_SIZE, channels), F32),
+            shape((1, 2 * P_SIZE), F32),
+            shape((P_SIZE * P_SIZE, Z), F32),
+            shape((1, Z), F32),
+            shape((1, channels), F32),
+            shape((1, channels), F32),
+        ],
+        [VMEM_SPEC] * 3,
+        [partial, received, theirs],
+        [pltpu.VMEM((count, SENT, LANES), BF16)],
+    )
+    return (activation, input_grad.T, bias_grad[0], weight_grad, out_bias_grad[0], gain_grad[0], shift_grad[0])
+
+
+def local(*args):
+    alignment, cotangent = args[0], args[8]
+    seqs, own, channels = alignment.shape
+    total = cotangent.shape[1]
+    count = lax.axis_size("col")
+    fits = (
+        2 * seqs == LANES
+        and 2 * total == LANES
+        and own == 8
+        and channels == 2 * LANES
+        and count == 8
+        and lax.axis_size("row") == 2
+    )
+    return tiled(*args) if fits else general(*args)
+
+
 def solution(mesh):
     in_specs = (
         P(("group", "row"), "col", None),

time: 234 us -> 45.9 us (0.20)
  blocking collectives: 98.1 us -> 0 us
  waiting for transfers between devices: 68.1 us -> 11.8 us
  local copies, waits for them, and re-layouts: 35.5 us -> 0 us
  starting transfers between devices: 0.08 us -> 23.3 us
  between operations: 14.3 us -> 0.72 us
  matrix products: 11.7 us -> 0 us
  Pallas kernels: 0 us -> 10 us
  other arithmetic: 5.27 us -> 0 us
    all_gather x2 -> x0, blocking collectives: 64.1 us -> none  [the longest x1 32.2 us: local(): lax.all_gather(live_int, 'col', axis=1, tiled=True)]
    psum x1 -> x0, waiting for transfers between devices: 60 us -> none  [local(): lax.psum((weight_part, bias_part, gain_part, shift_part, weight_out, bias...]
    psum x2 -> x0, blocking collectives: 34 us -> none  [the longest x1 31.5 us: local(): lax.psum((weight_part, bias_part, gain_part, shift_part, weight_out, bias...]
    ppermute x0 -> x15, starting transfers between devices: none -> 23.3 us  [the longest x7 16.9 us: tiled(): lax.ppermute(messages[k], 'col', [(c, c ^ ORDER[k]) for c in range(count)])]
    convert_element_type x6 -> x0, local copies, waits for them, and re-layouts: 12.2 us -> none  [the longest x2 6.19 us: contract(): outer_high = outer.astype(jnp.bfloat16)]
    ppermute x0 -> x15, waiting for transfers between devices: none -> 11.8 us  [the longest x7 5.37 us: tiled(): lax.ppermute(messages[k], 'col', [(c, c ^ ORDER[k]) for c in range(count)])]
    dot_general x10 -> x0, matrix products: 11.7 us -> none  [the longest x1 3.44 us: contract(): jnp.einsum('ijpq,sjq->sip', outer_grad, right_cols, preferred_element_typ...]
    pallas_call x0 -> x9, Pallas kernels: none -> 10 us  [call(): pl.pallas_call(kernel, out_shape=outputs, in_specs=specs, out_specs=[VMEM...]
  transfers between devices with their start and end apart: 2 -> 15, of which waited for: 2 -> 6; matrix products, arithmetic and copies ran while one was open for 11% -> 0% of each run, Pallas kernels for 0% -> 11%
where the time goes in v3:
time: 45.9 us; the launch traced here: 45.8 us
  starting transfers between devices  23.3 us (51%)
  waiting for transfers between devices  11.8 us (26%)
  Pallas kernels  10 us (22%)
  between operations  0.72 us (2%)
    ppermute x7, starting transfers between devices, tiled(): lax.ppermute(messages[k], 'col', [(c, c ^ ORDER[k]) for c in range(count)])  16.9 us
    pallas_call x9, Pallas kernels, call(): pl.pallas_call(kernel, out_shape=outputs, in_specs=specs, out_specs=[VMEM...  10 us
    ppermute x7, waiting for transfers between devices, tiled(): lax.ppermute(messages[k], 'col', [(c, c ^ ORDER[k]) for c in range(count)])  5.37 us
    ppermute x4, waiting for transfers between devices, tiled(): parts.append(lax.ppermute(partial, ('row', 'col'), turns))  5.18 us
    ppermute x4, starting transfers between devices, tiled(): parts.append(lax.ppermute(partial, ('row', 'col'), turns))  5.1 us
    ppermute x1, waiting for transfers between devices, tiled(): given = lax.ppermute(keep, 'row', turn)  0.99 us
  transfers between devices with their start and end apart: 15, of which 6 were waited for; matrix products, arithmetic and copies ran while one was open for 0% of the time, Pallas kernels for 11%

profile of v3, /device:TPU:0, one launch (start us, length us, event | category | flops | bytes accessed | tf_op | source)
XLA Modules:
  0.0 45.8 jit_solution(7106453570340877010)
XLA Ops:
  0.6 0.5 %collective-permute-start = (s32[8,64]{1,0:T(8,128)}, s32[8,64]{1,0:T(8,128)S(1)}, u32[]{:S(2)}, u32[]{:S(2)}) collective-permute-start(s32[8,64]{1,0:T(8,128)} %bitcast.16), channel_id=1, source_target_pairs={{0,8},{8,0},{1,9},{9,1},{2,10},{10,2},{3,11},{11,3},{4,12},{12,4},... | collective-permute-start | bytes 6152 | tf_op jit(solution)/shard_map/ppermute | solution.py:515
  1.2 2.1 %prepare.1 = (s32[8,64]{1,0:T(8,128)S(1)}, f32[1,256]{1,0:T(1,128)S(1)}, f32[1,256]{1,0:T(1,128)S(1)}, bf16[64,256]{1,0:T(8,128)(2,1)S(1)}, bf16[8,64,128]{2,1,0...) custom-call(bf16[64,8,256]{2,1,0:T(8,128)(2,1)} %rest_0_.1, ...), custom_call_target="tpu_custom_call" | custom-call | tf_op jit(solution)/shard_map/prepare/pallas_call | solution.py:484
  3.2 0.0 collective-permute-done.mate
  3.2 0.1 add_masks.1
  3.3 3.6 %collective-permute-start.1 = (bf16[336,128]{1,0:T(8,128)(2,1)S(1)}, bf16[336,128]{1,0:T(8,128)(2,1)S(1)}, u32[]{:S(2)}, u32[]{:S(2)}) collective-permute-start(bf16[336,128]{1,0:T(8,128)(2,1)S(1)} %get-tuple-element.57), channel_id=1, source_target_pairs={{0,4},{1,5},{2,6},{3,7},{4,0},{5,1},{6,2},{7,3},{8,12},{9,13},{10,... | collective-permute-start | bytes 258056 | tf_op jit(solution)/shard_map/ppermute | solution.py:545
  6.9 1.5 %collective-permute-start.2 = (bf16[336,128]{1,0:T(8,128)(2,1)S(1)}, bf16[336,128]{1,0:T(8,128)(2,1)S(1)}, u32[]{:S(2)}, u32[]{:S(2)}) collective-permute-start(bf16[336,128]{1,0:T(8,128)(2,1)S(1)} %get-tuple-element.58), channel_id=1, source_target_pairs={{0,1},{1,0},{2,3},{3,2},{4,5},{5,4},{6,7},{7,6},{8,9},{9,8},{10,11... | collective-permute-start | bytes 258056 | tf_op jit(solution)/shard_map/ppermute | solution.py:545
  8.4 0.0 collective-permute-start.3
  8.5 3.9 %collective-permute-start.4 = (bf16[336,128]{1,0:T(8,128)(2,1)S(1)}, bf16[336,128]{1,0:T(8,128)(2,1)S(1)}, u32[]{:S(2)}, u32[]{:S(2)}) collective-permute-start(bf16[336,128]{1,0:T(8,128)(2,1)S(1)} %get-tuple-element.60), channel_id=1, source_target_pairs={{0,6},{1,7},{2,4},{3,5},{4,2},{5,3},{6,0},{7,1},{8,14},{9,15},{10,... | collective-permute-start | bytes 258056 | tf_op jit(solution)/shard_map/ppermute | solution.py:545
  12.3 0.0 collective-permute-start.5
  12.3 0.0 collective-permute-done.1.rest_1_
  12.3 7.9 %collective-permute-start.6 = (bf16[336,128]{1,0:T(8,128)(2,1)S(1)}, bf16[336,128]{1,0:T(8,128)(2,1)S(1)}, u32[]{:S(2)}, u32[]{:S(2)}) collective-permute-start(bf16[336,128]{1,0:T(8,128)(2,1)S(1)} %get-tuple-element.62), channel_id=1, source_target_pairs={{0,7},{1,6},{2,5},{3,4},{4,3},{5,2},{6,1},{7,0},{8,15},{9,14},{10,... | collective-permute-start | bytes 258056 | tf_op jit(solution)/shard_map/ppermute | solution.py:545
  20.2 0.0 collective-permute-done.2.rest_2_
  20.2 0.0 collective-permute-start.7
  20.2 0.0 collective-permute-done.3.rest_3_
  20.2 0.0 collective-permute-done.4.rest_4_
  20.2 0.0 collective-permute-done.5.rest_5_
  20.3 3.4 %collective-permute-done.6.rest_6_ = bf16[336,128]{1,0:T(8,128)(2,1)S(1)} collective-permute-done((bf16[336,128]{1,0:T(8,128)(2,1)S(1)}, bf16[336,128]{1,0:T(8,128)(2,1)S(1)}, u32[]{:S(2)}, u32[]{:S(2)}) %collective-permute-start.6) | collective-permute-done | bytes 86048 | tf_op jit(solution)/shard_map/ppermute | solution.py:545
  23.6 2.0 %collective-permute-done.7.rest_7_ = bf16[336,128]{1,0:T(8,128)(2,1)S(1)} collective-permute-done((bf16[336,128]{1,0:T(8,128)(2,1)S(1)}, bf16[336,128]{1,0:T(8,128)(2,1)S(1)}, u32[]{:S(2)}, u32[]{:S(2)}) %collective-permute-start.7) | collective-permute-done | bytes 86048 | tf_op jit(solution)/shard_map/ppermute | solution.py:545
  25.6 0.1 collective-permute-start.8
  25.7 1.5 %left_part.1 = (f32[2048,128]{1,0:T(8,128)S(1)}, bf16[2048,128]{1,0:T(8,128)(2,1)S(1)}, f32[64,128]{1,0:T(8,128)S(1)}, f32[64,128]{1,0:T(8,128)S(1)}, f32[8,128]{1,0:T(8,128)S(1)}, /*index=5*/f32[256,128]{1,0:T(8,128)S(1)}) custom-call(bf16[8,64,128]{2,1,0:T(8,128)(2,1)S(1)} %get-tuple-element.65.cotangent, ...), custom_call_target="tpu_custom_call" | custom-call | tf_op jit(solution)/shard_map/left_part/pallas_call | solution.py:484
  27.2 0.0 collective-permute-done.8.mate
  27.2 3.8 %sums_part.1 = (f32[8,64,256]{2,1,0:T(8,128)S(1)}, f32[264,128]{1,0:T(8,128)S(1)}) custom-call(bf16[8,64,128]{2,1,0:T(8,128)(2,1)S(1)} %collect.1.cots, bf16[8,64,128]{2,1,0:T(8,128)(2,1)S(1)} %collective-permute-done.8.mate, bf16[1024,128]{1,0:T(8,128)(2,1)S(1)} %get-tuple-element.64.out_weight, f32[2048,128]{1,0:T(8,128)S(1)} %get-tuple-element.66.every, ...), custom_call_target="tpu_custom_call" | custom-call | tf_op jit(solution)/shard_map/sums_part/pallas_call | solution.py:484
  31.0 0.6 %collective-permute-start.9 = (f32[264,128]{1,0:T(8,128)S(1)}, f32[264,128]{1,0:T(8,128)S(1)}, u32[]{:S(2)}, u32[]{:S(2)}) collective-permute-start(f32[264,128]{1,0:T(8,128)S(1)} %get-tuple-element.78.kept), channel_id=1, source_target_pairs={{0,8},{8,0},{1,9},{9,1},{2,10},{10,2},{3,11},{11,3},{4,12},{12,4},... | collective-permute-start | bytes 405512 | tf_op jit(solution)/shard_map/ppermute | solution.py:589
  31.6 1.0 %collective-permute-done.9.given = f32[264,128]{1,0:T(8,128)S(1)} collective-permute-done((f32[264,128]{1,0:T(8,128)S(1)}, f32[264,128]{1,0:T(8,128)S(1)}, u32[]{:S(2)}, u32[]{:S(2)}) %collective-permute-start.9) | collective-permute-done | bytes 135200 | tf_op jit(solution)/shard_map/ppermute | solution.py:589
  32.6 1.1 %collective-permute-start.10 = (bf16[272,128]{1,0:T(8,128)(2,1)S(1)}, bf16[272,128]{1,0:T(8,128)(2,1)S(1)}, u32[]{:S(2)}, u32[]{:S(2)}) collective-permute-start(bf16[272,128]{1,0:T(8,128)(2,1)S(1)} %pack.1.own), channel_id=1, source_target_pairs={{0,4},{1,5},{2,6},{3,7},{4,0},{5,1},{6,2},{7,3},{8,14},{9,15},{10,... | collective-permute-start | bytes 208904 | tf_op jit(solution)/shard_map/ppermute | solution.py:603
  33.7 1.9 %collective-permute-start.11 = (bf16[272,128]{1,0:T(8,128)(2,1)S(1)}, bf16[272,128]{1,0:T(8,128)(2,1)S(1)}, u32[]{:S(2)}, u32[]{:S(2)}) collective-permute-start(bf16[272,128]{1,0:T(8,128)(2,1)S(1)} %pack.1.own), channel_id=1, source_target_pairs={{0,5},{1,4},{2,7},{3,6},{4,1},{5,0},{6,3},{7,2},{8,15},{9,14},{10,... | collective-permute-start | bytes 208904 | tf_op jit(solution)/shard_map/ppermute | solution.py:603
  35.5 1.5 %collective-permute-start.12 = (bf16[272,128]{1,0:T(8,128)(2,1)S(1)}, bf16[272,128]{1,0:T(8,128)(2,1)S(1)}, u32[]{:S(2)}, u32[]{:S(2)}) collective-permute-start(bf16[272,128]{1,0:T(8,128)(2,1)S(1)} %pack.1.own), channel_id=1, source_target_pairs={{0,1},{1,0},{2,3},{3,2},{4,5},{5,4},{6,7},{7,6},{8,10},{9,11},{10,... | collective-permute-start | bytes 208904 | tf_op jit(solution)/shard_map/ppermute | solution.py:603
  37.0 0.7 %collective-permute-start.13 = (bf16[272,128]{1,0:T(8,128)(2,1)S(1)}, bf16[272,128]{1,0:T(8,128)(2,1)S(1)}, u32[]{:S(2)}, u32[]{:S(2)}) collective-permute-start(bf16[272,128]{1,0:T(8,128)(2,1)S(1)} %pack.1.own), channel_id=1, source_target_pairs={{8,11},{9,10},{10,9},{11,8},{12,15},{13,14},{14,13},{15,12},{24,27... | collective-permute-start | bytes 208904 | tf_op jit(solution)/shard_map/ppermute | solution.py:603
  37.7 3.7 %collective-permute-done.10.rest_0_ = bf16[272,128]{1,0:T(8,128)(2,1)S(1)} collective-permute-done((bf16[272,128]{1,0:T(8,128)(2,1)S(1)}, bf16[272,128]{1,0:T(8,128)(2,1)S(1)}, u32[]{:S(2)}, u32[]{:S(2)}) %collective-permute-start.10) | collective-permute-done | bytes 69664 | tf_op jit(solution)/shard_map/ppermute | solution.py:603
  41.4 1.5 %collective-permute-done.11.rest_1_ = bf16[272,128]{1,0:T(8,128)(2,1)S(1)} collective-permute-done((bf16[272,128]{1,0:T(8,128)(2,1)S(1)}, bf16[272,128]{1,0:T(8,128)(2,1)S(1)}, u32[]{:S(2)}, u32[]{:S(2)}) %collective-permute-start.11) | collective-permute-done | bytes 69664 | tf_op jit(solution)/shard_map/ppermute | solution.py:603
  42.9 0.0 collective-permute-done.12.rest_2_
  42.9 0.0 collective-permute-done.13.rest_3_
  42.9 0.1 collective-permute-start.14
  43.0 1.3 %activations.1 = bf16[64,8,256]{2,1,0:T(8,128)(2,1)} custom-call(f32[8,64,256]{2,1,0:T(8,128)S(1)} %get-tuple-element.76.normed_grads, f32[8,64,256]{2,1,0:T(8,128)S(1)} %get-tuple-element.72.hat, f32[128,128]{1,0:T(8,128)S(1)} %get-tuple-element.77.stats, f32[1,256]{1,0:T(1,128)S(1)} %get-tuple-element.73.gain), custom_call_target="tpu_custom_call" | custom-call | tf_op jit(solution)/shard_map/activations/pallas_call | solution.py:484
  44.3 0.2 collective-permute-done.14.mate
  44.5 1.2 %finish.1 = (f32[64,256]{1,0:T(8,128)}, f32[1,64]{1,0:T(1,128)}, f32[1024,128]{1,0:T(8,128)}, f32[1,128]{1,0:T(1,128)}, f32[1,256]{1,0:T(1,128)}, /*index=5*/f32[1,256]{1,0:T(1,128)}) custom-call(bf16[272,128]{1,0:T(8,128)(2,1)S(1)} %pack.1.own, bf16[4,272,128]{2,1,0:T(8,128)(2,1)S(1)} %stack.1.received, bf16[4,272,128]{2,1,0:T(8,128)(2,1)S(1)} %collective-permute-done.14.mate), custom_call_target="tpu_custom_call" | custom-call | tf_op jit(solution)/shard_map/finish/pallas_call | solution.py:484
  (3 shorter events, 0.1 us)
Async XLA Ops:
  0.6 2.6 %collective-permute-start = (s32[8,64]{1,0:T(8,128)}, s32[8,64]{1,0:T(8,128)S(1)}, u32[]{:S(2)}, u32[]{:S(2)}) collective-permute-start(s32[8,64]{1,0:T(8,128)} %bitcast.16), channel_id=1, source_target_pairs={{0,8},{8,0},{1,9},{9,1},{2,10},{10,2},{3,11},{11,3},{4,12},{12,4},... | collective-permute-start | bytes 6152 | tf_op jit(solution)/shard_map/ppermute | solution.py:515
  3.3 9.0 %collective-permute-start.1 = (bf16[336,128]{1,0:T(8,128)(2,1)S(1)}, bf16[336,128]{1,0:T(8,128)(2,1)S(1)}, u32[]{:S(2)}, u32[]{:S(2)}) collective-permute-start(bf16[336,128]{1,0:T(8,128)(2,1)S(1)} %get-tuple-element.57), channel_id=1, source_target_pairs={{0,4},{1,5},{2,6},{3,7},{4,0},{5,1},{6,2},{7,3},{8,12},{9,13},{10,... | collective-permute-start | bytes 258056 | tf_op jit(solution)/shard_map/ppermute | solution.py:545
  6.9 13.3 %collective-permute-start.2 = (bf16[336,128]{1,0:T(8,128)(2,1)S(1)}, bf16[336,128]{1,0:T(8,128)(2,1)S(1)}, u32[]{:S(2)}, u32[]{:S(2)}) collective-permute-start(bf16[336,128]{1,0:T(8,128)(2,1)S(1)} %get-tuple-element.58), channel_id=1, source_target_pairs={{0,1},{1,0},{2,3},{3,2},{4,5},{5,4},{6,7},{7,6},{8,9},{9,8},{10,11... | collective-permute-start | bytes 258056 | tf_op jit(solution)/shard_map/ppermute | solution.py:545
  8.4 11.8 %collective-permute-start.3 = (bf16[336,128]{1,0:T(8,128)(2,1)S(1)}, bf16[336,128]{1,0:T(8,128)(2,1)S(1)}, u32[]{:S(2)}, u32[]{:S(2)}) collective-permute-start(bf16[336,128]{1,0:T(8,128)(2,1)S(1)} %get-tuple-element.59), channel_id=1, source_target_pairs={{0,5},{1,4},{2,7},{3,6},{4,1},{5,0},{6,3},{7,2},{8,13},{9,12},{10,... | collective-permute-start | bytes 258056 | tf_op jit(solution)/shard_map/ppermute | solution.py:545
  8.5 11.8 %collective-permute-start.4 = (bf16[336,128]{1,0:T(8,128)(2,1)S(1)}, bf16[336,128]{1,0:T(8,128)(2,1)S(1)}, u32[]{:S(2)}, u32[]{:S(2)}) collective-permute-start(bf16[336,128]{1,0:T(8,128)(2,1)S(1)} %get-tuple-element.60), channel_id=1, source_target_pairs={{0,6},{1,7},{2,4},{3,5},{4,2},{5,3},{6,0},{7,1},{8,14},{9,15},{10,... | collective-permute-start | bytes 258056 | tf_op jit(solution)/shard_map/ppermute | solution.py:545
  12.3 7.9 %collective-permute-start.5 = (bf16[336,128]{1,0:T(8,128)(2,1)S(1)}, bf16[336,128]{1,0:T(8,128)(2,1)S(1)}, u32[]{:S(2)}, u32[]{:S(2)}) collective-permute-start(bf16[336,128]{1,0:T(8,128)(2,1)S(1)} %get-tuple-element.61), channel_id=1, source_target_pairs={{0,2},{1,3},{2,0},{3,1},{4,6},{5,7},{6,4},{7,5},{8,10},{9,11},{10,... | collective-permute-start | bytes 258056 | tf_op jit(solution)/shard_map/ppermute | solution.py:545
  12.3 11.3 %collective-permute-start.6 = (bf16[336,128]{1,0:T(8,128)(2,1)S(1)}, bf16[336,128]{1,0:T(8,128)(2,1)S(1)}, u32[]{:S(2)}, u32[]{:S(2)}) collective-permute-start(bf16[336,128]{1,0:T(8,128)(2,1)S(1)} %get-tuple-element.62), channel_id=1, source_target_pairs={{0,7},{1,6},{2,5},{3,4},{4,3},{5,2},{6,1},{7,0},{8,15},{9,14},{10,... | collective-permute-start | bytes 258056 | tf_op jit(solution)/shard_map/ppermute | solution.py:545
  20.2 5.4 %collective-permute-start.7 = (bf16[336,128]{1,0:T(8,128)(2,1)S(1)}, bf16[336,128]{1,0:T(8,128)(2,1)S(1)}, u32[]{:S(2)}, u32[]{:S(2)}) collective-permute-start(bf16[336,128]{1,0:T(8,128)(2,1)S(1)} %get-tuple-element.63), channel_id=1, source_target_pairs={{0,3},{1,2},{2,1},{3,0},{4,7},{5,6},{6,5},{7,4},{8,11},{9,10},{10,... | collective-permute-start | bytes 258056 | tf_op jit(solution)/shard_map/ppermute | solution.py:545
  25.6 1.6 %collective-permute-start.8 = (bf16[8,64,128]{2,1,0:T(8,128)(2,1)S(1)}, bf16[8,64,128]{2,1,0:T(8,128)(2,1)S(1)}, u32[]{:S(2)}, u32[]{:S(2)}) collective-permute-start(bf16[8,64,128]{2,1,0:T(8,128)(2,1)S(1)} %collect.1.cots), channel_id=1, source_target_pairs={{0,8},{8,0},{1,9},{9,1},{2,10},{10,2},{3,11},{11,3},{4,12},{12,4},... | collective-permute-start | bytes 393224 | tf_op jit(solution)/shard_map/ppermute | solution.py:553
  31.0 1.5 %collective-permute-start.9 = (f32[264,128]{1,0:T(8,128)S(1)}, f32[264,128]{1,0:T(8,128)S(1)}, u32[]{:S(2)}, u32[]{:S(2)}) collective-permute-start(f32[264,128]{1,0:T(8,128)S(1)} %get-tuple-element.78.kept), channel_id=1, source_target_pairs={{0,8},{8,0},{1,9},{9,1},{2,10},{10,2},{3,11},{11,3},{4,12},{12,4},... | collective-permute-start | bytes 405512 | tf_op jit(solution)/shard_map/ppermute | solution.py:589
  32.6 8.8 %collective-permute-start.10 = (bf16[272,128]{1,0:T(8,128)(2,1)S(1)}, bf16[272,128]{1,0:T(8,128)(2,1)S(1)}, u32[]{:S(2)}, u32[]{:S(2)}) collective-permute-start(bf16[272,128]{1,0:T(8,128)(2,1)S(1)} %pack.1.own), channel_id=1, source_target_pairs={{0,4},{1,5},{2,6},{3,7},{4,0},{5,1},{6,2},{7,3},{8,14},{9,15},{10,... | collective-permute-start | bytes 208904 | tf_op jit(solution)/shard_map/ppermute | solution.py:603
  33.7 9.2 %collective-permute-start.11 = (bf16[272,128]{1,0:T(8,128)(2,1)S(1)}, bf16[272,128]{1,0:T(8,128)(2,1)S(1)}, u32[]{:S(2)}, u32[]{:S(2)}) collective-permute-start(bf16[272,128]{1,0:T(8,128)(2,1)S(1)} %pack.1.own), channel_id=1, source_target_pairs={{0,5},{1,4},{2,7},{3,6},{4,1},{5,0},{6,3},{7,2},{8,15},{9,14},{10,... | collective-permute-start | bytes 208904 | tf_op jit(solution)/shard_map/ppermute | solution.py:603
  35.5 7.4 %collective-permute-start.12 = (bf16[272,128]{1,0:T(8,128)(2,1)S(1)}, bf16[272,128]{1,0:T(8,128)(2,1)S(1)}, u32[]{:S(2)}, u32[]{:S(2)}) collective-permute-start(bf16[272,128]{1,0:T(8,128)(2,1)S(1)} %pack.1.own), channel_id=1, source_target_pairs={{0,1},{1,0},{2,3},{3,2},{4,5},{5,4},{6,7},{7,6},{8,10},{9,11},{10,... | collective-permute-start | bytes 208904 | tf_op jit(solution)/shard_map/ppermute | solution.py:603
  37.0 5.8 %collective-permute-start.13 = (bf16[272,128]{1,0:T(8,128)(2,1)S(1)}, bf16[272,128]{1,0:T(8,128)(2,1)S(1)}, u32[]{:S(2)}, u32[]{:S(2)}) collective-permute-start(bf16[272,128]{1,0:T(8,128)(2,1)S(1)} %pack.1.own), channel_id=1, source_target_pairs={{8,11},{9,10},{10,9},{11,8},{12,15},{13,14},{14,13},{15,12},{24,27... | collective-permute-start | bytes 208904 | tf_op jit(solution)/shard_map/ppermute | solution.py:603
  42.9 1.6 %collective-permute-start.14 = (bf16[4,272,128]{2,1,0:T(8,128)(2,1)S(1)}, bf16[4,272,128]{2,1,0:T(8,128)(2,1)S(1)}, u32[]{:S(2)}, u32[]{:S(2)}) collective-permute-start(bf16[4,272,128]{2,1,0:T(8,128)(2,1)S(1)} %stack.1.received), channel_id=1, source_target_pairs={{0,8},{8,0},{1,9},{9,1},{2,10},{10,2},{3,11},{11,3},{4,12},{12,4},... | collective-permute-start | bytes 835592 | tf_op jit(solution)/shard_map/ppermute | solution.py:607

commit v4 on v3

--- a/solution.py
+++ b/solution.py
@@ -137,14 +137,14 @@
 
 LANES = 128
 PROJ_ROWS = 256
-MASK_AT = 256
-COT_AT = 272
-MESSAGE = 336
+COT_AT = 256
+MESSAGE = 320
+DEAD = 32768.0
 SMALL_AT = 256
 PARTIAL = 264
 SENT = 272
-PEERS = ((4, 5, 1, 0), (6, 7, 2, 3))
-ORDER = (0, 4, 1, 5, 6, 2, 7, 3)
+PEERS = ((0, 6, 1, 5), (2, 4, 3, 7))
+ORDER = (0, 6, 1, 7, 2, 5, 3, 4)
 VMEM = pltpu.CompilerParams(vmem_limit_bytes=24 * 1024 * 1024)
 F32 = jnp.float32
 BF16 = jnp.bfloat16
@@ -172,29 +172,52 @@
 
 def prepare(*rest):
     sources = rest[:11]
-    mask, gain, shift, weight, cotangent, out_weight, hat, stats, present = rest[11:20]
-    messages = rest[20:-12]
+    gain, shift, weight, cotangent, out_weight, hat, stats, present = rest[11:19]
+    messages = rest[19:-13]
     count = len(messages)
-    alignment, mean, inverse, bias, residue, wide, packed, cot, turned, square, arrived, late = rest[-12:]
-    targets = (alignment, mean, inverse, bias, residue, mask, gain, shift, weight, cotangent)
+    alignment, mean, inverse, bias, residue, mask, wide, packed, cot, turned, square, arrived, late = rest[-13:]
+    targets = (alignment, mean, inverse, bias, residue, mask, gain, shift, weight)
+    first = pltpu.make_async_copy(sources[-2], cotangent, late.at[0])
+    first.start()
     copies = [pltpu.make_async_copy(f, t, arrived.at[i]) for i, (f, t) in enumerate(zip(sources, targets))]
     for copy in copies:
         copy.start()
-    last = pltpu.make_async_copy(sources[-1], out_weight, late)
+    last = pltpu.make_async_copy(sources[-1], out_weight, late.at[1])
     last.start()
-    for copy in copies:
-        copy.wait()
     col, row = lax.axis_index("col"), lax.axis_index("row")
     seqs, own, channels = alignment.shape
     total = cotangent.shape[1]
+    depth = Z // count
+    first.wait()
+
+    @pl.when(row == 0)
+    def _():
+        cot[...] = cotangent[...].astype(F32).reshape(own * total, Z)
+        for k, message in enumerate(messages):
+            peer = col ^ ORDER[k]
+            message[COT_AT:MESSAGE, :] = jnp.concatenate(
+                [cot[pl.ds(own * peer + j, own, stride=total), :] for j in range(own)], axis=0
+            ).astype(BF16)
+
+    @pl.when(row != 0)
+    def _():
+        for i in range(own // 2):
+            pair = jnp.concatenate([cotangent[i], cotangent[i + own // 2]], axis=0).astype(F32)
+            turned[i] = pair.T.astype(BF16)
+        for k, message in enumerate(messages):
+            at = pl.multiple_of((col ^ ORDER[k]) * depth, depth)
+            for i in range(own // 2):
+                message[COT_AT + i * depth : COT_AT + (i + 1) * depth, :] = turned[i, pl.ds(at, depth), :]
+
+    for copy in copies:
+        copy.wait()
     square[0:own, :seqs] = mean[...]
     square[own : 2 * own, :seqs] = inverse[...]
     square[2 * own : 3 * own, : 2 * P_SIZE] = jnp.broadcast_to(bias[...], (own, 2 * P_SIZE))
     square[3 * own : 4 * own, :total] = jnp.broadcast_to(residue[...].astype(F32), (own, total))
     stats[...] = square[...].T
-    own_rows = pl.ds(pl.multiple_of(col * own, own), own)
-    present[...] = jnp.broadcast_to(stats[own_rows, 3 * own : 3 * own + 1], (own, LANES))
-    live = mask[...].astype(F32) * present[:, :seqs]
+    present[...] = jnp.broadcast_to(stats[:total, 3 * own : 3 * own + 1], (total, LANES))
+    live = mask[...].astype(F32) * present[pl.ds(pl.multiple_of(col * own, own), own), :seqs]
     values = alignment[...].astype(F32)
     for h in range(2):
         wide[h] = values[:, :, h * LANES : (h + 1) * LANES].reshape(seqs * own, LANES)
@@ -205,51 +228,28 @@
         hat[r] = hatted
         normed = (hatted * gain[...] + shift[...]).astype(BF16)
         projected = dot_nt(weight[...], normed) + stats[: 2 * P_SIZE, 2 * own : 2 * own + 1]
-        projected = projected * live[r : r + 1]
+        projected = jnp.where(live[r : r + 1] > 0.0, projected, DEAD)
         packed[pl.ds(r, P_SIZE, stride=own), :] = jnp.concatenate(
             [projected[:P_SIZE], projected[P_SIZE:]], axis=1
         )
     shared = packed[...].astype(BF16)
-    depth = Z // count
     for message in messages:
         message[0:PROJ_ROWS, :] = shared
-
-    @pl.when(row == 0)
-    def _():
-        cot[...] = cotangent[...].astype(F32).reshape(own * total, Z)
-        for k, message in enumerate(messages):
-            peer = col ^ ORDER[k]
-            message[COT_AT:MESSAGE, :] = jnp.concatenate(
-                [cot[pl.ds(own * peer + j, own, stride=total), :] for j in range(own)], axis=0
-            ).astype(BF16)
-
-    @pl.when(row != 0)
-    def _():
-        for i in range(own // 2):
-            pair = jnp.concatenate([cotangent[i], cotangent[i + own // 2]], axis=0).astype(F32)
-            turned[i] = pair.T.astype(BF16)
-        for k, message in enumerate(messages):
-            at = pl.multiple_of((col ^ ORDER[k]) * depth, depth)
-            for i in range(own // 2):
-                message[COT_AT + i * depth : COT_AT + (i + 1) * depth, :] = turned[i, pl.ds(at, depth), :]
-
     last.wait()
 
 
-def add_masks(mask, present, mate, *rest):
-    messages = rest[len(rest) // 2 :]
-    here = present[...]
-    live = jnp.concatenate([mask[...], mate[...]], axis=1).astype(F32) * here
-    masks = jnp.concatenate([live, here], axis=0).astype(BF16)
-    for message in messages:
-        message[MASK_AT:COT_AT, :] = masks
-
-
 def collect(*rest):
-    messages, cots = rest[:-1], rest[-1]
+    messages, out = rest[:-2], rest[-2]
+    live = rest[-1]
     col = lax.axis_index("col")
+    count = len(messages)
+    own = live.shape[0] // count
     for k, message in enumerate(messages):
-        cots[col ^ ORDER[k]] = message[COT_AT:MESSAGE, :]
+        peer = col ^ ORDER[k]
+        out[peer] = message[COT_AT:MESSAGE, :]
+        here = message[0 : 2 * own, :].astype(F32)[:own]
+        live[pl.ds(pl.multiple_of(peer * own, own), own), :] = jnp.where(here < 0.5 * DEAD, 1.0, 0.0)
+    out[count] = live[...].astype(BF16)
 
 
 def interleave(product, target, group, at):
@@ -269,46 +269,25 @@
 
 
 BLOCK = 8
-
-
-def left_part(cotangent, out_weight, *rest):
-    messages = rest[:-11]
-    every, gathered, scale_own, scale_twice, live_out, left_grad, live_all, present_all, grad_own, outer, wide = rest[-11:]
+STEPS = 3
+
+
+def arrange(out_weight, *rest):
+    messages = rest[:-4]
+    every, gathered, by_second, wide = rest[-4:]
     col = lax.axis_index("col")
-    own, total = cotangent.shape[:2]
+    own = PROJ_ROWS // P_SIZE
+    total = own * len(messages)
+    wide[...] = out_weight[...].astype(F32)
     for k, message in enumerate(messages):
         at = pl.multiple_of((col ^ ORDER[k]) * own, own)
         block = message[0:PROJ_ROWS, :].astype(F32)
+        block = jnp.where(block < 0.5 * DEAD, block, 0.0)
         for q in range(P_SIZE):
             every[pl.ds(q * total + at, own), :] = block[q * own : (q + 1) * own]
-        masks = message[MASK_AT:COT_AT, :].astype(F32)
-        live_all[pl.ds(at, own), :] = masks[:own]
-        present_all[pl.ds(at, own), :] = masks[own:]
-    live = live_all[...].astype(BF16)
-    present = present_all[...].astype(BF16)
-    masks = messages[0][MASK_AT:COT_AT, :]
-    live_out[...] = masks[:own].astype(F32)
-
-    def scale_of(live_other, present_other):
-        counts = dot_nt(live, live_other)
-        return dot_nt(present, present_other) * (1.0 / LANES) / jnp.maximum(counts, 1.0)
-
-    scale_own[:, :own] = scale_of(masks[:own], masks[own:])
-    scale_twice[...] = scale_of(
-        jnp.concatenate([live, live], axis=0), jnp.concatenate([present, present], axis=0)
-    )
-    for i in range(own):
-        grad_own[i * total : (i + 1) * total, :] = (
-            cotangent[i].astype(F32) * scale_own[:, i : i + 1]
-        ).astype(BF16)
-    wide[...] = out_weight[...].astype(F32)
-    for a in range(0, P_SIZE, BLOCK):
-        by_second = jnp.concatenate(
-            [wide[pl.ds(q, P_SIZE, stride=P_SIZE), :] for q in range(a, a + BLOCK)], axis=0
-        ).astype(BF16)
-        interleave(dot_nt(by_second, grad_own[...]), outer, own, a)
+    for q in range(P_SIZE):
+        by_second[q * P_SIZE : (q + 1) * P_SIZE, :] = wide[pl.ds(q, P_SIZE, stride=P_SIZE), :].astype(BF16)
     gathered[...] = every[...].astype(BF16)
-    left_grad[...] = swap_halves(dot_nn(outer[...], gathered[...]))
 
 
 def quad_members(quad):
@@ -316,26 +295,59 @@
     return ((base, base + 4), (base + 1, base + 5))
 
 
+def take_turns(*tracks):
+    results = [None] * len(tracks)
+    going = set(range(len(tracks)))
+    while going:
+        for t, (track, steps) in enumerate(tracks):
+            for _ in range(steps):
+                if t in going:
+                    try:
+                        next(track)
+                    except StopIteration as end:
+                        results[t] = end.value
+                        going.discard(t)
+    return results
+
+
 def sums_part(
-    cots, mate, out_weight, every, gathered, scale_own, scale_twice, live, left_grad, hat, gain, shift, weight, normed_grads, keep, turned, grad_turned, grad_slice, outer, corner, mixed, square
+    pieces, mate, cotangent, by_second, present, out_weight, every, gathered, hat, gain, shift, weight, normed_grads, keep, turned, grad_own, grad_turned, grad_slice, outer, scales, corner, mixed, square
 ):
-    row = lax.axis_index("row")
-    count = cots.shape[0]
+    col, row = lax.axis_index("col"), lax.axis_index("row")
+    count = pieces.shape[0] - 1
     own, seqs, channels = hat.shape
     total = grad_turned.shape[0] // own
     depth = Z // count
     half = LANES // 2
     pairs = own // 2
     mine = row == 0
+    here = present[...].astype(BF16)
+    counts = sum(
+        dot_nt(m, jnp.concatenate([m, m], axis=0)) for m in (pieces[count], mate[count])
+    )
+    scales[...] = (
+        dot_nt(here, jnp.concatenate([here, here], axis=0))
+        * (1.0 / LANES)
+        / jnp.maximum(counts * 0.5, 1.0)
+    )
+    own_at = pl.ds(pl.multiple_of(col * own, own), own)
+    scale_own = dot_nt(here, present[own_at, :].astype(BF16)) * (1.0 / LANES)
+    counts_own = jnp.zeros((total, own), F32)
+    for m in (pieces, mate):
+        square[0:total, :] = m[count].astype(F32)
+        counts_own = counts_own + dot_nt(m[count], square[own_at, :].astype(BF16))
+    scale_own = scale_own / jnp.maximum(counts_own * 0.5, 1.0)
+    square[0:total, :] = pieces[count].astype(F32)
+    live = square[own_at, :]
     low = low_lanes((own, LANES))
     bias_acc = jnp.zeros((depth, LANES), F32)
     for c in range(count):
-        one, two = cots[c].astype(F32), mate[c].astype(F32)
+        one, two = pieces[c].astype(F32), mate[c].astype(F32)
         block = jnp.where(mine, one, two)
         for j in range(own):
             turned[j * total + c * own : j * total + (c + 1) * own, :] = block[j * own : (j + 1) * own]
         block = jnp.where(mine, two, one)
-        tile = scale_twice[c * own : (c + 1) * own, :]
+        tile = scales[c * own : (c + 1) * own, :]
         tile = jnp.where(low, tile, jnp.concatenate([tile[pairs:], tile[:pairs]], axis=0))
         for i in range(pairs):
             piece = block[i * depth : (i + 1) * depth] * tile[i : i + 1, :]
@@ -344,55 +356,73 @@
                 (c * 2 + i // 2) * depth : (c * 2 + i // 2 + 1) * depth,
                 i % 2 * LANES : (i % 2 + 1) * LANES,
             ] = piece.astype(BF16)
-    for j in range(own):
-        spot = slice(j * total, (j + 1) * total)
-        grad_turned[spot, :] = (turned[spot, :] * scale_own[:, j : j + 1]).astype(BF16)
-    for a in range(0, P_SIZE, BLOCK):
-        interleave(
-            dot_nt(out_weight[a * P_SIZE : (a + BLOCK) * P_SIZE, :], grad_turned[...]), outer, own, a
-        )
-    right_grad = dot_nn(outer[...], gathered[...])
-
-    input_acc = jnp.zeros((2 * P_SIZE, channels), F32)
-    proj_acc = jnp.zeros((2 * P_SIZE, seqs), F32)
-    gain_acc = jnp.zeros((1, channels), F32)
-    shift_acc = jnp.zeros((1, channels), F32)
-    for r in range(own):
-        hatted = hat[r]
-        normed = (hatted * gain[...] + shift[...]).astype(BF16)
-        spot = slice(r * P_SIZE, (r + 1) * P_SIZE)
-        proj_grad = jnp.concatenate([left_grad[spot, :seqs], right_grad[spot, :seqs]], axis=0)
-        proj_grad = proj_grad * live[r : r + 1, :seqs]
-        proj_acc = proj_acc + proj_grad
-        input_acc = input_acc + dot_nn(proj_grad.astype(BF16), normed)
-        normed_grad = dot_nn(proj_grad.T.astype(BF16), weight[...])
-        gain_acc = gain_acc + jnp.sum(normed_grad * hatted, axis=0, keepdims=True)
-        shift_acc = shift_acc + jnp.sum(normed_grad, axis=0, keepdims=True)
-        normed_grads[r] = normed_grad
+    for i in range(own):
+        rows = slice(i * total, (i + 1) * total)
+        grad_own[rows, :] = (cotangent[i].astype(F32) * scale_own[:, i : i + 1]).astype(BF16)
+        grad_turned[rows, :] = (turned[rows, :] * scale_own[:, i : i + 1]).astype(BF16)
+
+    def grads():
+        for a in range(0, P_SIZE, BLOCK):
+            rows = slice(a * P_SIZE, (a + BLOCK) * P_SIZE)
+            interleave(dot_nt(by_second[rows, :], grad_own[...]), outer.at[0], own, a)
+            yield
+        left_grad = swap_halves(dot_nn(outer[0], gathered[...]))
+        yield
+        for a in range(0, P_SIZE, BLOCK):
+            rows = slice(a * P_SIZE, (a + BLOCK) * P_SIZE)
+            interleave(dot_nt(out_weight[rows, :], grad_turned[...]), outer.at[1], own, a)
+            yield
+        right_grad = dot_nn(outer[1], gathered[...])
+        yield
+        input_acc = jnp.zeros((2 * P_SIZE, channels), F32)
+        proj_acc = jnp.zeros((2 * P_SIZE, seqs), F32)
+        gain_acc = jnp.zeros((1, channels), F32)
+        shift_acc = jnp.zeros((1, channels), F32)
+        for r in range(own):
+            hatted = hat[r]
+            normed = (hatted * gain[...] + shift[...]).astype(BF16)
+            spot = slice(r * P_SIZE, (r + 1) * P_SIZE)
+            proj_grad = jnp.concatenate([left_grad[spot, :seqs], right_grad[spot, :seqs]], axis=0)
+            proj_grad = proj_grad * live[r : r + 1, :seqs]
+            proj_acc = proj_acc + proj_grad
+            input_acc = input_acc + dot_nn(proj_grad.astype(BF16), normed)
+            normed_grad = dot_nn(proj_grad.T.astype(BF16), weight[...])
+            gain_acc = gain_acc + jnp.sum(normed_grad * hatted, axis=0, keepdims=True)
+            shift_acc = shift_acc + jnp.sum(normed_grad, axis=0, keepdims=True)
+            normed_grads[r] = normed_grad
+            yield
+        return (input_acc, proj_acc, gain_acc, shift_acc)
 
     quads = count * own // 4
-    low = low_lanes((total, LANES))
-    corner[...] = jnp.zeros_like(corner)
-    for q in range(P_SIZE):
-        block = every[q * total : (q + 1) * total, :]
-        here = jnp.where(low, 0.0, block)
-        moved = swap_halves(here).astype(BF16)
-        here = here.astype(BF16)
-        slot = q % corner.shape[0]
-        for at in range(4):
-            lanes = slice(at // 2 * LANES, (at // 2 + 1) * LANES)
-            corner[slot, at * total : (at + 1) * total, lanes] = here if at % 2 else moved
-        mixed[:, q * depth : (q + 1) * depth, :] = (
-            dot_nn(grad_slice[...], corner[slot]).astype(BF16).reshape(quads, depth, 4 * total)
-        )
-    low = low_lanes((P_SIZE, LANES))
-    weight_acc = jnp.zeros((P_SIZE * depth, P_SIZE), F32)
-    for quad in range(quads):
-        rhs = []
-        for pair in quad_members(quad):
-            one, two = (every[pl.ds(i, P_SIZE, stride=total), :] for i in pair)
-            rhs.append(jnp.where(low, one, swap_halves(two)))
-        weight_acc = weight_acc + dot_nt(mixed[quad], jnp.concatenate(rhs, axis=1).astype(BF16))
+
+    def slices():
+        low = low_lanes((total, LANES))
+        corner[...] = jnp.zeros_like(corner)
+        for q in range(P_SIZE):
+            block = every[q * total : (q + 1) * total, :]
+            here = jnp.where(low, 0.0, block)
+            moved = swap_halves(here).astype(BF16)
+            here = here.astype(BF16)
+            slot = q % corner.shape[0]
+            for at in range(4):
+                lanes = slice(at // 2 * LANES, (at // 2 + 1) * LANES)
+                corner[slot, at * total : (at + 1) * total, lanes] = here if at % 2 else moved
+            mixed[:, q * depth : (q + 1) * depth, :] = (
+                dot_nn(grad_slice[...], corner[slot]).astype(BF16).reshape(quads, depth, 4 * total)
+            )
+            yield
+        low = low_lanes((P_SIZE, LANES))
+        weight_acc = jnp.zeros((P_SIZE * depth, P_SIZE), F32)
+        for quad in range(quads):
+            rhs = []
+            for pair in quad_members(quad):
+                one, two = (every[pl.ds(i, P_SIZE, stride=total), :] for i in pair)
+                rhs.append(jnp.where(low, one, swap_halves(two)))
+            weight_acc = weight_acc + dot_nt(mixed[quad], jnp.concatenate(rhs, axis=1).astype(BF16))
+            yield
+        return weight_acc
+
+    (input_acc, proj_acc, gain_acc, shift_acc), weight_acc = take_turns((grads(), 1), (slices(), STEPS))
     group = P_SIZE * depth // 4
     weight_acc = jnp.concatenate([weight_acc[b * group : (b + 1) * group] for b in range(4)], axis=1)
 
@@ -510,16 +540,14 @@
     seqs, own, channels = alignment.shape
     total = pair_cotangent.shape[1]
     depth = Z // count
-    mask = sequence_mask.T
     turn = [(0, 1), (1, 0)]
-    mate = lax.ppermute(mask, "row", turn)
-    fetched = [alignment, norm_mean.T, norm_inverse.T, input_bias[None, :], residue_mask[None, :]]
-    passed = [mask, norm_gain[None, :], norm_shift[None, :], input_weight.T, pair_cotangent, output_weight]
+    fetched = [alignment, norm_mean.T, norm_inverse.T, input_bias[None, :], residue_mask[None, :], sequence_mask.T]
+    passed = [norm_gain[None, :], norm_shift[None, :], input_weight.T, pair_cotangent, output_weight]
     operands = [pltpu.with_memory_space_constraint(a, pltpu.HBM) for a in fetched + passed]
-    mask, gain, shift, weight, cotangent, out_weight, hat, stats, present, *messages = call(
+    gain, shift, weight, cotangent, out_weight, hat, stats, present, *messages = call(
         prepare,
         [shape(a.shape, a.dtype) for a in passed]
-        + [shape((own, seqs, channels), F32), shape((LANES, LANES), F32), shape((own, LANES), F32)]
+        + [shape((own, seqs, channels), F32), shape((LANES, LANES), F32), shape((total, LANES), F32)]
         + [shape((MESSAGE, LANES), BF16)] * count,
         [HBM_SPEC] * len(operands),
         operands,
@@ -530,57 +558,44 @@
             pltpu.VMEM((own * total, Z), F32),
             pltpu.VMEM((own // 2, Z, LANES), BF16),
             pltpu.VMEM((LANES, LANES), F32),
-            pltpu.SemaphoreType.DMA((len(operands) - 1,)),
-            pltpu.SemaphoreType.DMA,
+            pltpu.SemaphoreType.DMA((len(operands) - 2,)),
+            pltpu.SemaphoreType.DMA((2,)),
         ],
-    )
-    messages = call(
-        add_masks,
-        [shape((MESSAGE, LANES), BF16)] * count,
-        [VMEM_SPEC] * (3 + count),
-        [mask, present, mate, *messages],
-        aliases={3 + k: k for k in range(count)},
     )
     messages = [messages[0]] + [
         lax.ppermute(messages[k], "col", [(c, c ^ ORDER[k]) for c in range(count)]) for k in range(1, count)
     ]
-    (cots,) = call(
+    (pieces,) = call(
         collect,
-        [shape((count, MESSAGE - COT_AT, LANES), BF16)],
+        [shape((count + 1, total, LANES), BF16)],
         [VMEM_SPEC] * count,
         messages,
-    )
-    mate_cots = lax.ppermute(cots, "row", turn)
-    every, gathered, scale_own, scale_twice, live, left_grad = call(
-        left_part,
+        [pltpu.VMEM((total, LANES), F32)],
+    )
+    mate_pieces = lax.ppermute(pieces, "row", turn)
+    every, gathered, by_second = call(
+        arrange,
         [
             shape((P_SIZE * total, LANES), F32),
             shape((P_SIZE * total, LANES), BF16),
-            shape((total, LANES), F32),
-            shape((total, LANES), F32),
-            shape((own, LANES), F32),
-            shape((own * P_SIZE, LANES), F32),
+            shape((P_SIZE * P_SIZE, LANES), BF16),
         ],
-        [VMEM_SPEC] * (2 + count),
-        [cotangent, out_weight, *messages],
-        [
-            pltpu.VMEM((total, LANES), F32),
-            pltpu.VMEM((total, LANES), F32),
-            pltpu.VMEM((own * total, Z), BF16),
-            pltpu.VMEM((own * P_SIZE, P_SIZE * total), BF16),
-            pltpu.VMEM((P_SIZE * P_SIZE, LANES), F32),
-        ],
+        [VMEM_SPEC] * (1 + count),
+        [out_weight, *messages],
+        [pltpu.VMEM((P_SIZE * P_SIZE, LANES), F32)],
     )
     normed_grads, keep = call(
         sums_part,
         [shape((own, seqs, channels), F32), shape((PARTIAL, LANES), F32)],
-        [VMEM_SPEC] * 13,
-        [cots, mate_cots, out_weight, every, gathered, scale_own, scale_twice, live, left_grad, hat, gain, shift, weight],
+        [VMEM_SPEC] * 12,
+        [pieces, mate_pieces, cotangent, by_second, present, out_weight, every, gathered, hat, gain, shift, weight],
         [
             pltpu.VMEM((own * total, Z), F32),
             pltpu.VMEM((own * total, Z), BF16),
+            pltpu.VMEM((own * total, Z), BF16),
             pltpu.VMEM((count * own // 4 * depth, 2 * LANES), BF16),
-            pltpu.VMEM((own * P_SIZE, P_SIZE * total), BF16),
+            pltpu.VMEM((2, own * P_SIZE, P_SIZE * total), BF16),
+            pltpu.VMEM((total, LANES), F32),
             pltpu.VMEM((4, 4 * total, 2 * LANES), BF16),
             pltpu.VMEM((count * own // 4, P_SIZE * depth, 4 * seqs), BF16),
             pltpu.VMEM((LANES, LANES), F32),
@@ -594,7 +609,9 @@
         [normed_grads, hat, stats, gain],
         [pltpu.VMEM((2, seqs * own, LANES), F32)],
     )
-    (partial,) = call(pack, [shape((SENT, LANES), BF16)], [VMEM_SPEC] * 2, [keep, given])
+    (partial,) = call(
+        pack, [shape((SENT, LANES), BF16)], [VMEM_SPEC] * 2, [keep, given]
+    )
     parts = []
     for pair in zip(*PEERS):
         turns = [

time: 45.9 us -> 41.5 us (0.904)
  starting transfers between devices: 23.3 us -> 20.8 us
  waiting for transfers between devices: 11.8 us -> 9.92 us
    ppermute x7, starting transfers between devices: 16.9 us -> 13.7 us  [tiled(): lax.ppermute(messages[k], 'col', [(c, c ^ ORDER[k]) for c in range(count)])]
    ppermute x4, waiting for transfers between devices: 5.18 us -> 3.35 us  [tiled(): parts.append(lax.ppermute(partial, ('row', 'col'), turns))]
    ppermute x1, starting transfers between devices: 0.1 us -> 1.06 us  [tiled(): theirs = lax.ppermute(received, 'row', turn)]
    ppermute x7, waiting for transfers between devices: 5.37 us -> 4.59 us  [tiled(): lax.ppermute(messages[k], 'col', [(c, c ^ ORDER[k]) for c in range(count)])]
    ppermute x2 -> x1, waiting for transfers between devices: 0.01 us -> 0.76 us  [tiled(): mate_pieces = lax.ppermute(pieces, 'row', turn)]
    ppermute x4, starting transfers between devices: 5.1 us -> 5.83 us  [tiled(): parts.append(lax.ppermute(partial, ('row', 'col'), turns))]
    ppermute x2 -> x1, starting transfers between devices: 0.59 us -> 0.07 us  [tiled(): mate_pieces = lax.ppermute(pieces, 'row', turn)]
    pallas_call x9 -> x8, Pallas kernels: 10 us -> 9.89 us  [call(): pl.pallas_call(kernel, out_shape=outputs, in_specs=specs, out_specs=[VMEM...]
  transfers between devices with their start and end apart: 15 -> 14, of which waited for: 6 -> 8; matrix products, arithmetic and copies ran while one was open for 0% -> 0% of each run, Pallas kernels for 11% -> 5%
where the time goes in v4:
time: 41.5 us; the launch traced here: 41.3 us
  starting transfers between devices  20.8 us (50%)
  waiting for transfers between devices  9.92 us (24%)
  Pallas kernels  9.89 us (24%)
  between operations  0.69 us (2%)
    ppermute x7, starting transfers between devices, tiled(): lax.ppermute(messages[k], 'col', [(c, c ^ ORDER[k]) for c in range(count)])  13.7 us
    pallas_call x8, Pallas kernels, call(): pl.pallas_call(kernel, out_shape=outputs, in_specs=specs, out_specs=[VMEM...  9.89 us
    ppermute x4, starting transfers between devices, tiled(): parts.append(lax.ppermute(partial, ('row', 'col'), turns))  5.83 us
    ppermute x7, waiting for transfers between devices, tiled(): lax.ppermute(messages[k], 'col', [(c, c ^ ORDER[k]) for c in range(count)])  4.59 us
    ppermute x4, waiting for transfers between devices, tiled(): parts.append(lax.ppermute(partial, ('row', 'col'), turns))  3.35 us
    ppermute x1, waiting for transfers between devices, tiled(): given = lax.ppermute(keep, 'row', turn)  1.21 us
    ppermute x1, starting transfers between devices, tiled(): theirs = lax.ppermute(received, 'row', turn)  1.06 us
  transfers between devices with their start and end apart: 14, of which 8 were waited for; matrix products, arithmetic and copies ran while one was open for 0% of the time, Pallas kernels for 5%

profile of v4, /device:TPU:0, one launch (start us, length us, event | category | flops | bytes accessed | tf_op | source)
XLA Modules:
  0.0 41.3 jit_solution(14382256238124414568)
XLA Ops:
  0.6 2.1 %prepare.1 = (f32[1,256]{1,0:T(1,128)S(1)}, f32[1,256]{1,0:T(1,128)S(1)}, bf16[64,256]{1,0:T(8,128)(2,1)S(1)}, bf16[8,64,128]{2,1,0:T(8,128)(2,1)S(1)}, bf16[102...) custom-call(bf16[64,8,256]{2,1,0:T(8,128)(2,1)} %rest_0_.1, ...), custom_call_target="tpu_custom_call" | custom-call | tf_op jit(solution)/shard_map/prepare/pallas_call | solution.py:514
  2.7 5.1 %collective-permute-start = (bf16[320,128]{1,0:T(8,128)(2,1)S(1)}, bf16[320,128]{1,0:T(8,128)(2,1)S(1)}, u32[]{:S(2)}, u32[]{:S(2)}) collective-permute-start(bf16[320,128]{1,0:T(8,128)(2,1)S(1)} %get-tuple-element.35), channel_id=1, source_target_pairs={{0,6},{1,7},{2,4},{3,5},{4,2},{5,3},{6,0},{7,1},{8,14},{9,15},{10,... | collective-permute-start | bytes 245768 | tf_op jit(solution)/shard_map/ppermute | solution.py:566
  7.8 1.5 %collective-permute-start.1 = (bf16[320,128]{1,0:T(8,128)(2,1)S(1)}, bf16[320,128]{1,0:T(8,128)(2,1)S(1)}, u32[]{:S(2)}, u32[]{:S(2)}) collective-permute-start(bf16[320,128]{1,0:T(8,128)(2,1)S(1)} %get-tuple-element.36), channel_id=1, source_target_pairs={{0,1},{1,0},{2,3},{3,2},{4,5},{5,4},{6,7},{7,6},{8,9},{9,8},{10,11... | collective-permute-start | bytes 245768 | tf_op jit(solution)/shard_map/ppermute | solution.py:566
  9.3 0.0 collective-permute-start.2
  9.4 0.0 collective-permute-start.3
  9.4 5.3 %collective-permute-start.4 = (bf16[320,128]{1,0:T(8,128)(2,1)S(1)}, bf16[320,128]{1,0:T(8,128)(2,1)S(1)}, u32[]{:S(2)}, u32[]{:S(2)}) collective-permute-start(bf16[320,128]{1,0:T(8,128)(2,1)S(1)} %get-tuple-element.39), channel_id=1, source_target_pairs={{0,5},{1,4},{2,7},{3,6},{4,1},{5,0},{6,3},{7,2},{8,13},{9,12},{10,... | collective-permute-start | bytes 245768 | tf_op jit(solution)/shard_map/ppermute | solution.py:566
  14.6 0.0 collective-permute-done.rest_1_
  14.6 0.0 collective-permute-start.5
  14.6 0.0 collective-permute-done.1.rest_2_
  14.6 1.8 %collective-permute-start.6 = (bf16[320,128]{1,0:T(8,128)(2,1)S(1)}, bf16[320,128]{1,0:T(8,128)(2,1)S(1)}, u32[]{:S(2)}, u32[]{:S(2)}) collective-permute-start(bf16[320,128]{1,0:T(8,128)(2,1)S(1)} %get-tuple-element.41), channel_id=1, source_target_pairs={{0,4},{1,5},{2,6},{3,7},{4,0},{5,1},{6,2},{7,3},{8,12},{9,13},{10,... | collective-permute-start | bytes 245768 | tf_op jit(solution)/shard_map/ppermute | solution.py:566
  16.4 1.1 %collective-permute-done.2.rest_3_ = bf16[320,128]{1,0:T(8,128)(2,1)S(1)} collective-permute-done((bf16[320,128]{1,0:T(8,128)(2,1)S(1)}, bf16[320,128]{1,0:T(8,128)(2,1)S(1)}, u32[]{:S(2)}, u32[]{:S(2)}) %collective-permute-start.2) | collective-permute-done | bytes 81952 | tf_op jit(solution)/shard_map/ppermute | solution.py:566
  17.5 1.0 %collective-permute-done.3.rest_4_ = bf16[320,128]{1,0:T(8,128)(2,1)S(1)} collective-permute-done((bf16[320,128]{1,0:T(8,128)(2,1)S(1)}, bf16[320,128]{1,0:T(8,128)(2,1)S(1)}, u32[]{:S(2)}, u32[]{:S(2)}) %collective-permute-start.3) | collective-permute-done | bytes 81952 | tf_op jit(solution)/shard_map/ppermute | solution.py:566
  18.5 0.5 %collective-permute-done.4.rest_5_ = bf16[320,128]{1,0:T(8,128)(2,1)S(1)} collective-permute-done((bf16[320,128]{1,0:T(8,128)(2,1)S(1)}, bf16[320,128]{1,0:T(8,128)(2,1)S(1)}, u32[]{:S(2)}, u32[]{:S(2)}) %collective-permute-start.4) | collective-permute-done | bytes 81952 | tf_op jit(solution)/shard_map/ppermute | solution.py:566
  19.0 1.9 %collective-permute-done.5.rest_6_ = bf16[320,128]{1,0:T(8,128)(2,1)S(1)} collective-permute-done((bf16[320,128]{1,0:T(8,128)(2,1)S(1)}, bf16[320,128]{1,0:T(8,128)(2,1)S(1)}, u32[]{:S(2)}, u32[]{:S(2)}) %collective-permute-start.5) | collective-permute-done | bytes 81952 | tf_op jit(solution)/shard_map/ppermute | solution.py:566
  21.0 0.0 collective-permute-done.6.rest_7_
  21.0 0.1 collective-permute-start.7
  21.1 0.6 %arrange.1 = (f32[2048,128]{1,0:T(8,128)S(1)}, bf16[2048,128]{1,0:T(8,128)(2,1)S(1)}, bf16[1024,128]{1,0:T(8,128)(2,1)S(1)}) custom-call(bf16[1024,128]{1,0:T(8,128)(2,1)S(1)} %get-tuple-element.43.out_weight, bf16[320,128]{1,0:T(8,128)(2,1)S(1)} %get-tuple-element.34.rest_0_, bf16[320,128]{1,0:T(8,128)(2,1)S(1)} %collective-permute-done.rest_1_, ...), custom_call_target="tpu_custom_call" | custom-call | tf_op jit(solution)/shard_map/arrange/pallas_call | solution.py:514
  21.7 0.8 %collective-permute-done.7.mate = bf16[9,64,128]{2,1,0:T(8,128)(2,1)S(1)} collective-permute-done((bf16[9,64,128]{2,1,0:T(8,128)(2,1)S(1)}, bf16[9,64,128]{2,1,0:T(8,128)(2,1)S(1)}, u32[]{:S(2)}, u32[]{:S(2)}) %collective-permute-start.7) | collective-permute-done | bytes 147488 | tf_op jit(solution)/shard_map/ppermute | solution.py:575
  22.4 4.6 %sums_part.1 = (f32[8,64,256]{2,1,0:T(8,128)S(1)}, f32[264,128]{1,0:T(8,128)S(1)}) custom-call(bf16[9,64,128]{2,1,0:T(8,128)(2,1)S(1)} %collect.1.pieces, bf16[9,64,128]{2,1,0:T(8,128)(2,1)S(1)} %collective-permute-done.7.mate, bf16[8,64,128]{2,1,0:T(8,128)(2,1)S(1)} %get-tuple-element.42.cotangent, bf16[1024,128]{1,0:T(8,128)(2,1)S(1)} %get-tuple-element.44.by_second, ...), custom_call_target="tpu_custom_call" | custom-call | tf_op jit(solution)/shard_map/sums_part/pallas_call | solution.py:514
  27.1 0.2 collective-permute-start.8
  27.3 1.2 %collective-permute-done.8.given = f32[264,128]{1,0:T(8,128)S(1)} collective-permute-done((f32[264,128]{1,0:T(8,128)S(1)}, f32[264,128]{1,0:T(8,128)S(1)}, u32[]{:S(2)}, u32[]{:S(2)}) %collective-permute-start.8) | collective-permute-done | bytes 135200 | tf_op jit(solution)/shard_map/ppermute | solution.py:604
  28.5 2.1 %collective-permute-start.12 = (bf16[272,128]{1,0:T(8,128)(2,1)S(1)}, bf16[272,128]{1,0:T(8,128)(2,1)S(1)}, u32[]{:S(2)}, u32[]{:S(2)}) collective-permute-start(bf16[272,128]{1,0:T(8,128)(2,1)S(1)} %pack.1.own), channel_id=1, source_target_pairs={{0,5},{1,4},{2,7},{3,6},{4,1},{5,0},{6,3},{7,2},{8,15},{9,14},{10,... | collective-permute-start | bytes 208904 | tf_op jit(solution)/shard_map/ppermute | solution.py:620
  30.7 0.8 %collective-permute-start.11 = (bf16[272,128]{1,0:T(8,128)(2,1)S(1)}, bf16[272,128]{1,0:T(8,128)(2,1)S(1)}, u32[]{:S(2)}, u32[]{:S(2)}) collective-permute-start(bf16[272,128]{1,0:T(8,128)(2,1)S(1)} %pack.1.own), channel_id=1, source_target_pairs={{0,1},{1,0},{2,3},{3,2},{4,5},{5,4},{6,7},{7,6},{8,11},{9,10},{10,... | collective-permute-start | bytes 208904 | tf_op jit(solution)/shard_map/ppermute | solution.py:620
  31.4 2.3 %collective-permute-start.10 = (bf16[272,128]{1,0:T(8,128)(2,1)S(1)}, bf16[272,128]{1,0:T(8,128)(2,1)S(1)}, u32[]{:S(2)}, u32[]{:S(2)}) collective-permute-start(bf16[272,128]{1,0:T(8,128)(2,1)S(1)} %pack.1.own), channel_id=1, source_target_pairs={{0,6},{1,7},{2,4},{3,5},{4,2},{5,3},{6,0},{7,1},{8,12},{9,13},{10,... | collective-permute-start | bytes 208904 | tf_op jit(solution)/shard_map/ppermute | solution.py:620
  33.7 0.7 %collective-permute-start.9 = (bf16[272,128]{1,0:T(8,128)(2,1)S(1)}, bf16[272,128]{1,0:T(8,128)(2,1)S(1)}, u32[]{:S(2)}, u32[]{:S(2)}) collective-permute-start(bf16[272,128]{1,0:T(8,128)(2,1)S(1)} %pack.1.own), channel_id=1, source_target_pairs={{8,10},{9,11},{10,8},{11,9},{12,14},{13,15},{14,12},{15,13},{24,26... | collective-permute-start | bytes 208904 | tf_op jit(solution)/shard_map/ppermute | solution.py:620
  34.4 1.8 %collective-permute-done.12.rest_3_ = bf16[272,128]{1,0:T(8,128)(2,1)S(1)} collective-permute-done((bf16[272,128]{1,0:T(8,128)(2,1)S(1)}, bf16[272,128]{1,0:T(8,128)(2,1)S(1)}, u32[]{:S(2)}, u32[]{:S(2)}) %collective-permute-start.12) | collective-permute-done | bytes 69664 | tf_op jit(solution)/shard_map/ppermute | solution.py:620
  36.2 0.0 collective-permute-done.11.rest_2_
  36.2 1.5 %collective-permute-done.10.rest_1_ = bf16[272,128]{1,0:T(8,128)(2,1)S(1)} collective-permute-done((bf16[272,128]{1,0:T(8,128)(2,1)S(1)}, bf16[272,128]{1,0:T(8,128)(2,1)S(1)}, u32[]{:S(2)}, u32[]{:S(2)}) %collective-permute-start.10) | collective-permute-done | bytes 69664 | tf_op jit(solution)/shard_map/ppermute | solution.py:620
  37.7 0.0 collective-permute-done.9.rest_0_
  37.8 1.1 %collective-permute-start.13 = (bf16[4,272,128]{2,1,0:T(8,128)(2,1)S(1)}, bf16[4,272,128]{2,1,0:T(8,128)(2,1)S(1)}, u32[]{:S(2)}, u32[]{:S(2)}) collective-permute-start(bf16[4,272,128]{2,1,0:T(8,128)(2,1)S(1)} %stack.1.received), channel_id=1, source_target_pairs={{0,8},{8,0},{1,9},{9,1},{2,10},{10,2},{3,11},{11,3},{4,12},{12,4},... | collective-permute-start | bytes 835592 | tf_op jit(solution)/shard_map/ppermute | solution.py:624
  38.8 1.3 %activations.1 = bf16[64,8,256]{2,1,0:T(8,128)(2,1)} custom-call(f32[8,64,256]{2,1,0:T(8,128)S(1)} %get-tuple-element.52.normed_grads, f32[8,64,256]{2,1,0:T(8,128)S(1)} %get-tuple-element.48.hat, f32[128,128]{1,0:T(8,128)S(1)} %get-tuple-element.53.stats, f32[1,256]{1,0:T(1,128)S(1)} %get-tuple-element.49.gain), custom_call_target="tpu_custom_call" | custom-call | tf_op jit(solution)/shard_map/activations/pallas_call | solution.py:514
  40.1 0.0 collective-permute-done.13.mate
  40.1 1.2 %finish.1 = (f32[64,256]{1,0:T(8,128)}, f32[1,64]{1,0:T(1,128)}, f32[1024,128]{1,0:T(8,128)}, f32[1,128]{1,0:T(1,128)}, f32[1,256]{1,0:T(1,128)}, /*index=5*/f32[1,256]{1,0:T(1,128)}) custom-call(bf16[272,128]{1,0:T(8,128)(2,1)S(1)} %pack.1.own, bf16[4,272,128]{2,1,0:T(8,128)(2,1)S(1)} %stack.1.received, bf16[4,272,128]{2,1,0:T(8,128)(2,1)S(1)} %collective-permute-done.13.mate), custom_call_target="tpu_custom_call" | custom-call | tf_op jit(solution)/shard_map/finish/pallas_call | solution.py:514
  (3 shorter events, 0.1 us)
Async XLA Ops:
  2.7 11.9 %collective-permute-start = (bf16[320,128]{1,0:T(8,128)(2,1)S(1)}, bf16[320,128]{1,0:T(8,128)(2,1)S(1)}, u32[]{:S(2)}, u32[]{:S(2)}) collective-permute-start(bf16[320,128]{1,0:T(8,128)(2,1)S(1)} %get-tuple-element.35), channel_id=1, source_target_pairs={{0,6},{1,7},{2,4},{3,5},{4,2},{5,3},{6,0},{7,1},{8,14},{9,15},{10,... | collective-permute-start | bytes 245768 | tf_op jit(solution)/shard_map/ppermute | solution.py:566
  7.8 6.8 %collective-permute-start.1 = (bf16[320,128]{1,0:T(8,128)(2,1)S(1)}, bf16[320,128]{1,0:T(8,128)(2,1)S(1)}, u32[]{:S(2)}, u32[]{:S(2)}) collective-permute-start(bf16[320,128]{1,0:T(8,128)(2,1)S(1)} %get-tuple-element.36), channel_id=1, source_target_pairs={{0,1},{1,0},{2,3},{3,2},{4,5},{5,4},{6,7},{7,6},{8,9},{9,8},{10,11... | collective-permute-start | bytes 245768 | tf_op jit(solution)/shard_map/ppermute | solution.py:566
  9.3 8.1 %collective-permute-start.2 = (bf16[320,128]{1,0:T(8,128)(2,1)S(1)}, bf16[320,128]{1,0:T(8,128)(2,1)S(1)}, u32[]{:S(2)}, u32[]{:S(2)}) collective-permute-start(bf16[320,128]{1,0:T(8,128)(2,1)S(1)} %get-tuple-element.37), channel_id=1, source_target_pairs={{0,7},{1,6},{2,5},{3,4},{4,3},{5,2},{6,1},{7,0},{8,15},{9,14},{10,... | collective-permute-start | bytes 245768 | tf_op jit(solution)/shard_map/ppermute | solution.py:566
  9.4 9.1 %collective-permute-start.3 = (bf16[320,128]{1,0:T(8,128)(2,1)S(1)}, bf16[320,128]{1,0:T(8,128)(2,1)S(1)}, u32[]{:S(2)}, u32[]{:S(2)}) collective-permute-start(bf16[320,128]{1,0:T(8,128)(2,1)S(1)} %get-tuple-element.38), channel_id=1, source_target_pairs={{0,2},{1,3},{2,0},{3,1},{4,6},{5,7},{6,4},{7,5},{8,10},{9,11},{10,... | collective-permute-start | bytes 245768 | tf_op jit(solution)/shard_map/ppermute | solution.py:566
  9.4 9.7 %collective-permute-start.4 = (bf16[320,128]{1,0:T(8,128)(2,1)S(1)}, bf16[320,128]{1,0:T(8,128)(2,1)S(1)}, u32[]{:S(2)}, u32[]{:S(2)}) collective-permute-start(bf16[320,128]{1,0:T(8,128)(2,1)S(1)} %get-tuple-element.39), channel_id=1, source_target_pairs={{0,5},{1,4},{2,7},{3,6},{4,1},{5,0},{6,3},{7,2},{8,13},{9,12},{10,... | collective-permute-start | bytes 245768 | tf_op jit(solution)/shard_map/ppermute | solution.py:566
  14.6 6.3 %collective-permute-start.5 = (bf16[320,128]{1,0:T(8,128)(2,1)S(1)}, bf16[320,128]{1,0:T(8,128)(2,1)S(1)}, u32[]{:S(2)}, u32[]{:S(2)}) collective-permute-start(bf16[320,128]{1,0:T(8,128)(2,1)S(1)} %get-tuple-element.40), channel_id=1, source_target_pairs={{0,3},{1,2},{2,1},{3,0},{4,7},{5,6},{6,5},{7,4},{8,11},{9,10},{10,... | collective-permute-start | bytes 245768 | tf_op jit(solution)/shard_map/ppermute | solution.py:566
  14.6 6.3 %collective-permute-start.6 = (bf16[320,128]{1,0:T(8,128)(2,1)S(1)}, bf16[320,128]{1,0:T(8,128)(2,1)S(1)}, u32[]{:S(2)}, u32[]{:S(2)}) collective-permute-start(bf16[320,128]{1,0:T(8,128)(2,1)S(1)} %get-tuple-element.41), channel_id=1, source_target_pairs={{0,4},{1,5},{2,6},{3,7},{4,0},{5,1},{6,2},{7,3},{8,12},{9,13},{10,... | collective-permute-start | bytes 245768 | tf_op jit(solution)/shard_map/ppermute | solution.py:566
  21.0 1.4 %collective-permute-start.7 = (bf16[9,64,128]{2,1,0:T(8,128)(2,1)S(1)}, bf16[9,64,128]{2,1,0:T(8,128)(2,1)S(1)}, u32[]{:S(2)}, u32[]{:S(2)}) collective-permute-start(bf16[9,64,128]{2,1,0:T(8,128)(2,1)S(1)} %collect.1.pieces), channel_id=1, source_target_pairs={{0,8},{8,0},{1,9},{9,1},{2,10},{10,2},{3,11},{11,3},{4,12},{12,4},... | collective-permute-start | bytes 442376 | tf_op jit(solution)/shard_map/ppermute | solution.py:575
  27.1 1.4 %collective-permute-start.8 = (f32[264,128]{1,0:T(8,128)S(1)}, f32[264,128]{1,0:T(8,128)S(1)}, u32[]{:S(2)}, u32[]{:S(2)}) collective-permute-start(f32[264,128]{1,0:T(8,128)S(1)} %get-tuple-element.54.kept), channel_id=1, source_target_pairs={{0,8},{8,0},{1,9},{9,1},{2,10},{10,2},{3,11},{11,3},{4,12},{12,4},... | collective-permute-start | bytes 405512 | tf_op jit(solution)/shard_map/ppermute | solution.py:604
  28.5 7.7 %collective-permute-start.12 = (bf16[272,128]{1,0:T(8,128)(2,1)S(1)}, bf16[272,128]{1,0:T(8,128)(2,1)S(1)}, u32[]{:S(2)}, u32[]{:S(2)}) collective-permute-start(bf16[272,128]{1,0:T(8,128)(2,1)S(1)} %pack.1.own), channel_id=1, source_target_pairs={{0,5},{1,4},{2,7},{3,6},{4,1},{5,0},{6,3},{7,2},{8,15},{9,14},{10,... | collective-permute-start | bytes 208904 | tf_op jit(solution)/shard_map/ppermute | solution.py:620
  30.7 5.5 %collective-permute-start.11 = (bf16[272,128]{1,0:T(8,128)(2,1)S(1)}, bf16[272,128]{1,0:T(8,128)(2,1)S(1)}, u32[]{:S(2)}, u32[]{:S(2)}) collective-permute-start(bf16[272,128]{1,0:T(8,128)(2,1)S(1)} %pack.1.own), channel_id=1, source_target_pairs={{0,1},{1,0},{2,3},{3,2},{4,5},{5,4},{6,7},{7,6},{8,11},{9,10},{10,... | collective-permute-start | bytes 208904 | tf_op jit(solution)/shard_map/ppermute | solution.py:620
  31.4 6.3 %collective-permute-start.10 = (bf16[272,128]{1,0:T(8,128)(2,1)S(1)}, bf16[272,128]{1,0:T(8,128)(2,1)S(1)}, u32[]{:S(2)}, u32[]{:S(2)}) collective-permute-start(bf16[272,128]{1,0:T(8,128)(2,1)S(1)} %pack.1.own), channel_id=1, source_target_pairs={{0,6},{1,7},{2,4},{3,5},{4,2},{5,3},{6,0},{7,1},{8,12},{9,13},{10,... | collective-permute-start | bytes 208904 | tf_op jit(solution)/shard_map/ppermute | solution.py:620
  33.7 4.0 %collective-permute-start.9 = (bf16[272,128]{1,0:T(8,128)(2,1)S(1)}, bf16[272,128]{1,0:T(8,128)(2,1)S(1)}, u32[]{:S(2)}, u32[]{:S(2)}) collective-permute-start(bf16[272,128]{1,0:T(8,128)(2,1)S(1)} %pack.1.own), channel_id=1, source_target_pairs={{8,10},{9,11},{10,8},{11,9},{12,14},{13,15},{14,12},{15,13},{24,26... | collective-permute-start | bytes 208904 | tf_op jit(solution)/shard_map/ppermute | solution.py:620
  37.8 2.3 %collective-permute-start.13 = (bf16[4,272,128]{2,1,0:T(8,128)(2,1)S(1)}, bf16[4,272,128]{2,1,0:T(8,128)(2,1)S(1)}, u32[]{:S(2)}, u32[]{:S(2)}) collective-permute-start(bf16[4,272,128]{2,1,0:T(8,128)(2,1)S(1)} %stack.1.received), channel_id=1, source_target_pairs={{0,8},{8,0},{1,9},{9,1},{2,10},{10,2},{3,11},{11,3},{4,12},{12,4},... | collective-permute-start | bytes 835592 | tf_op jit(solution)/shard_map/ppermute | solution.py:624

commit v5 on v4

--- a/solution.py
+++ b/solution.py
@@ -195,8 +195,13 @@
         cot[...] = cotangent[...].astype(F32).reshape(own * total, Z)
         for k, message in enumerate(messages):
             peer = col ^ ORDER[k]
+            block = square.at[k % 2 * own * own : (k % 2 + 1) * own * own, :]
+            for i in range(own):
+                block[i * own : (i + 1) * own, :] = cot[
+                    pl.ds(pl.multiple_of(i * total + own * peer, own), own), :
+                ]
             message[COT_AT:MESSAGE, :] = jnp.concatenate(
-                [cot[pl.ds(own * peer + j, own, stride=total), :] for j in range(own)], axis=0
+                [block[pl.ds(j, own, stride=own), :] for j in range(own)], axis=0
             ).astype(BF16)
 
     @pl.when(row != 0)
@@ -311,7 +316,7 @@
 
 
 def sums_part(
-    pieces, mate, cotangent, by_second, present, out_weight, every, gathered, hat, gain, shift, weight, normed_grads, keep, turned, grad_own, grad_turned, grad_slice, outer, scales, corner, mixed, square
+    pieces, mate, cotangent, by_second, present, out_weight, every, gathered, hat, gain, shift, weight, normed_grads, keep, turned, grad_own, grad_turned, grad_slice, outer, scales, corner, mixed, lefts, square
 ):
     col, row = lax.axis_index("col"), lax.axis_index("row")
     count = pieces.shape[0] - 1
@@ -407,19 +412,26 @@
             for at in range(4):
                 lanes = slice(at // 2 * LANES, (at // 2 + 1) * LANES)
                 corner[slot, at * total : (at + 1) * total, lanes] = here if at % 2 else moved
-            mixed[:, q * depth : (q + 1) * depth, :] = (
-                dot_nn(grad_slice[...], corner[slot]).astype(BF16).reshape(quads, depth, 4 * total)
-            )
+            product = dot_nn(grad_slice[...], corner[slot]).astype(BF16)
+            for quad in range(quads):
+                mixed[q * depth : (q + 1) * depth, quad * 4 * total : (quad + 1) * 4 * total] = product[
+                    quad * depth : (quad + 1) * depth
+                ]
             yield
         low = low_lanes((P_SIZE, LANES))
-        weight_acc = jnp.zeros((P_SIZE * depth, P_SIZE), F32)
+        rhs = []
         for quad in range(quads):
-            rhs = []
             for pair in quad_members(quad):
                 one, two = (every[pl.ds(i, P_SIZE, stride=total), :] for i in pair)
-                rhs.append(jnp.where(low, one, swap_halves(two)))
-            weight_acc = weight_acc + dot_nt(mixed[quad], jnp.concatenate(rhs, axis=1).astype(BF16))
+                rhs.append(jnp.where(low, one, swap_halves(two)).astype(BF16))
+        lefts[...] = jnp.concatenate(rhs, axis=1)
+        yield
+        weight_acc = []
+        chunk = P_SIZE * depth // 2
+        for b in range(2):
+            weight_acc.append(dot_nt(mixed[b * chunk : (b + 1) * chunk, :], lefts[...]))
             yield
+        weight_acc = jnp.concatenate(weight_acc, axis=0)
         return weight_acc
 
     (input_acc, proj_acc, gain_acc, shift_acc), weight_acc = take_turns((grads(), 1), (slices(), STEPS))
@@ -597,7 +609,8 @@
             pltpu.VMEM((2, own * P_SIZE, P_SIZE * total), BF16),
             pltpu.VMEM((total, LANES), F32),
             pltpu.VMEM((4, 4 * total, 2 * LANES), BF16),
-            pltpu.VMEM((count * own // 4, P_SIZE * depth, 4 * seqs), BF16),
+            pltpu.VMEM((P_SIZE * depth, count * own * seqs), BF16),
+            pltpu.VMEM((P_SIZE, count * own * seqs), BF16),
             pltpu.VMEM((LANES, LANES), F32),
         ],
     )

time: 41.5 us -> 41.3 us (level)
  no operation moved by 1% of the time
where the time goes in v5:
time: 41.3 us; the launch traced here: 41.1 us
  starting transfers between devices  20.6 us (50%)
  waiting for transfers between devices  10.1 us (24%)
  Pallas kernels  9.7 us (23%)
  between operations  0.7 us (2%)
    ppermute x7, starting transfers between devices, tiled(): lax.ppermute(messages[k], 'col', [(c, c ^ ORDER[k]) for c in range(count)])  13.6 us
    pallas_call x8, Pallas kernels, call(): pl.pallas_call(kernel, out_shape=outputs, in_specs=specs, out_specs=[VMEM...  9.7 us
    ppermute x4, starting transfers between devices, tiled(): parts.append(lax.ppermute(partial, ('row', 'col'), turns))  5.86 us
    ppermute x7, waiting for transfers between devices, tiled(): lax.ppermute(messages[k], 'col', [(c, c ^ ORDER[k]) for c in range(count)])  4.72 us
    ppermute x4, waiting for transfers between devices, tiled(): parts.append(lax.ppermute(partial, ('row', 'col'), turns))  3.42 us
    ppermute x1, waiting for transfers between devices, tiled(): given = lax.ppermute(keep, 'row', turn)  1.21 us
    ppermute x1, starting transfers between devices, tiled(): theirs = lax.ppermute(received, 'row', turn)  0.85 us
  transfers between devices with their start and end apart: 14, of which 8 were waited for; matrix products, arithmetic and copies ran while one was open for 0% of the time, Pallas kernels for 5%

profile of v5, /device:TPU:0, one launch (start us, length us, event | category | flops | bytes accessed | tf_op | source)
XLA Modules:
  0.0 41.1 jit_solution(6401848690155472043)
XLA Ops:
  0.6 2.0 %prepare.1 = (f32[1,256]{1,0:T(1,128)S(1)}, f32[1,256]{1,0:T(1,128)S(1)}, bf16[64,256]{1,0:T(8,128)(2,1)S(1)}, bf16[8,64,128]{2,1,0:T(8,128)(2,1)S(1)}, bf16[102...) custom-call(bf16[64,8,256]{2,1,0:T(8,128)(2,1)} %rest_0_.1, ...), custom_call_target="tpu_custom_call" | custom-call | tf_op jit(solution)/shard_map/prepare/pallas_call | solution.py:526
  2.6 5.1 %collective-permute-start = (bf16[320,128]{1,0:T(8,128)(2,1)S(1)}, bf16[320,128]{1,0:T(8,128)(2,1)S(1)}, u32[]{:S(2)}, u32[]{:S(2)}) collective-permute-start(bf16[320,128]{1,0:T(8,128)(2,1)S(1)} %get-tuple-element.35), channel_id=1, source_target_pairs={{0,6},{1,7},{2,4},{3,5},{4,2},{5,3},{6,0},{7,1},{8,14},{9,15},{10,... | collective-permute-start | bytes 245768 | tf_op jit(solution)/shard_map/ppermute | solution.py:578
  7.8 1.5 %collective-permute-start.1 = (bf16[320,128]{1,0:T(8,128)(2,1)S(1)}, bf16[320,128]{1,0:T(8,128)(2,1)S(1)}, u32[]{:S(2)}, u32[]{:S(2)}) collective-permute-start(bf16[320,128]{1,0:T(8,128)(2,1)S(1)} %get-tuple-element.36), channel_id=1, source_target_pairs={{0,1},{1,0},{2,3},{3,2},{4,5},{5,4},{6,7},{7,6},{8,9},{9,8},{10,11... | collective-permute-start | bytes 245768 | tf_op jit(solution)/shard_map/ppermute | solution.py:578
  9.3 0.0 collective-permute-start.2
  9.3 0.0 collective-permute-start.3
  9.3 5.3 %collective-permute-start.4 = (bf16[320,128]{1,0:T(8,128)(2,1)S(1)}, bf16[320,128]{1,0:T(8,128)(2,1)S(1)}, u32[]{:S(2)}, u32[]{:S(2)}) collective-permute-start(bf16[320,128]{1,0:T(8,128)(2,1)S(1)} %get-tuple-element.39), channel_id=1, source_target_pairs={{0,5},{1,4},{2,7},{3,6},{4,1},{5,0},{6,3},{7,2},{8,13},{9,12},{10,... | collective-permute-start | bytes 245768 | tf_op jit(solution)/shard_map/ppermute | solution.py:578
  14.6 0.0 collective-permute-done.rest_1_
  14.6 0.0 collective-permute-start.5
  14.6 0.0 collective-permute-done.1.rest_2_
  14.6 1.7 %collective-permute-start.6 = (bf16[320,128]{1,0:T(8,128)(2,1)S(1)}, bf16[320,128]{1,0:T(8,128)(2,1)S(1)}, u32[]{:S(2)}, u32[]{:S(2)}) collective-permute-start(bf16[320,128]{1,0:T(8,128)(2,1)S(1)} %get-tuple-element.41), channel_id=1, source_target_pairs={{0,4},{1,5},{2,6},{3,7},{4,0},{5,1},{6,2},{7,3},{8,12},{9,13},{10,... | collective-permute-start | bytes 245768 | tf_op jit(solution)/shard_map/ppermute | solution.py:578
  16.2 1.2 %collective-permute-done.2.rest_3_ = bf16[320,128]{1,0:T(8,128)(2,1)S(1)} collective-permute-done((bf16[320,128]{1,0:T(8,128)(2,1)S(1)}, bf16[320,128]{1,0:T(8,128)(2,1)S(1)}, u32[]{:S(2)}, u32[]{:S(2)}) %collective-permute-start.2) | collective-permute-done | bytes 81952 | tf_op jit(solution)/shard_map/ppermute | solution.py:578
  17.5 1.0 %collective-permute-done.3.rest_4_ = bf16[320,128]{1,0:T(8,128)(2,1)S(1)} collective-permute-done((bf16[320,128]{1,0:T(8,128)(2,1)S(1)}, bf16[320,128]{1,0:T(8,128)(2,1)S(1)}, u32[]{:S(2)}, u32[]{:S(2)}) %collective-permute-start.3) | collective-permute-done | bytes 81952 | tf_op jit(solution)/shard_map/ppermute | solution.py:578
  18.4 0.6 %collective-permute-done.4.rest_5_ = bf16[320,128]{1,0:T(8,128)(2,1)S(1)} collective-permute-done((bf16[320,128]{1,0:T(8,128)(2,1)S(1)}, bf16[320,128]{1,0:T(8,128)(2,1)S(1)}, u32[]{:S(2)}, u32[]{:S(2)}) %collective-permute-start.4) | collective-permute-done | bytes 81952 | tf_op jit(solution)/shard_map/ppermute | solution.py:578
  19.1 1.9 %collective-permute-done.5.rest_6_ = bf16[320,128]{1,0:T(8,128)(2,1)S(1)} collective-permute-done((bf16[320,128]{1,0:T(8,128)(2,1)S(1)}, bf16[320,128]{1,0:T(8,128)(2,1)S(1)}, u32[]{:S(2)}, u32[]{:S(2)}) %collective-permute-start.5) | collective-permute-done | bytes 81952 | tf_op jit(solution)/shard_map/ppermute | solution.py:578
  21.0 0.0 collective-permute-done.6.rest_7_
  21.0 0.1 collective-permute-start.7
  21.1 0.6 %arrange.1 = (f32[2048,128]{1,0:T(8,128)S(1)}, bf16[2048,128]{1,0:T(8,128)(2,1)S(1)}, bf16[1024,128]{1,0:T(8,128)(2,1)S(1)}) custom-call(bf16[1024,128]{1,0:T(8,128)(2,1)S(1)} %get-tuple-element.43.out_weight, bf16[320,128]{1,0:T(8,128)(2,1)S(1)} %get-tuple-element.34.rest_0_, bf16[320,128]{1,0:T(8,128)(2,1)S(1)} %collective-permute-done.rest_1_, ...), custom_call_target="tpu_custom_call" | custom-call | tf_op jit(solution)/shard_map/arrange/pallas_call | solution.py:526
  21.7 0.8 %collective-permute-done.7.mate = bf16[9,64,128]{2,1,0:T(8,128)(2,1)S(1)} collective-permute-done((bf16[9,64,128]{2,1,0:T(8,128)(2,1)S(1)}, bf16[9,64,128]{2,1,0:T(8,128)(2,1)S(1)}, u32[]{:S(2)}, u32[]{:S(2)}) %collective-permute-start.7) | collective-permute-done | bytes 147488 | tf_op jit(solution)/shard_map/ppermute | solution.py:587
  22.4 4.5 %sums_part.1 = (f32[8,64,256]{2,1,0:T(8,128)S(1)}, f32[264,128]{1,0:T(8,128)S(1)}) custom-call(bf16[9,64,128]{2,1,0:T(8,128)(2,1)S(1)} %collect.1.pieces, bf16[9,64,128]{2,1,0:T(8,128)(2,1)S(1)} %collective-permute-done.7.mate, bf16[8,64,128]{2,1,0:T(8,128)(2,1)S(1)} %get-tuple-element.42.cotangent, bf16[1024,128]{1,0:T(8,128)(2,1)S(1)} %get-tuple-element.44.by_second, ...), custom_call_target="tpu_custom_call" | custom-call | tf_op jit(solution)/shard_map/sums_part/pallas_call | solution.py:526
  27.0 0.2 collective-permute-start.8
  27.2 1.2 %collective-permute-done.8.given = f32[264,128]{1,0:T(8,128)S(1)} collective-permute-done((f32[264,128]{1,0:T(8,128)S(1)}, f32[264,128]{1,0:T(8,128)S(1)}, u32[]{:S(2)}, u32[]{:S(2)}) %collective-permute-start.8) | collective-permute-done | bytes 135200 | tf_op jit(solution)/shard_map/ppermute | solution.py:617
  28.4 2.1 %collective-permute-start.12 = (bf16[272,128]{1,0:T(8,128)(2,1)S(1)}, bf16[272,128]{1,0:T(8,128)(2,1)S(1)}, u32[]{:S(2)}, u32[]{:S(2)}) collective-permute-start(bf16[272,128]{1,0:T(8,128)(2,1)S(1)} %pack.1.own), channel_id=1, source_target_pairs={{0,5},{1,4},{2,7},{3,6},{4,1},{5,0},{6,3},{7,2},{8,15},{9,14},{10,... | collective-permute-start | bytes 208904 | tf_op jit(solution)/shard_map/ppermute | solution.py:633
  30.5 0.8 %collective-permute-start.11 = (bf16[272,128]{1,0:T(8,128)(2,1)S(1)}, bf16[272,128]{1,0:T(8,128)(2,1)S(1)}, u32[]{:S(2)}, u32[]{:S(2)}) collective-permute-start(bf16[272,128]{1,0:T(8,128)(2,1)S(1)} %pack.1.own), channel_id=1, source_target_pairs={{0,1},{1,0},{2,3},{3,2},{4,5},{5,4},{6,7},{7,6},{8,11},{9,10},{10,... | collective-permute-start | bytes 208904 | tf_op jit(solution)/shard_map/ppermute | solution.py:633
  31.3 2.3 %collective-permute-start.10 = (bf16[272,128]{1,0:T(8,128)(2,1)S(1)}, bf16[272,128]{1,0:T(8,128)(2,1)S(1)}, u32[]{:S(2)}, u32[]{:S(2)}) collective-permute-start(bf16[272,128]{1,0:T(8,128)(2,1)S(1)} %pack.1.own), channel_id=1, source_target_pairs={{0,6},{1,7},{2,4},{3,5},{4,2},{5,3},{6,0},{7,1},{8,12},{9,13},{10,... | collective-permute-start | bytes 208904 | tf_op jit(solution)/shard_map/ppermute | solution.py:633
  33.6 0.7 %collective-permute-start.9 = (bf16[272,128]{1,0:T(8,128)(2,1)S(1)}, bf16[272,128]{1,0:T(8,128)(2,1)S(1)}, u32[]{:S(2)}, u32[]{:S(2)}) collective-permute-start(bf16[272,128]{1,0:T(8,128)(2,1)S(1)} %pack.1.own), channel_id=1, source_target_pairs={{8,10},{9,11},{10,8},{11,9},{12,14},{13,15},{14,12},{15,13},{24,26... | collective-permute-start | bytes 208904 | tf_op jit(solution)/shard_map/ppermute | solution.py:633
  34.3 1.8 %collective-permute-done.12.rest_3_ = bf16[272,128]{1,0:T(8,128)(2,1)S(1)} collective-permute-done((bf16[272,128]{1,0:T(8,128)(2,1)S(1)}, bf16[272,128]{1,0:T(8,128)(2,1)S(1)}, u32[]{:S(2)}, u32[]{:S(2)}) %collective-permute-start.12) | collective-permute-done | bytes 69664 | tf_op jit(solution)/shard_map/ppermute | solution.py:633
  36.1 0.0 collective-permute-done.11.rest_2_
  36.1 1.6 %collective-permute-done.10.rest_1_ = bf16[272,128]{1,0:T(8,128)(2,1)S(1)} collective-permute-done((bf16[272,128]{1,0:T(8,128)(2,1)S(1)}, bf16[272,128]{1,0:T(8,128)(2,1)S(1)}, u32[]{:S(2)}, u32[]{:S(2)}) %collective-permute-start.10) | collective-permute-done | bytes 69664 | tf_op jit(solution)/shard_map/ppermute | solution.py:633
  37.7 0.0 collective-permute-done.9.rest_0_
  37.7 0.8 %collective-permute-start.13 = (bf16[4,272,128]{2,1,0:T(8,128)(2,1)S(1)}, bf16[4,272,128]{2,1,0:T(8,128)(2,1)S(1)}, u32[]{:S(2)}, u32[]{:S(2)}) collective-permute-start(bf16[4,272,128]{2,1,0:T(8,128)(2,1)S(1)} %stack.1.received), channel_id=1, source_target_pairs={{0,8},{8,0},{1,9},{9,1},{2,10},{10,2},{3,11},{11,3},{4,12},{12,4},... | collective-permute-start | bytes 835592 | tf_op jit(solution)/shard_map/ppermute | solution.py:637
  38.6 1.3 %activations.1 = bf16[64,8,256]{2,1,0:T(8,128)(2,1)} custom-call(f32[8,64,256]{2,1,0:T(8,128)S(1)} %get-tuple-element.52.normed_grads, f32[8,64,256]{2,1,0:T(8,128)S(1)} %get-tuple-element.48.hat, f32[128,128]{1,0:T(8,128)S(1)} %get-tuple-element.53.stats, f32[1,256]{1,0:T(1,128)S(1)} %get-tuple-element.49.gain), custom_call_target="tpu_custom_call" | custom-call | tf_op jit(solution)/shard_map/activations/pallas_call | solution.py:526
  39.9 0.0 collective-permute-done.13.mate
  39.9 1.2 %finish.1 = (f32[64,256]{1,0:T(8,128)}, f32[1,64]{1,0:T(1,128)}, f32[1024,128]{1,0:T(8,128)}, f32[1,128]{1,0:T(1,128)}, f32[1,256]{1,0:T(1,128)}, /*index=5*/f32[1,256]{1,0:T(1,128)}) custom-call(bf16[272,128]{1,0:T(8,128)(2,1)S(1)} %pack.1.own, bf16[4,272,128]{2,1,0:T(8,128)(2,1)S(1)} %stack.1.received, bf16[4,272,128]{2,1,0:T(8,128)(2,1)S(1)} %collective-permute-done.13.mate), custom_call_target="tpu_custom_call" | custom-call | tf_op jit(solution)/shard_map/finish/pallas_call | solution.py:526
  (3 shorter events, 0.1 us)
Async XLA Ops:
  2.6 11.9 %collective-permute-start = (bf16[320,128]{1,0:T(8,128)(2,1)S(1)}, bf16[320,128]{1,0:T(8,128)(2,1)S(1)}, u32[]{:S(2)}, u32[]{:S(2)}) collective-permute-start(bf16[320,128]{1,0:T(8,128)(2,1)S(1)} %get-tuple-element.35), channel_id=1, source_target_pairs={{0,6},{1,7},{2,4},{3,5},{4,2},{5,3},{6,0},{7,1},{8,14},{9,15},{10,... | collective-permute-start | bytes 245768 | tf_op jit(solution)/shard_map/ppermute | solution.py:578
  7.8 6.8 %collective-permute-start.1 = (bf16[320,128]{1,0:T(8,128)(2,1)S(1)}, bf16[320,128]{1,0:T(8,128)(2,1)S(1)}, u32[]{:S(2)}, u32[]{:S(2)}) collective-permute-start(bf16[320,128]{1,0:T(8,128)(2,1)S(1)} %get-tuple-element.36), channel_id=1, source_target_pairs={{0,1},{1,0},{2,3},{3,2},{4,5},{5,4},{6,7},{7,6},{8,9},{9,8},{10,11... | collective-permute-start | bytes 245768 | tf_op jit(solution)/shard_map/ppermute | solution.py:578
  9.3 8.2 %collective-permute-start.2 = (bf16[320,128]{1,0:T(8,128)(2,1)S(1)}, bf16[320,128]{1,0:T(8,128)(2,1)S(1)}, u32[]{:S(2)}, u32[]{:S(2)}) collective-permute-start(bf16[320,128]{1,0:T(8,128)(2,1)S(1)} %get-tuple-element.37), channel_id=1, source_target_pairs={{0,7},{1,6},{2,5},{3,4},{4,3},{5,2},{6,1},{7,0},{8,15},{9,14},{10,... | collective-permute-start | bytes 245768 | tf_op jit(solution)/shard_map/ppermute | solution.py:578
  9.3 9.1 %collective-permute-start.3 = (bf16[320,128]{1,0:T(8,128)(2,1)S(1)}, bf16[320,128]{1,0:T(8,128)(2,1)S(1)}, u32[]{:S(2)}, u32[]{:S(2)}) collective-permute-start(bf16[320,128]{1,0:T(8,128)(2,1)S(1)} %get-tuple-element.38), channel_id=1, source_target_pairs={{0,2},{1,3},{2,0},{3,1},{4,6},{5,7},{6,4},{7,5},{8,10},{9,11},{10,... | collective-permute-start | bytes 245768 | tf_op jit(solution)/shard_map/ppermute | solution.py:578
  9.3 9.8 %collective-permute-start.4 = (bf16[320,128]{1,0:T(8,128)(2,1)S(1)}, bf16[320,128]{1,0:T(8,128)(2,1)S(1)}, u32[]{:S(2)}, u32[]{:S(2)}) collective-permute-start(bf16[320,128]{1,0:T(8,128)(2,1)S(1)} %get-tuple-element.39), channel_id=1, source_target_pairs={{0,5},{1,4},{2,7},{3,6},{4,1},{5,0},{6,3},{7,2},{8,13},{9,12},{10,... | collective-permute-start | bytes 245768 | tf_op jit(solution)/shard_map/ppermute | solution.py:578
  14.6 6.4 %collective-permute-start.5 = (bf16[320,128]{1,0:T(8,128)(2,1)S(1)}, bf16[320,128]{1,0:T(8,128)(2,1)S(1)}, u32[]{:S(2)}, u32[]{:S(2)}) collective-permute-start(bf16[320,128]{1,0:T(8,128)(2,1)S(1)} %get-tuple-element.40), channel_id=1, source_target_pairs={{0,3},{1,2},{2,1},{3,0},{4,7},{5,6},{6,5},{7,4},{8,11},{9,10},{10,... | collective-permute-start | bytes 245768 | tf_op jit(solution)/shard_map/ppermute | solution.py:578
  14.6 6.4 %collective-permute-start.6 = (bf16[320,128]{1,0:T(8,128)(2,1)S(1)}, bf16[320,128]{1,0:T(8,128)(2,1)S(1)}, u32[]{:S(2)}, u32[]{:S(2)}) collective-permute-start(bf16[320,128]{1,0:T(8,128)(2,1)S(1)} %get-tuple-element.41), channel_id=1, source_target_pairs={{0,4},{1,5},{2,6},{3,7},{4,0},{5,1},{6,2},{7,3},{8,12},{9,13},{10,... | collective-permute-start | bytes 245768 | tf_op jit(solution)/shard_map/ppermute | solution.py:578
  21.0 1.4 %collective-permute-start.7 = (bf16[9,64,128]{2,1,0:T(8,128)(2,1)S(1)}, bf16[9,64,128]{2,1,0:T(8,128)(2,1)S(1)}, u32[]{:S(2)}, u32[]{:S(2)}) collective-permute-start(bf16[9,64,128]{2,1,0:T(8,128)(2,1)S(1)} %collect.1.pieces), channel_id=1, source_target_pairs={{0,8},{8,0},{1,9},{9,1},{2,10},{10,2},{3,11},{11,3},{4,12},{12,4},... | collective-permute-start | bytes 442376 | tf_op jit(solution)/shard_map/ppermute | solution.py:587
  27.0 1.4 %collective-permute-start.8 = (f32[264,128]{1,0:T(8,128)S(1)}, f32[264,128]{1,0:T(8,128)S(1)}, u32[]{:S(2)}, u32[]{:S(2)}) collective-permute-start(f32[264,128]{1,0:T(8,128)S(1)} %get-tuple-element.54.kept), channel_id=1, source_target_pairs={{0,8},{8,0},{1,9},{9,1},{2,10},{10,2},{3,11},{11,3},{4,12},{12,4},... | collective-permute-start | bytes 405512 | tf_op jit(solution)/shard_map/ppermute | solution.py:617
  28.4 7.7 %collective-permute-start.12 = (bf16[272,128]{1,0:T(8,128)(2,1)S(1)}, bf16[272,128]{1,0:T(8,128)(2,1)S(1)}, u32[]{:S(2)}, u32[]{:S(2)}) collective-permute-start(bf16[272,128]{1,0:T(8,128)(2,1)S(1)} %pack.1.own), channel_id=1, source_target_pairs={{0,5},{1,4},{2,7},{3,6},{4,1},{5,0},{6,3},{7,2},{8,15},{9,14},{10,... | collective-permute-start | bytes 208904 | tf_op jit(solution)/shard_map/ppermute | solution.py:633
  30.5 5.6 %collective-permute-start.11 = (bf16[272,128]{1,0:T(8,128)(2,1)S(1)}, bf16[272,128]{1,0:T(8,128)(2,1)S(1)}, u32[]{:S(2)}, u32[]{:S(2)}) collective-permute-start(bf16[272,128]{1,0:T(8,128)(2,1)S(1)} %pack.1.own), channel_id=1, source_target_pairs={{0,1},{1,0},{2,3},{3,2},{4,5},{5,4},{6,7},{7,6},{8,11},{9,10},{10,... | collective-permute-start | bytes 208904 | tf_op jit(solution)/shard_map/ppermute | solution.py:633
  31.3 6.4 %collective-permute-start.10 = (bf16[272,128]{1,0:T(8,128)(2,1)S(1)}, bf16[272,128]{1,0:T(8,128)(2,1)S(1)}, u32[]{:S(2)}, u32[]{:S(2)}) collective-permute-start(bf16[272,128]{1,0:T(8,128)(2,1)S(1)} %pack.1.own), channel_id=1, source_target_pairs={{0,6},{1,7},{2,4},{3,5},{4,2},{5,3},{6,0},{7,1},{8,12},{9,13},{10,... | collective-permute-start | bytes 208904 | tf_op jit(solution)/shard_map/ppermute | solution.py:633
  33.6 4.1 %collective-permute-start.9 = (bf16[272,128]{1,0:T(8,128)(2,1)S(1)}, bf16[272,128]{1,0:T(8,128)(2,1)S(1)}, u32[]{:S(2)}, u32[]{:S(2)}) collective-permute-start(bf16[272,128]{1,0:T(8,128)(2,1)S(1)} %pack.1.own), channel_id=1, source_target_pairs={{8,10},{9,11},{10,8},{11,9},{12,14},{13,15},{14,12},{15,13},{24,26... | collective-permute-start | bytes 208904 | tf_op jit(solution)/shard_map/ppermute | solution.py:633
  37.7 2.1 %collective-permute-start.13 = (bf16[4,272,128]{2,1,0:T(8,128)(2,1)S(1)}, bf16[4,272,128]{2,1,0:T(8,128)(2,1)S(1)}, u32[]{:S(2)}, u32[]{:S(2)}) collective-permute-start(bf16[4,272,128]{2,1,0:T(8,128)(2,1)S(1)} %stack.1.received), channel_id=1, source_target_pairs={{0,8},{8,0},{1,9},{9,1},{2,10},{10,2},{3,11},{11,3},{4,12},{12,4},... | collective-permute-start | bytes 835592 | tf_op jit(solution)/shard_map/ppermute | solution.py:637

commit v6 on v5

--- a/solution.py
+++ b/solution.py
@@ -188,32 +188,6 @@
     seqs, own, channels = alignment.shape
     total = cotangent.shape[1]
     depth = Z // count
-    first.wait()
-
-    @pl.when(row == 0)
-    def _():
-        cot[...] = cotangent[...].astype(F32).reshape(own * total, Z)
-        for k, message in enumerate(messages):
-            peer = col ^ ORDER[k]
-            block = square.at[k % 2 * own * own : (k % 2 + 1) * own * own, :]
-            for i in range(own):
-                block[i * own : (i + 1) * own, :] = cot[
-                    pl.ds(pl.multiple_of(i * total + own * peer, own), own), :
-                ]
-            message[COT_AT:MESSAGE, :] = jnp.concatenate(
-                [block[pl.ds(j, own, stride=own), :] for j in range(own)], axis=0
-            ).astype(BF16)
-
-    @pl.when(row != 0)
-    def _():
-        for i in range(own // 2):
-            pair = jnp.concatenate([cotangent[i], cotangent[i + own // 2]], axis=0).astype(F32)
-            turned[i] = pair.T.astype(BF16)
-        for k, message in enumerate(messages):
-            at = pl.multiple_of((col ^ ORDER[k]) * depth, depth)
-            for i in range(own // 2):
-                message[COT_AT + i * depth : COT_AT + (i + 1) * depth, :] = turned[i, pl.ds(at, depth), :]
-
     for copy in copies:
         copy.wait()
     square[0:own, :seqs] = mean[...]
@@ -240,6 +214,32 @@
     shared = packed[...].astype(BF16)
     for message in messages:
         message[0:PROJ_ROWS, :] = shared
+    first.wait()
+
+    @pl.when(row == 0)
+    def _():
+        cot[...] = cotangent[...].astype(F32).reshape(own * total, Z)
+        for k, message in enumerate(messages):
+            peer = col ^ ORDER[k]
+            block = square.at[k % 2 * own * own : (k % 2 + 1) * own * own, :]
+            for i in range(own):
+                block[i * own : (i + 1) * own, :] = cot[
+                    pl.ds(pl.multiple_of(i * total + own * peer, own), own), :
+                ]
+            message[COT_AT:MESSAGE, :] = jnp.concatenate(
+                [block[pl.ds(j, own, stride=own), :] for j in range(own)], axis=0
+            ).astype(BF16)
+
+    @pl.when(row != 0)
+    def _():
+        for i in range(own // 2):
+            pair = jnp.concatenate([cotangent[i], cotangent[i + own // 2]], axis=0).astype(F32)
+            turned[i] = pair.T.astype(BF16)
+        for k, message in enumerate(messages):
+            at = pl.multiple_of((col ^ ORDER[k]) * depth, depth)
+            for i in range(own // 2):
+                message[COT_AT + i * depth : COT_AT + (i + 1) * depth, :] = turned[i, pl.ds(at, depth), :]
+
     last.wait()
 
 
@@ -631,6 +631,7 @@
             (row * count + c, row * count + (c ^ pair[row])) for row in range(2) if pair[row] for c in range(count)
         ]
         parts.append(lax.ppermute(partial, ("row", "col"), turns))
+    parts[-1], activation = lax.optimization_barrier((parts[-1], activation))
     (received,) = call(
         stack, [shape((len(parts), SENT, LANES), BF16)], [VMEM_SPEC] * len(parts), parts
     )

time: 41.3 us -> 41.1 us (level)
    ppermute x4, waiting for transfers between devices: 3.42 us -> 2.14 us  [tiled(): parts.append(lax.ppermute(partial, ('row', 'col'), turns))]
    ppermute x1, waiting for transfers between devices: 0.01 us -> 1.19 us  [tiled(): theirs = lax.ppermute(received, 'row', turn)]
  transfers between devices with their start and end apart: 14 -> 14, of which waited for: 8 -> 9; matrix products, arithmetic and copies ran while one was open for 0% -> 0% of each run, Pallas kernels for 5% -> 5%
where the time goes in v6:
time: 41.1 us; the launch traced here: 40.9 us
  starting transfers between devices  20.6 us (50%)
  waiting for transfers between devices  10 us (24%)
  Pallas kernels  9.62 us (23%)
  between operations  0.7 us (2%)
    ppermute x7, starting transfers between devices, tiled(): lax.ppermute(messages[k], 'col', [(c, c ^ ORDER[k]) for c in range(count)])  13.6 us
    pallas_call x8, Pallas kernels, call(): pl.pallas_call(kernel, out_shape=outputs, in_specs=specs, out_specs=[VMEM...  9.62 us
    ppermute x4, starting transfers between devices, tiled(): parts.append(lax.ppermute(partial, ('row', 'col'), turns))  5.86 us
    ppermute x7, waiting for transfers between devices, tiled(): lax.ppermute(messages[k], 'col', [(c, c ^ ORDER[k]) for c in range(count)])  4.73 us
    ppermute x4, waiting for transfers between devices, tiled(): parts.append(lax.ppermute(partial, ('row', 'col'), turns))  2.14 us
    ppermute x1, waiting for transfers between devices, tiled(): given = lax.ppermute(keep, 'row', turn)  1.21 us
    ppermute x1, waiting for transfers between devices, tiled(): theirs = lax.ppermute(received, 'row', turn)  1.19 us
    ppermute x1, starting transfers between devices, tiled(): theirs = lax.ppermute(received, 'row', turn)  0.84 us
  transfers between devices with their start and end apart: 14, of which 9 were waited for; matrix products, arithmetic and copies ran while one was open for 0% of the time, Pallas kernels for 5%

profile of v6, /device:TPU:0, one launch (start us, length us, event | category | flops | bytes accessed | tf_op | source)
XLA Modules:
  0.0 40.9 jit_solution(11211392426770714152)
XLA Ops:
  0.6 1.9 %prepare.1 = (f32[1,256]{1,0:T(1,128)S(1)}, f32[1,256]{1,0:T(1,128)S(1)}, bf16[64,256]{1,0:T(8,128)(2,1)S(1)}, bf16[8,64,128]{2,1,0:T(8,128)(2,1)S(1)}, bf16[102...) custom-call(bf16[64,8,256]{2,1,0:T(8,128)(2,1)} %rest_0_.1, ...), custom_call_target="tpu_custom_call" | custom-call | tf_op jit(solution)/shard_map/prepare/pallas_call | solution.py:526
  2.5 5.1 %collective-permute-start = (bf16[320,128]{1,0:T(8,128)(2,1)S(1)}, bf16[320,128]{1,0:T(8,128)(2,1)S(1)}, u32[]{:S(2)}, u32[]{:S(2)}) collective-permute-start(bf16[320,128]{1,0:T(8,128)(2,1)S(1)} %get-tuple-element.37), channel_id=1, source_target_pairs={{0,6},{1,7},{2,4},{3,5},{4,2},{5,3},{6,0},{7,1},{8,14},{9,15},{10,... | collective-permute-start | bytes 245768 | tf_op jit(solution)/shard_map/ppermute | solution.py:578
  7.7 1.5 %collective-permute-start.1 = (bf16[320,128]{1,0:T(8,128)(2,1)S(1)}, bf16[320,128]{1,0:T(8,128)(2,1)S(1)}, u32[]{:S(2)}, u32[]{:S(2)}) collective-permute-start(bf16[320,128]{1,0:T(8,128)(2,1)S(1)} %get-tuple-element.38), channel_id=1, source_target_pairs={{0,1},{1,0},{2,3},{3,2},{4,5},{5,4},{6,7},{7,6},{8,9},{9,8},{10,11... | collective-permute-start | bytes 245768 | tf_op jit(solution)/shard_map/ppermute | solution.py:578
  9.2 0.0 collective-permute-start.2
  9.2 0.0 collective-permute-start.3
  9.2 5.3 %collective-permute-start.4 = (bf16[320,128]{1,0:T(8,128)(2,1)S(1)}, bf16[320,128]{1,0:T(8,128)(2,1)S(1)}, u32[]{:S(2)}, u32[]{:S(2)}) collective-permute-start(bf16[320,128]{1,0:T(8,128)(2,1)S(1)} %get-tuple-element.41), channel_id=1, source_target_pairs={{0,5},{1,4},{2,7},{3,6},{4,1},{5,0},{6,3},{7,2},{8,13},{9,12},{10,... | collective-permute-start | bytes 245768 | tf_op jit(solution)/shard_map/ppermute | solution.py:578
  14.5 0.0 collective-permute-done.rest_1_
  14.5 0.0 collective-permute-start.5
  14.5 0.0 collective-permute-done.1.rest_2_
  14.5 1.7 %collective-permute-start.6 = (bf16[320,128]{1,0:T(8,128)(2,1)S(1)}, bf16[320,128]{1,0:T(8,128)(2,1)S(1)}, u32[]{:S(2)}, u32[]{:S(2)}) collective-permute-start(bf16[320,128]{1,0:T(8,128)(2,1)S(1)} %get-tuple-element.43), channel_id=1, source_target_pairs={{0,4},{1,5},{2,6},{3,7},{4,0},{5,1},{6,2},{7,3},{8,12},{9,13},{10,... | collective-permute-start | bytes 245768 | tf_op jit(solution)/shard_map/ppermute | solution.py:578
  16.2 1.2 %collective-permute-done.2.rest_3_ = bf16[320,128]{1,0:T(8,128)(2,1)S(1)} collective-permute-done((bf16[320,128]{1,0:T(8,128)(2,1)S(1)}, bf16[320,128]{1,0:T(8,128)(2,1)S(1)}, u32[]{:S(2)}, u32[]{:S(2)}) %collective-permute-start.2) | collective-permute-done | bytes 81952 | tf_op jit(solution)/shard_map/ppermute | solution.py:578
  17.4 1.0 %collective-permute-done.3.rest_4_ = bf16[320,128]{1,0:T(8,128)(2,1)S(1)} collective-permute-done((bf16[320,128]{1,0:T(8,128)(2,1)S(1)}, bf16[320,128]{1,0:T(8,128)(2,1)S(1)}, u32[]{:S(2)}, u32[]{:S(2)}) %collective-permute-start.3) | collective-permute-done | bytes 81952 | tf_op jit(solution)/shard_map/ppermute | solution.py:578
  18.3 0.6 %collective-permute-done.4.rest_5_ = bf16[320,128]{1,0:T(8,128)(2,1)S(1)} collective-permute-done((bf16[320,128]{1,0:T(8,128)(2,1)S(1)}, bf16[320,128]{1,0:T(8,128)(2,1)S(1)}, u32[]{:S(2)}, u32[]{:S(2)}) %collective-permute-start.4) | collective-permute-done | bytes 81952 | tf_op jit(solution)/shard_map/ppermute | solution.py:578
  19.0 1.9 %collective-permute-done.5.rest_6_ = bf16[320,128]{1,0:T(8,128)(2,1)S(1)} collective-permute-done((bf16[320,128]{1,0:T(8,128)(2,1)S(1)}, bf16[320,128]{1,0:T(8,128)(2,1)S(1)}, u32[]{:S(2)}, u32[]{:S(2)}) %collective-permute-start.5) | collective-permute-done | bytes 81952 | tf_op jit(solution)/shard_map/ppermute | solution.py:578
  20.9 0.0 collective-permute-done.6.rest_7_
  20.9 0.1 collective-permute-start.7
  21.0 0.6 %arrange.1 = (f32[2048,128]{1,0:T(8,128)S(1)}, bf16[2048,128]{1,0:T(8,128)(2,1)S(1)}, bf16[1024,128]{1,0:T(8,128)(2,1)S(1)}) custom-call(bf16[1024,128]{1,0:T(8,128)(2,1)S(1)} %get-tuple-element.45.out_weight, bf16[320,128]{1,0:T(8,128)(2,1)S(1)} %get-tuple-element.36.rest_0_, bf16[320,128]{1,0:T(8,128)(2,1)S(1)} %collective-permute-done.rest_1_, ...), custom_call_target="tpu_custom_call" | custom-call | tf_op jit(solution)/shard_map/arrange/pallas_call | solution.py:526
  21.6 0.8 %collective-permute-done.7.mate = bf16[9,64,128]{2,1,0:T(8,128)(2,1)S(1)} collective-permute-done((bf16[9,64,128]{2,1,0:T(8,128)(2,1)S(1)}, bf16[9,64,128]{2,1,0:T(8,128)(2,1)S(1)}, u32[]{:S(2)}, u32[]{:S(2)}) %collective-permute-start.7) | collective-permute-done | bytes 147488 | tf_op jit(solution)/shard_map/ppermute | solution.py:587
  22.3 4.5 %sums_part.1 = (f32[8,64,256]{2,1,0:T(8,128)S(1)}, f32[264,128]{1,0:T(8,128)S(1)}) custom-call(bf16[9,64,128]{2,1,0:T(8,128)(2,1)S(1)} %collect.1.pieces, bf16[9,64,128]{2,1,0:T(8,128)(2,1)S(1)} %collective-permute-done.7.mate, bf16[8,64,128]{2,1,0:T(8,128)(2,1)S(1)} %get-tuple-element.44.cotangent, bf16[1024,128]{1,0:T(8,128)(2,1)S(1)} %get-tuple-element.46.by_second, ...), custom_call_target="tpu_custom_call" | custom-call | tf_op jit(solution)/shard_map/sums_part/pallas_call | solution.py:526
  26.9 0.2 collective-permute-start.8
  27.1 1.2 %collective-permute-done.8.given = f32[264,128]{1,0:T(8,128)S(1)} collective-permute-done((f32[264,128]{1,0:T(8,128)S(1)}, f32[264,128]{1,0:T(8,128)S(1)}, u32[]{:S(2)}, u32[]{:S(2)}) %collective-permute-start.8) | collective-permute-done | bytes 135200 | tf_op jit(solution)/shard_map/ppermute | solution.py:617
  28.3 2.1 %collective-permute-start.9 = (bf16[272,128]{1,0:T(8,128)(2,1)S(1)}, bf16[272,128]{1,0:T(8,128)(2,1)S(1)}, u32[]{:S(2)}, u32[]{:S(2)}) collective-permute-start(bf16[272,128]{1,0:T(8,128)(2,1)S(1)} %pack.1.own), channel_id=1, source_target_pairs={{0,5},{1,4},{2,7},{3,6},{4,1},{5,0},{6,3},{7,2},{8,15},{9,14},{10,... | collective-permute-start | bytes 208904 | tf_op jit(solution)/shard_map/ppermute | solution.py:633
  30.4 0.8 %collective-permute-start.12 = (bf16[272,128]{1,0:T(8,128)(2,1)S(1)}, bf16[272,128]{1,0:T(8,128)(2,1)S(1)}, u32[]{:S(2)}, u32[]{:S(2)}) collective-permute-start(bf16[272,128]{1,0:T(8,128)(2,1)S(1)} %pack.1.own), channel_id=1, source_target_pairs={{0,1},{1,0},{2,3},{3,2},{4,5},{5,4},{6,7},{7,6},{8,11},{9,10},{10,... | collective-permute-start | bytes 208904 | tf_op jit(solution)/shard_map/ppermute | solution.py:633
  31.2 2.3 %collective-permute-start.11 = (bf16[272,128]{1,0:T(8,128)(2,1)S(1)}, bf16[272,128]{1,0:T(8,128)(2,1)S(1)}, u32[]{:S(2)}, u32[]{:S(2)}) collective-permute-start(bf16[272,128]{1,0:T(8,128)(2,1)S(1)} %pack.1.own), channel_id=1, source_target_pairs={{0,6},{1,7},{2,4},{3,5},{4,2},{5,3},{6,0},{7,1},{8,12},{9,13},{10,... | collective-permute-start | bytes 208904 | tf_op jit(solution)/shard_map/ppermute | solution.py:633
  33.5 0.7 %collective-permute-start.10 = (bf16[272,128]{1,0:T(8,128)(2,1)S(1)}, bf16[272,128]{1,0:T(8,128)(2,1)S(1)}, u32[]{:S(2)}, u32[]{:S(2)}) collective-permute-start(bf16[272,128]{1,0:T(8,128)(2,1)S(1)} %pack.1.own), channel_id=1, source_target_pairs={{8,10},{9,11},{10,8},{11,9},{12,14},{13,15},{14,12},{15,13},{24,26... | collective-permute-start | bytes 208904 | tf_op jit(solution)/shard_map/ppermute | solution.py:633
  34.2 1.3 %activations.1 = bf16[64,8,256]{2,1,0:T(8,128)(2,1)} custom-call(f32[8,64,256]{2,1,0:T(8,128)S(1)} %get-tuple-element.55.normed_grads, f32[8,64,256]{2,1,0:T(8,128)S(1)} %get-tuple-element.50.hat, f32[128,128]{1,0:T(8,128)S(1)} %get-tuple-element.56.stats, f32[1,256]{1,0:T(1,128)S(1)} %get-tuple-element.51.gain), custom_call_target="tpu_custom_call" | custom-call | tf_op jit(solution)/shard_map/activations/pallas_call | solution.py:526
  35.5 0.5 %collective-permute-done.9.rest_3_ = bf16[272,128]{1,0:T(8,128)(2,1)S(1)} collective-permute-done((bf16[272,128]{1,0:T(8,128)(2,1)S(1)}, bf16[272,128]{1,0:T(8,128)(2,1)S(1)}, u32[]{:S(2)}, u32[]{:S(2)}) %collective-permute-start.9) | collective-permute-done | bytes 69664 | tf_op jit(solution)/shard_map/ppermute | solution.py:633
  36.0 0.0 collective-permute-done.12.rest_2_
  36.0 1.6 %collective-permute-done.11.rest_1_ = bf16[272,128]{1,0:T(8,128)(2,1)S(1)} collective-permute-done((bf16[272,128]{1,0:T(8,128)(2,1)S(1)}, bf16[272,128]{1,0:T(8,128)(2,1)S(1)}, u32[]{:S(2)}, u32[]{:S(2)}) %collective-permute-start.11) | collective-permute-done | bytes 69664 | tf_op jit(solution)/shard_map/ppermute | solution.py:633
  37.6 0.0 collective-permute-done.10.rest_0_
  37.6 0.8 %collective-permute-start.13 = (bf16[4,272,128]{2,1,0:T(8,128)(2,1)S(1)}, bf16[4,272,128]{2,1,0:T(8,128)(2,1)S(1)}, u32[]{:S(2)}, u32[]{:S(2)}) collective-permute-start(bf16[4,272,128]{2,1,0:T(8,128)(2,1)S(1)} %stack.1.received), channel_id=1, source_target_pairs={{0,8},{8,0},{1,9},{9,1},{2,10},{10,2},{3,11},{11,3},{4,12},{12,4},... | collective-permute-start | bytes 835592 | tf_op jit(solution)/shard_map/ppermute | solution.py:638
  38.5 1.2 %collective-permute-done.13.mate = bf16[4,272,128]{2,1,0:T(8,128)(2,1)S(1)} collective-permute-done((bf16[4,272,128]{2,1,0:T(8,128)(2,1)S(1)}, bf16[4,272,128]{2,1,0:T(8,128)(2,1)S(1)}, u32[]{:S(2)}, u32[]{:S(2)}) %collective-permute-start.13) | collective-permute-done | bytes 278560 | tf_op jit(solution)/shard_map/ppermute | solution.py:638
  39.7 1.2 %finish.1 = (f32[64,256]{1,0:T(8,128)}, f32[1,64]{1,0:T(1,128)}, f32[1024,128]{1,0:T(8,128)}, f32[1,128]{1,0:T(1,128)}, f32[1,256]{1,0:T(1,128)}, /*index=5*/f32[1,256]{1,0:T(1,128)}) custom-call(bf16[272,128]{1,0:T(8,128)(2,1)S(1)} %pack.1.own, bf16[4,272,128]{2,1,0:T(8,128)(2,1)S(1)} %stack.1.received, bf16[4,272,128]{2,1,0:T(8,128)(2,1)S(1)} %collective-permute-done.13.mate), custom_call_target="tpu_custom_call" | custom-call | tf_op jit(solution)/shard_map/finish/pallas_call | solution.py:526
  (3 shorter events, 0.1 us)
Async XLA Ops:
  2.5 11.9 %collective-permute-start = (bf16[320,128]{1,0:T(8,128)(2,1)S(1)}, bf16[320,128]{1,0:T(8,128)(2,1)S(1)}, u32[]{:S(2)}, u32[]{:S(2)}) collective-permute-start(bf16[320,128]{1,0:T(8,128)(2,1)S(1)} %get-tuple-element.37), channel_id=1, source_target_pairs={{0,6},{1,7},{2,4},{3,5},{4,2},{5,3},{6,0},{7,1},{8,14},{9,15},{10,... | collective-permute-start | bytes 245768 | tf_op jit(solution)/shard_map/ppermute | solution.py:578
  7.7 6.8 %collective-permute-start.1 = (bf16[320,128]{1,0:T(8,128)(2,1)S(1)}, bf16[320,128]{1,0:T(8,128)(2,1)S(1)}, u32[]{:S(2)}, u32[]{:S(2)}) collective-permute-start(bf16[320,128]{1,0:T(8,128)(2,1)S(1)} %get-tuple-element.38), channel_id=1, source_target_pairs={{0,1},{1,0},{2,3},{3,2},{4,5},{5,4},{6,7},{7,6},{8,9},{9,8},{10,11... | collective-permute-start | bytes 245768 | tf_op jit(solution)/shard_map/ppermute | solution.py:578
  9.2 8.2 %collective-permute-start.2 = (bf16[320,128]{1,0:T(8,128)(2,1)S(1)}, bf16[320,128]{1,0:T(8,128)(2,1)S(1)}, u32[]{:S(2)}, u32[]{:S(2)}) collective-permute-start(bf16[320,128]{1,0:T(8,128)(2,1)S(1)} %get-tuple-element.39), channel_id=1, source_target_pairs={{0,7},{1,6},{2,5},{3,4},{4,3},{5,2},{6,1},{7,0},{8,15},{9,14},{10,... | collective-permute-start | bytes 245768 | tf_op jit(solution)/shard_map/ppermute | solution.py:578
  9.2 9.1 %collective-permute-start.3 = (bf16[320,128]{1,0:T(8,128)(2,1)S(1)}, bf16[320,128]{1,0:T(8,128)(2,1)S(1)}, u32[]{:S(2)}, u32[]{:S(2)}) collective-permute-start(bf16[320,128]{1,0:T(8,128)(2,1)S(1)} %get-tuple-element.40), channel_id=1, source_target_pairs={{0,2},{1,3},{2,0},{3,1},{4,6},{5,7},{6,4},{7,5},{8,10},{9,11},{10,... | collective-permute-start | bytes 245768 | tf_op jit(solution)/shard_map/ppermute | solution.py:578
  9.2 9.8 %collective-permute-start.4 = (bf16[320,128]{1,0:T(8,128)(2,1)S(1)}, bf16[320,128]{1,0:T(8,128)(2,1)S(1)}, u32[]{:S(2)}, u32[]{:S(2)}) collective-permute-start(bf16[320,128]{1,0:T(8,128)(2,1)S(1)} %get-tuple-element.41), channel_id=1, source_target_pairs={{0,5},{1,4},{2,7},{3,6},{4,1},{5,0},{6,3},{7,2},{8,13},{9,12},{10,... | collective-permute-start | bytes 245768 | tf_op jit(solution)/shard_map/ppermute | solution.py:578
  14.5 6.4 %collective-permute-start.5 = (bf16[320,128]{1,0:T(8,128)(2,1)S(1)}, bf16[320,128]{1,0:T(8,128)(2,1)S(1)}, u32[]{:S(2)}, u32[]{:S(2)}) collective-permute-start(bf16[320,128]{1,0:T(8,128)(2,1)S(1)} %get-tuple-element.42), channel_id=1, source_target_pairs={{0,3},{1,2},{2,1},{3,0},{4,7},{5,6},{6,5},{7,4},{8,11},{9,10},{10,... | collective-permute-start | bytes 245768 | tf_op jit(solution)/shard_map/ppermute | solution.py:578
  14.5 6.4 %collective-permute-start.6 = (bf16[320,128]{1,0:T(8,128)(2,1)S(1)}, bf16[320,128]{1,0:T(8,128)(2,1)S(1)}, u32[]{:S(2)}, u32[]{:S(2)}) collective-permute-start(bf16[320,128]{1,0:T(8,128)(2,1)S(1)} %get-tuple-element.43), channel_id=1, source_target_pairs={{0,4},{1,5},{2,6},{3,7},{4,0},{5,1},{6,2},{7,3},{8,12},{9,13},{10,... | collective-permute-start | bytes 245768 | tf_op jit(solution)/shard_map/ppermute | solution.py:578
  20.9 1.4 %collective-permute-start.7 = (bf16[9,64,128]{2,1,0:T(8,128)(2,1)S(1)}, bf16[9,64,128]{2,1,0:T(8,128)(2,1)S(1)}, u32[]{:S(2)}, u32[]{:S(2)}) collective-permute-start(bf16[9,64,128]{2,1,0:T(8,128)(2,1)S(1)} %collect.1.pieces), channel_id=1, source_target_pairs={{0,8},{8,0},{1,9},{9,1},{2,10},{10,2},{3,11},{11,3},{4,12},{12,4},... | collective-permute-start | bytes 442376 | tf_op jit(solution)/shard_map/ppermute | solution.py:587
  26.9 1.4 %collective-permute-start.8 = (f32[264,128]{1,0:T(8,128)S(1)}, f32[264,128]{1,0:T(8,128)S(1)}, u32[]{:S(2)}, u32[]{:S(2)}) collective-permute-start(f32[264,128]{1,0:T(8,128)S(1)} %get-tuple-element.54.kept), channel_id=1, source_target_pairs={{0,8},{8,0},{1,9},{9,1},{2,10},{10,2},{3,11},{11,3},{4,12},{12,4},... | collective-permute-start | bytes 405512 | tf_op jit(solution)/shard_map/ppermute | solution.py:617
  28.3 7.7 %collective-permute-start.9 = (bf16[272,128]{1,0:T(8,128)(2,1)S(1)}, bf16[272,128]{1,0:T(8,128)(2,1)S(1)}, u32[]{:S(2)}, u32[]{:S(2)}) collective-permute-start(bf16[272,128]{1,0:T(8,128)(2,1)S(1)} %pack.1.own), channel_id=1, source_target_pairs={{0,5},{1,4},{2,7},{3,6},{4,1},{5,0},{6,3},{7,2},{8,15},{9,14},{10,... | collective-permute-start | bytes 208904 | tf_op jit(solution)/shard_map/ppermute | solution.py:633
  30.4 5.6 %collective-permute-start.12 = (bf16[272,128]{1,0:T(8,128)(2,1)S(1)}, bf16[272,128]{1,0:T(8,128)(2,1)S(1)}, u32[]{:S(2)}, u32[]{:S(2)}) collective-permute-start(bf16[272,128]{1,0:T(8,128)(2,1)S(1)} %pack.1.own), channel_id=1, source_target_pairs={{0,1},{1,0},{2,3},{3,2},{4,5},{5,4},{6,7},{7,6},{8,11},{9,10},{10,... | collective-permute-start | bytes 208904 | tf_op jit(solution)/shard_map/ppermute | solution.py:633
  31.2 6.4 %collective-permute-start.11 = (bf16[272,128]{1,0:T(8,128)(2,1)S(1)}, bf16[272,128]{1,0:T(8,128)(2,1)S(1)}, u32[]{:S(2)}, u32[]{:S(2)}) collective-permute-start(bf16[272,128]{1,0:T(8,128)(2,1)S(1)} %pack.1.own), channel_id=1, source_target_pairs={{0,6},{1,7},{2,4},{3,5},{4,2},{5,3},{6,0},{7,1},{8,12},{9,13},{10,... | collective-permute-start | bytes 208904 | tf_op jit(solution)/shard_map/ppermute | solution.py:633
  33.5 4.1 %collective-permute-start.10 = (bf16[272,128]{1,0:T(8,128)(2,1)S(1)}, bf16[272,128]{1,0:T(8,128)(2,1)S(1)}, u32[]{:S(2)}, u32[]{:S(2)}) collective-permute-start(bf16[272,128]{1,0:T(8,128)(2,1)S(1)} %pack.1.own), channel_id=1, source_target_pairs={{8,10},{9,11},{10,8},{11,9},{12,14},{13,15},{14,12},{15,13},{24,26... | collective-permute-start | bytes 208904 | tf_op jit(solution)/shard_map/ppermute | solution.py:633
  37.6 2.0 %collective-permute-start.13 = (bf16[4,272,128]{2,1,0:T(8,128)(2,1)S(1)}, bf16[4,272,128]{2,1,0:T(8,128)(2,1)S(1)}, u32[]{:S(2)}, u32[]{:S(2)}) collective-permute-start(bf16[4,272,128]{2,1,0:T(8,128)(2,1)S(1)} %stack.1.received), channel_id=1, source_target_pairs={{0,8},{8,0},{1,9},{9,1},{2,10},{10,2},{3,11},{11,3},{4,12},{12,4},... | collective-permute-start | bytes 835592 | tf_op jit(solution)/shard_map/ppermute | solution.py:638
